TPU v7x, 128 devices: a whole 4x4x4 slice. The times are simulated.
128 devices in a mesh: row: 16 (over x, z), col: 8 (over y, core).
Axes of the slice: x: 4, y: 4, z: 4, core: 2. Of those that a mesh axis runs over, the one named last changes fastest.
Arguments:
- object_slices: float32 [2, 2, 4096, 4096], P(None, None, 'row', 'col'), may hold values from -5 to 5
- probe: float32 [2, 128, 128], replicated, may hold values from -4 to 4
- measured: float32 [2048, 128, 128], P(('row', 'col')), may hold values from 0.1 to 2
- offsets: int32 [2, 2048], P(None, ('row', 'col')), may hold values from 0 to 3968, as said below
Outputs:
- object_gradient: float32 [2, 2, 4096, 4096], P(None, None, 'row', 'col')
Inputs may be any that keep to these rules, and one draw needn't show every extreme that they name: `offsets`: every offset is a multiple of 64 and every patch lies inside the object. The positions of the device at (row r, col c), which hold entries r * 16 * 8 + c * 16 onward, have their corner column inside tile column c. Among one device's positions at most 2 have their corner row in any one tile row, and in every tile column one tile row has exactly 2 corners from every device of that column.
All inputs are finite; a program needn't handle non-finite values.
Results may differ from a plain program's by a relative error of at most 0.0003.
Values sent between devices are 32-bit elements; how exact they have to be, the bound alone decides.
No kernel may reach another device: no remote copies, remote signals or barrier semaphores. Data moves between devices by JAX's collectives and lax.ppermute only.
A program may use at most 128 MiB of HBM per device.

v0:
```python
import math

import jax
import jax.numpy as jnp
from jax import lax
from jax.sharding import PartitionSpec as P

PHASE = 40.0
HIGHEST = lax.Precision.HIGHEST
batch_rows = 16


def from_behind(shard, axis, by):
    size = lax.axis_size(axis)
    pairs = [(i, i + by) for i in range(size) if 0 <= i + by < size]
    return lax.ppermute(shard, axis, pairs)


def dft_tables(length):
    index = jnp.arange(length, dtype=jnp.int32)
    product = index[:, None] * index[None, :] % length
    angle = product.astype(jnp.float32) * (2.0 * math.pi / length)
    scale = 1.0 / math.sqrt(length)
    return (jnp.cos(angle) * scale, jnp.sin(angle) * scale)


def fresnel_kernel(length):
    index = jnp.arange(length, dtype=jnp.int32)
    freq = jnp.where(index < length // 2, index, index - length).astype(jnp.float32) / length
    phase = PHASE * (freq[:, None] * freq[:, None] + freq[None, :] * freq[None, :])
    return (jnp.cos(phase), -jnp.sin(phase))


def complex_mul(left_re, left_im, right_re, right_im):
    return (left_re * right_re - left_im * right_im, left_re * right_im + left_im * right_re)


def transform(field_re, field_im, tables, direction):
    cosine, sine = tables
    sine = sine * direction
    part_re = jnp.einsum("jk,bkl->bjl", cosine, field_re, precision=HIGHEST) - jnp.einsum(
        "jk,bkl->bjl", sine, field_im, precision=HIGHEST
    )
    part_im = jnp.einsum("jk,bkl->bjl", cosine, field_im, precision=HIGHEST) + jnp.einsum(
        "jk,bkl->bjl", sine, field_re, precision=HIGHEST
    )
    out_re = jnp.einsum("bjk,kl->bjl", part_re, cosine, precision=HIGHEST) - jnp.einsum(
        "bjk,kl->bjl", part_im, sine, precision=HIGHEST
    )
    out_im = jnp.einsum("bjk,kl->bjl", part_re, sine, precision=HIGHEST) + jnp.einsum(
        "bjk,kl->bjl", part_im, cosine, precision=HIGHEST
    )
    return (out_re, out_im)


def propagate(field_re, field_im, tables, kernel, adjoint):
    freq_re, freq_im = transform(field_re, field_im, tables, -1.0)
    kernel_re, kernel_im = kernel
    if adjoint:
        kernel_im = -kernel_im
    freq_re, freq_im = complex_mul(kernel_re, kernel_im, freq_re, freq_im)
    return transform(freq_re, freq_im, tables, 1.0)


def patch_gradients(patches, measured_rows, probe, tables, kernel):
    slices = patches.shape[1]
    trans = [(patches[:, level, 0], patches[:, level, 1]) for level in range(slices)]
    wave_re, wave_im = complex_mul(probe[0][None], probe[1][None], trans[0][0], trans[0][1])
    level = 1
    wave_re, wave_im = propagate(wave_re, wave_im, tables, kernel, False)
    entering = [(wave_re, wave_im)]
    wave_re, wave_im = complex_mul(wave_re, wave_im, trans[level][0], trans[level][1])
    far_re, far_im = transform(wave_re, wave_im, tables, -1.0)
    misfit = far_re * far_re + far_im * far_im - measured_rows
    back_re, back_im = transform(2.0 * misfit * far_re, 2.0 * misfit * far_im, tables, 1.0)
    grads = [(back_re, back_im)] * slices
    level = 1
    enter_re, enter_im = entering[level - 1]
    grads[level] = complex_mul(enter_re, -enter_im, back_re, back_im)
    back_re, back_im = complex_mul(trans[level][0], -trans[level][1], back_re, back_im)
    back_re, back_im = propagate(back_re, back_im, tables, kernel, True)
    grads[0] = complex_mul(probe[0][None], -probe[1][None], back_re, back_im)
    return jnp.stack(
        [jnp.stack([grad_pair[0], grad_pair[1]], axis=1) for grad_pair in grads], axis=1
    )


def gradients_by_batch(patches, measured_rows, probe, tables, kernel):
    groups = patches.shape[0] // batch_rows
    grouped_patches = patches.reshape((groups, batch_rows) + patches.shape[1:])
    grouped_rows = measured_rows.reshape((groups, batch_rows) + measured_rows.shape[1:])
    result = lax.map(
        lambda paired: patch_gradients(paired[0], paired[1], probe, tables, kernel),
        (grouped_patches, grouped_rows),
    )
    return result.reshape(patches.shape)


def cut_patches(extended, row_index, col_index, block, length):
    slices = extended.shape[0]
    zero_index = jnp.zeros((), jnp.int32)

    def take_one(row_one, col_one):
        return lax.dynamic_slice(
            extended,
            (zero_index, zero_index, row_one * block, col_one * block),
            (slices, 2, length, length),
        )

    return jax.vmap(take_one)(row_index, col_index)


def accumulate(grads, row_index, col_index, in_use, extent_rows, extent_cols, block):
    items = grads.shape[0]
    slices = grads.shape[1]
    pieces = grads.reshape(items, slices, 2, 2, block, 2, block).transpose(0, 3, 5, 1, 2, 4, 6)
    pieces = pieces.reshape(items * 4, slices * 2 * block * block)
    block_rows = extent_rows // block
    block_cols = extent_cols // block
    offset_pair = jnp.arange(2, dtype=jnp.int32)
    target = (
        (row_index[:, None, None] + offset_pair[None, :, None]) * block_cols
        + col_index[:, None, None]
        + offset_pair[None, None, :]
    )
    target = jnp.where(in_use[:, None, None] > 0, target, -1).reshape(items * 4)
    onehot = (
        target[:, None] == jnp.arange(block_rows * block_cols, dtype=jnp.int32)[None, :]
    ).astype(jnp.float32)
    summed = jnp.einsum("mb,mk->bk", onehot, pieces, precision=HIGHEST)
    summed = summed.reshape(block_rows, block_cols, slices, 2, block, block).transpose(
        2, 3, 0, 4, 1, 5
    )
    return summed.reshape(slices, 2, extent_rows, extent_cols)


def body(object_slices, probe, measured, offsets):
    slices = object_slices.shape[0]
    tile_rows = object_slices.shape[2]
    tile_cols = object_slices.shape[3]
    length = measured.shape[1]
    block = length // 2
    per_device = measured.shape[0]
    row_total = lax.axis_size("row")
    capacity = max(2, 2 * per_device // row_total)
    slot_total = row_total * capacity
    tables = dft_tables(length)
    kernel = fresnel_kernel(length)
    rim_below = from_behind(object_slices[:, :, :block, :], "row", -1)
    taller = jnp.concatenate([object_slices, rim_below], axis=2)
    strip = taller[:, :, :, :block].reshape(slices * 2, (tile_rows + block) * block)
    rim_right = from_behind(strip, "col", -1).reshape(slices, 2, tile_rows + block, block)
    extended = jnp.concatenate([taller, rim_right], axis=3)
    my_col = lax.axis_index("col")
    owner_row = offsets[0] // tile_rows
    block_row = (offsets[0] - owner_row * tile_rows) // block
    block_col = (offsets[1] - my_col * tile_cols) // block
    owner_hits = (owner_row[:, None] == jnp.arange(row_total, dtype=jnp.int32)[None, :]).astype(
        jnp.int32
    )
    ranks = jnp.sum((jnp.cumsum(owner_hits, axis=0) - 1) * owner_hits, axis=1)
    slot_of = owner_row * capacity + ranks
    matches = slot_of[None, :] == jnp.arange(slot_total, dtype=jnp.int32)[:, None]
    in_use = jnp.any(matches, axis=1).astype(jnp.int32)
    source_pos = jnp.sum(
        jnp.where(matches, jnp.arange(per_device, dtype=jnp.int32)[None, :], 0), axis=1
    )
    requests = jnp.stack(
        [jnp.take(block_row, source_pos) * in_use, jnp.take(block_col, source_pos) * in_use, in_use]
    )
    requests = requests.reshape(3, row_total, capacity).transpose(1, 0, 2)
    use_mask = in_use.astype(jnp.float32)
    patch_shape = (slices, 2, length, length)
    arrived = lax.all_to_all(requests, "row", split_axis=0, concat_axis=0, tiled=True)
    asked = arrived.transpose(1, 0, 2).reshape(3, slot_total)
    served = cut_patches(extended, asked[0], asked[1], block, length).reshape(
        (row_total, capacity) + patch_shape
    )
    fetched = lax.all_to_all(served, "row", split_axis=0, concat_axis=0, tiled=True).reshape(
        (slot_total,) + patch_shape
    )
    own_patches = jnp.take(fetched, slot_of, axis=0)
    grads = gradients_by_batch(own_patches, measured, probe, tables, kernel)
    outgoing = jnp.take(grads, source_pos, axis=0) * use_mask[:, None, None, None, None]
    returned = lax.all_to_all(
        outgoing.reshape((row_total, capacity) + patch_shape),
        "row",
        split_axis=0,
        concat_axis=0,
        tiled=True,
    )
    summed = accumulate(
        returned.reshape((slot_total,) + patch_shape),
        asked[0],
        asked[1],
        asked[2],
        tile_rows + block,
        tile_cols + block,
        block,
    )
    right_part = summed[:, :, :, tile_cols:].reshape(slices * 2, (tile_rows + block) * block)
    from_left = from_behind(right_part, "col", 1).reshape(slices, 2, tile_rows + block, block)
    core = summed[:, :, :, :tile_cols]
    core = jnp.concatenate([core[:, :, :, :block] + from_left, core[:, :, :, block:]], axis=3)
    from_above = from_behind(core[:, :, tile_rows:, :], "row", 1)
    result = jnp.concatenate(
        [core[:, :, :block, :] + from_above, core[:, :, block:tile_rows, :]], axis=2
    )
    return result


def solution(mesh):
    placed = (
        P(None, None, "row", "col"),
        P(),
        P(("row", "col"), None, None),
        P(None, ("row", "col")),
    )
    return jax.shard_map(
        body, mesh=mesh, in_specs=placed, out_specs=P(None, None, "row", "col"), check_vma=False
    )
```

profile of v0, /device:TPU:7, one launch (start us, length us, event | category | flops | bytes accessed | tf_op | source)
XLA Modules:
  0.0 735.9 jit_solution(14711953721929909663)
XLA Ops:
  1.9 5.9 collective-permute-start
  12.3 4.0 all-to-all-start
  23.5 4.1 collective-permute-start.1
  27.7 6.2 collective-permute-done.1
  37.3 125.8 %while.1 = (s32[]{:T(128)}, f32[2,2,320,576]{3,2,1,0:T(8,128)}, s32[32,4]{0,1:T(4,128)S(1)}, f32[32,2,2,128,128]{4,3,2,1,0:T(8,128)}, s32[]{:T(128)}) while((s32[]{:T(128)}, f32[2,2,320,576]{3,2,1,0:T(8,128)}, s32[32,4]{0,1:T(4,128)S(1)}, f32[32,2,2,128,128]{4,3,2,1,0:T(8,128)}, s32[]{:T(128)}) %tuple.41), condition=%wide.while_cond, body=%wide.while_body.sunk | while | flops 2 | bytes 525437 | solution.py:104
  53.7 3.3 bitcast_dynamic-update-slice_fusion.2
  57.6 3.3 bitcast_dynamic-update-slice_fusion.2
  65.5 3.3 bitcast_dynamic-update-slice_fusion.2
  69.4 3.3 bitcast_dynamic-update-slice_fusion.2
  81.2 3.3 bitcast_dynamic-update-slice_fusion.2
  112.6 3.3 bitcast_dynamic-update-slice_fusion.2
  120.5 3.3 bitcast_dynamic-update-slice_fusion.2
  128.4 3.3 bitcast_dynamic-update-slice_fusion.2
  140.2 3.3 bitcast_dynamic-update-slice_fusion.2
  144.1 3.3 bitcast_dynamic-update-slice_fusion.2
  159.8 3.3 bitcast_dynamic-update-slice_fusion.2
  163.1 7.2 all-to-all-start.1
  170.9 118.8 %all-to-all-done.1 = f32[16,2,2,2,128,128]{5,4,3,2,1,0:T(8,128)} async-done(((f32[16,2,2,2,128,128]{5,4,3,2,1,0:T(8,128)}), f32[16,2,2,2,128,128]{5,4,3,2,1,0:T(8,128)}, u32[]{:S(2)}, u32[]{:S(2)}) %all-to-all-start.1) | async-done | bytes 8388640 | tf_op jit(solution)/shard_map/all_to_all | solution.py:179
  289.7 6.1 gather_fusion
  399.0 6.5 gather_fusion.1
  405.5 8.6 %select_multiply_fusion = f32[16,2,2,2,128,128]{5,4,3,2,1,0:T(8,128)} fusion(f32[16,2,2,2,128,128]{5,4,3,2,1,0:T(8,128)} %bitcast.306, f32[16,2]{1,0:T(8,128)S(1)} %convert_element_type.164, pred[16,2]{1,0:T(8,128)(4,1)S(1)} %compare_and_fusion), kind=kLoop, calls=%fused_computation.6 | loop fusion | flops 4194304 | bytes 16777376 | tf_op jit(solution)/shard_map/mul | solution.py:184
  414.1 12.2 %all-to-all-start.2 = ((f32[16,2,2,2,128,128]{5,4,3,2,1,0:T(8,128)}), f32[16,2,2,2,128,128]{5,4,3,2,1,0:T(8,128)}, u32[]{:S(2)}, u32[]{:S(2)}) async-start(f32[16,2,2,2,128,128]{5,4,3,2,1,0:T(8,128)} %select_multiply_fusion), calls=%async_computation.2 | async-start | bytes 16777216 | tf_op jit(solution)/shard_map/all_to_all | solution.py:185
  427.4 117.2 %all-to-all-done.2 = f32[16,2,2,2,128,128]{5,4,3,2,1,0:T(8,128)} async-done(((f32[16,2,2,2,128,128]{5,4,3,2,1,0:T(8,128)}), f32[16,2,2,2,128,128]{5,4,3,2,1,0:T(8,128)}, u32[]{:S(2)}, u32[]{:S(2)}) %all-to-all-start.2) | async-done | bytes 8388640 | tf_op jit(solution)/shard_map/all_to_all | solution.py:185
  544.6 16.9 %reshape_reshape.3 = f32[32,2,2,2,64,2,64]{6,5,4,3,2,1,0:T(2,128)} reshape(f32[16,2,2,2,128,128]{5,4,3,2,1,0:T(8,128)} %all-to-all-done.2) | data formatting | bytes 16777216 | tf_op jit(solution)/shard_map/reshape;reshape | solution.py:116
  561.5 12.6 %copy.274 = f32[32,2,2,2,2,64,64]{6,5,4,3,2,1,0:T(8,128)} copy(f32[32,2,2,2,2,64,64]{6,2,5,1,4,3,0:T(2,128)} %bitcast.304) | data formatting | bytes 16777216 | tf_op jit(solution)/shard_map/transpose | solution.py:116
  574.1 12.9 %reshape.460 = f32[128,16384]{1,0:T(8,128)} reshape(f32[32,2,2,2,2,64,64]{6,5,4,3,2,1,0:T(8,128)} %copy.274) | data formatting | bytes 16777216 | tf_op jit(solution)/shard_map/reshape | solution.py:117
  587.0 9.2 %copy.275 = f32[16384,128]{1,0:T(8,128)} copy(f32[16384,128]{0,1:T(8,128)} %bitcast.305) | data formatting | bytes 16777216 | tf_op jit(solution)/shard_map/mb,mk->bk/dot_general | solution.py:130
  596.3 19.5 %convolution_bitcast_fusion = f32[2,2,5,64,9,64]{5,4,3,1,0,2:T(8,128)} fusion(f32[2,2,64,64,128,1]{4,3,2,1,0,5:T(8,128)} %bitcast.307, s32[5,9]{1,0:T(8,128)S(1)} %multiply_add_fusion.12, s32[128]{0:T(128)S(1)} %select_n.243), kind=kOutput, calls=%fused_computation.11 | convolution fusion | flops 1132467840 | bytes 11338420 | tf_op jit(solution)/shard_map/mb,mk->bk/dot_general | solution.py:130
  615.7 12.0 %copy.276 = f32[2,2,5,64,9,64]{3,2,5,4,1,0:T(8,128)} copy(f32[2,2,5,64,9,64]{5,4,3,1,0,2:T(8,128)} %convolution_bitcast_fusion) | data formatting | bytes 5898240 | tf_op jit(solution)/shard_map/transpose | solution.py:131
  627.7 6.2 reshape.461
  639.2 63.9 %collective-permute-start.2 = (f32[4,20480]{1,0:T(4,128)}, f32[4,20480]{1,0:T(4,128)}, u32[]{:S(2)}, u32[]{:S(2)}) collective-permute-start(f32[4,20480]{1,0:T(4,128)} %reshape.462), channel_id=1, source_target_pairs={{0,1},{1,2},{2,3},{3,4},{4,5},{5,6},{6,7},{8,9},{9,10},{10,11},{11... | collective-permute-start | bytes 983048 | tf_op jit(solution)/shard_map/ppermute | solution.py:16
  716.2 11.2 %collective-permute-done.3 = f32[2,2,64,512]{3,2,1,0:T(8,128)} collective-permute-done((f32[2,2,64,512]{3,2,1,0:T(8,128)}, f32[2,2,64,512]{3,2,1,0:T(8,128)}, u32[]{:S(2)}, u32[]{:S(2)}) %collective-permute-start.3) | collective-permute-done | bytes 524320 | tf_op jit(solution)/shard_map/ppermute | solution.py:16
  (214 shorter events, 237.7 us)
Async XLA Ops:
  1.9 20.5 %collective-permute-start = (f32[2,2,64,512]{3,2,1,0:T(8,128)}, f32[2,2,64,512]{3,2,1,0:T(8,128)S(1)}, u32[]{:S(2)}, u32[]{:S(2)}) collective-permute-start(f32[2,2,64,512]{3,2,1,0:T(8,128)} %slice.80), channel_id=1, source_target_pairs={{8,0},{16,8},{24,16},{32,24},{40,32},{48,40},{56,48},{64,56},{72,6... | collective-permute-start | bytes 1572872 | tf_op jit(solution)/shard_map/ppermute | solution.py:16
  12.3 8.7 %all-to-all-start = ((s32[16,3,2]{1,2,0:T(2,128)}), s32[16,3,2]{1,2,0:T(2,128)S(1)}, u32[]{:S(2)}, u32[]{:S(2)}) async-start(s32[16,3,2]{1,2,0:T(2,128)} %copy.224), calls=%async_computation | async-start | bytes 32768 | tf_op jit(solution)/shard_map/all_to_all | solution.py:174
  23.5 10.4 %collective-permute-start.1 = (f32[4,20480]{1,0:T(4,128)}, f32[4,20480]{1,0:T(4,128)}, u32[]{:S(2)}, u32[]{:S(2)}) collective-permute-start(f32[4,20480]{1,0:T(4,128)} %reshape.456), channel_id=1, source_target_pairs={{1,0},{2,1},{3,2},{4,3},{5,4},{6,5},{7,6},{9,8},{10,9},{11,10},{12... | collective-permute-start | bytes 983048 | tf_op jit(solution)/shard_map/ppermute | solution.py:16
  163.1 7.4 %copy-start.3 = (s32[2,16]{1,0:T(2,128)S(1)}, s32[2,16]{1,0:T(2,128)}, u32[]{:S(2)}) copy-start(s32[2,16]{1,0:T(2,128)} %param.9) | copy-start | bytes 388
  163.1 7.8 %copy-start.2 = (f32[2,128,128]{2,1,0:T(8,128)S(1)}, f32[2,128,128]{2,1,0:T(8,128)}, u32[]{:S(2)}) copy-start(f32[2,128,128]{2,1,0:T(8,128)} %param.7) | copy-start | bytes 393220
  163.1 126.6 %all-to-all-start.1 = ((f32[16,2,2,2,128,128]{5,4,3,2,1,0:T(8,128)}), f32[16,2,2,2,128,128]{5,4,3,2,1,0:T(8,128)}, u32[]{:S(2)}, u32[]{:S(2)}) async-start(f32[16,2,2,2,128,128]{5,4,3,2,1,0:T(8,128)} %bitcast.308), calls=%async_computation.1 | async-start | bytes 16777216 | tf_op jit(solution)/shard_map/all_to_all | solution.py:179
  340.9 6.1 copy-start
  414.1 130.5 %all-to-all-start.2 = ((f32[16,2,2,2,128,128]{5,4,3,2,1,0:T(8,128)}), f32[16,2,2,2,128,128]{5,4,3,2,1,0:T(8,128)}, u32[]{:S(2)}, u32[]{:S(2)}) async-start(f32[16,2,2,2,128,128]{5,4,3,2,1,0:T(8,128)} %select_multiply_fusion), calls=%async_computation.2 | async-start | bytes 16777216 | tf_op jit(solution)/shard_map/all_to_all | solution.py:185
  633.9 5.3 copy-start.1
  639.2 68.2 %collective-permute-start.2 = (f32[4,20480]{1,0:T(4,128)}, f32[4,20480]{1,0:T(4,128)}, u32[]{:S(2)}, u32[]{:S(2)}) collective-permute-start(f32[4,20480]{1,0:T(4,128)} %reshape.462), channel_id=1, source_target_pairs={{0,1},{1,2},{2,3},{3,4},{4,5},{5,6},{6,7},{8,9},{9,10},{10,11},{11... | collective-permute-start | bytes 983048 | tf_op jit(solution)/shard_map/ppermute | solution.py:16
  714.3 13.1 %collective-permute-start.3 = (f32[2,2,64,512]{3,2,1,0:T(8,128)}, f32[2,2,64,512]{3,2,1,0:T(8,128)}, u32[]{:S(2)}, u32[]{:S(2)}) collective-permute-start(f32[2,2,64,512]{3,2,1,0:T(8,128)} %copy.279), channel_id=1, source_target_pairs={{0,8},{8,16},{16,24},{24,32},{32,40},{40,48},{48,56},{56,64},{64,7... | collective-permute-start | bytes 1572872 | tf_op jit(solution)/shard_map/ppermute | solution.py:16
where the time goes:
time: 747 us; the launch traced here: 736 us
  waiting for transfers between devices  259 us (35%)
  local copies, waits for them, and re-layouts  235 us (31%)
  matrix products  117 us (16%)
  starting transfers between devices  99.2 us (13%)
  other arithmetic  25.4 us (3%)
    gather x96, local copies, waits for them, and re-layouts  126 us
    all_to_all x1, waiting for transfers between devices, body(): lax.all_to_all(served, 'row', split_axis=0, concat_axis=0, tiled=True)  119 us
    all_to_all x1, waiting for transfers between devices, body(): lax.all_to_all(outgoing.reshape((row_total, capacity) + patch_shape), 'ro...  117 us
    ppermute x4, starting transfers between devices, from_behind(): return lax.ppermute(shard, axis, pairs)  75.9 us
    ppermute x4, waiting for transfers between devices, from_behind(): return lax.ppermute(shard, axis, pairs)  19.7 us
    dot_general x1, matrix products, accumulate(): summed = jnp.einsum('mb,mk->bk', onehot, pieces, precision=HIGHEST)  19.5 us
    another operation x1, local copies, waits for them, and re-layouts, accumulate(): grads.reshape(items, slices, 2, 2, block, 2, block)  16.9 us
  transfers between devices with their start and end apart: 7, of which 6 were waited for; matrix products, arithmetic and copies ran while one was open for 2% of the time, Pallas kernels for 0%

commit v1 on v0

v1 whole, which is shorter than its diff:
```python
import math

import jax
import jax.numpy as jnp
import ml_dtypes
import numpy as np
from jax import lax
from jax.experimental import pallas as pl
from jax.experimental.pallas import tpu as pltpu
from jax.sharding import PartitionSpec as P

PHASE = 40.0
SIDE = 128
BLOCK = 64
CAP = 2
META = 8
VMEM_LIMIT = 48 * 1024 * 1024


def dft_matrix():
    index = np.arange(SIDE)
    angle = (index[:, None] * index[None, :] % SIDE) * (-2.0 * math.pi / SIDE)
    return np.exp(1j * angle) / math.sqrt(SIDE)


def propagation_matrix():
    index = np.arange(SIDE)
    freq = np.where(index < SIDE // 2, index, index - SIDE) / SIDE
    dft = dft_matrix()
    return np.conj(dft) @ (np.exp(-1j * PHASE * freq * freq)[:, None] * dft)


def real_forms(matrix):
    right = np.block([[matrix.real, matrix.imag], [-matrix.imag, matrix.real]])
    out = []
    for form in (right, right.T):
        form = form.astype(np.float32)
        high = form.astype(ml_dtypes.bfloat16)
        out.append(high)
        out.append((form - high.astype(np.float32)).astype(ml_dtypes.bfloat16))
    return np.stack(out)


TABLES = np.concatenate([real_forms(propagation_matrix()), real_forms(dft_matrix())])


def split(field):
    high = field.astype(jnp.bfloat16)
    low = (field - high.astype(jnp.float32)).astype(jnp.bfloat16)
    return high, low


def from_right(rows, tables, at):
    high, low = split(rows)
    left = jnp.concatenate([high, low, high], axis=1)
    right = jnp.concatenate([tables[at], tables[at], tables[at + 1]], axis=0)
    return jnp.dot(left, right, preferred_element_type=jnp.float32)


def from_left(columns, tables, at):
    high, low = split(columns)
    left = jnp.concatenate([tables[at], tables[at], tables[at + 1]], axis=1)
    right = jnp.concatenate([high, low, high], axis=0)
    return jnp.dot(left, right, preferred_element_type=jnp.float32)


def swap(pair):
    top = jnp.concatenate([pair[:SIDE, :SIDE], pair[SIDE:, :SIDE]], axis=1)
    bottom = jnp.concatenate([pair[:SIDE, SIDE:], pair[SIDE:, SIDE:]], axis=1)
    return jnp.concatenate([top, bottom], axis=0)


def two_sided(rows, tables, right_at, left_at):
    return from_left(swap(from_right(rows, tables, right_at)), tables, left_at)


def low_lanes(shape):
    return lax.broadcasted_iota(jnp.int32, shape, len(shape) - 1) < BLOCK


def cut_pair(ext_ref, comp, row, col):
    first = ext_ref[comp, pl.ds(row, SIDE), col : col + SIDE]
    second = ext_ref[comp, pl.ds(row, SIDE), col + SIDE : col + 2 * SIDE]
    mixed = jnp.where(low_lanes(first.shape), second, first)
    return first, pltpu.roll(mixed, BLOCK, 1)


def times(left_re, left_im, right_re, right_im):
    return (left_re * right_re - left_im * right_im, left_re * right_im + left_im * right_re)


def conj_times(left_re, left_im, right_re, right_im):
    return (left_re * right_re + left_im * right_im, left_re * right_im - left_im * right_re)


def load_extended(tile_ref, below_ref, right_ref, diag_ref, ext_ref, sems, comps):
    count = len(comps)
    rows, cols = tile_ref.shape[1:]
    first = comps[0]
    pieces = (
        (tile_ref, pl.ds(0, rows), pl.ds(0, cols)),
        (below_ref, pl.ds(rows, BLOCK), pl.ds(0, cols)),
        (right_ref, pl.ds(0, rows), pl.ds(cols, SIDE)),
        (diag_ref, pl.ds(rows, BLOCK), pl.ds(cols, SIDE)),
    )
    return [
        pltpu.make_async_copy(
            source.at[pl.ds(first, count)], ext_ref.at[pl.ds(0, count), at_rows, at_cols], sems.at[n]
        )
        for n, (source, at_rows, at_cols) in enumerate(pieces)
    ]


def pack_kernel(off_ref, meas_ref, send_ref, meta_ref, count_ref, corner_ref, sems):
    owners = send_ref.shape[0]
    positions = meas_ref.shape[0]
    for owner in range(owners):
        count_ref[owner] = 0
        for rank in range(CAP):
            corner_ref[owner * CAP + rank] = -1
    copies = []
    for pos in range(positions):
        y = off_ref[0, pos]
        x = off_ref[1, pos]
        owner = lax.shift_right_logical(y, 8)
        rank = jnp.minimum(count_ref[owner], CAP - 1)
        count_ref[owner] = rank + 1
        corner = (lax.shift_right_logical(y, 6) & 3) * 8 + (lax.shift_right_logical(x, 6) & 7)
        corner_ref[owner * CAP + rank] = corner
        copy = pltpu.make_async_copy(
            meas_ref.at[pos],
            send_ref.at[owner, pl.ds(pl.multiple_of(rank * SIDE, SIDE), SIDE)],
            sems.at[pos],
        )
        copy.start()
        copies.append(copy)
    row = lax.broadcasted_iota(jnp.int32, (META, SIDE), 0)
    for owner in range(owners):
        both = jnp.where(row == 0, corner_ref[owner * CAP], corner_ref[owner * CAP + 1])
        meta_ref[owner] = both.astype(jnp.float32)
    copy = pltpu.make_async_copy(
        meta_ref, send_ref.at[:, pl.ds(CAP * SIDE, META)], sems.at[positions]
    )
    copy.start()
    copies.append(copy)
    for copy in copies:
        copy.wait()


def pack(offsets, measured, owners):
    positions = measured.shape[0]
    return pl.pallas_call(
        pack_kernel,
        out_shape=jax.ShapeDtypeStruct((owners, CAP * SIDE + META, SIDE), jnp.float32),
        in_specs=[
            pl.BlockSpec(memory_space=pltpu.SMEM),
            pl.BlockSpec(memory_space=pl.ANY),
        ],
        out_specs=pl.BlockSpec(memory_space=pl.ANY),
        scratch_shapes=[
            pltpu.VMEM((owners, META, SIDE), jnp.float32),
            pltpu.SMEM((owners,), jnp.int32),
            pltpu.SMEM((owners * CAP,), jnp.int32),
            pltpu.SemaphoreType.DMA((positions + 1,)),
        ],
        name="pack_measured",
    )(offsets, measured)


def forward_kernel(
    tile_ref, below_ref, right_ref, diag_ref, probe_ref, tables, far_ref, enter_ref, ext_ref, sems
):
    step = pl.program_id(0)
    copies = load_extended(
        tile_ref, below_ref, right_ref, diag_ref, ext_ref, sems, range(tile_ref.shape[0])
    )

    @pl.when(step == 0)
    def _():
        for copy in copies:
            copy.start()
        for copy in copies:
            copy.wait()

    row = pl.multiple_of(step * BLOCK, BLOCK)
    probe_re = probe_ref[0]
    probe_im = probe_ref[1]
    for pair in range(far_ref.shape[0]):
        trans = [cut_pair(ext_ref, comp, row, pair * SIDE) for comp in range(4)]
        waves = [times(probe_re, probe_im, trans[0][n], trans[1][n]) for n in range(2)]
        rows = jnp.concatenate([jnp.concatenate(wave, axis=1) for wave in waves], axis=0)
        enter = two_sided(rows, tables, 0, 2)
        enter_ref[pair] = enter
        waves = [
            times(
                enter[:SIDE, n * SIDE : (n + 1) * SIDE],
                enter[SIDE:, n * SIDE : (n + 1) * SIDE],
                trans[2][n],
                trans[3][n],
            )
            for n in range(2)
        ]
        rows = jnp.concatenate([jnp.concatenate(wave, axis=1) for wave in waves], axis=0)
        far_ref[pair] = two_sided(rows, tables, 4, 6)


def stage_cost(pairs):
    return pl.CostEstimate(
        flops=pairs * 4 * 3 * 2 * 256**3, bytes_accessed=14 * 1024 * 1024, transcendentals=0
    )


def forward(tile, below, right, diag, probe, tables):
    steps = tile.shape[1] // BLOCK
    pairs = tile.shape[2] // SIDE
    field = jax.ShapeDtypeStruct((steps * pairs, 2 * SIDE, 2 * SIDE), jnp.float32)
    whole = pl.BlockSpec(memory_space=pl.ANY)
    block = pl.BlockSpec((pairs, 2 * SIDE, 2 * SIDE), lambda step: (step, 0, 0))
    return pl.pallas_call(
        forward_kernel,
        out_shape=(field, field),
        grid=(steps,),
        in_specs=[
            whole,
            whole,
            whole,
            whole,
            pl.BlockSpec(probe.shape, lambda step: (0, 0, 0)),
            pl.BlockSpec(tables.shape, lambda step: (0, 0, 0)),
        ],
        out_specs=(block, block),
        scratch_shapes=[
            pltpu.VMEM(
                (tile.shape[0], tile.shape[1] + BLOCK, tile.shape[2] + SIDE), jnp.float32
            ),
            pltpu.SemaphoreType.DMA((4,)),
        ],
        compiler_params=pltpu.CompilerParams(vmem_limit_bytes=VMEM_LIMIT),
        cost_estimate=stage_cost(steps * pairs),
        name="forward_fields",
    )(tile, below, right, diag, probe, tables)


def backward_kernel(
    corner_ref,
    recv_ref,
    tile_ref,
    below_ref,
    right_ref,
    diag_ref,
    probe_ref,
    tables,
    far_ref,
    enter_ref,
    out_ref,
    out_right_ref,
    out_below_ref,
    out_diag_ref,
    ext_ref,
    sum_ref,
    count_ref,
    even_ref,
    odd_ref,
    sems,
):
    step = pl.program_id(0)
    pairs = far_ref.shape[0]
    corners = sum_ref.shape[0]
    copies = load_extended(tile_ref, below_ref, right_ref, diag_ref, ext_ref, sems, (2, 3))

    @pl.when(step == 0)
    def _():
        for copy in copies:
            copy.start()
        sum_ref[...] = jnp.zeros_like(sum_ref)
        even_ref[...] = jnp.zeros_like(even_ref)
        odd_ref[...] = jnp.zeros_like(odd_ref)
        for corner in range(corners):
            count_ref[corner] = 0
        for source in range(recv_ref.shape[0]):
            for rank in range(CAP):
                corner = corner_ref[source, rank]

                @pl.when(corner >= 0)
                def _():
                    count_ref[corner] = count_ref[corner] + 1
                    sum_ref[corner] = (
                        sum_ref[corner] + recv_ref[source, rank * SIDE : (rank + 1) * SIDE]
                    )

        for copy in copies:
            copy.wait()

    row = pl.multiple_of(step * BLOCK, BLOCK)
    probe_re = probe_ref[0]
    probe_im = probe_ref[1]
    for pair in range(pairs):
        trans = [cut_pair(ext_ref, comp, row, pair * SIDE) for comp in range(2)]
        waves = []
        for n in range(2):
            corner = step * (2 * pairs) + 2 * pair + n
            hits = count_ref[corner].astype(jnp.float32)
            far_re = far_ref[pair, :SIDE, n * SIDE : (n + 1) * SIDE]
            far_im = far_ref[pair, SIDE:, n * SIDE : (n + 1) * SIDE]
            misfit = 2.0 * (hits * (far_re * far_re + far_im * far_im) - sum_ref[corner])
            waves.append((misfit * far_re, misfit * far_im))
        rows = jnp.concatenate([jnp.concatenate(wave, axis=1) for wave in waves], axis=0)
        back = two_sided(rows, tables, 6, 4)
        waves = []
        grads = []
        for n in range(2):
            back_re = back[:SIDE, n * SIDE : (n + 1) * SIDE]
            back_im = back[SIDE:, n * SIDE : (n + 1) * SIDE]
            enter_re = enter_ref[pair, :SIDE, n * SIDE : (n + 1) * SIDE]
            enter_im = enter_ref[pair, SIDE:, n * SIDE : (n + 1) * SIDE]
            grads.append(conj_times(enter_re, enter_im, back_re, back_im))
            waves.append(conj_times(trans[0][n], trans[1][n], back_re, back_im))
        rows = jnp.concatenate([jnp.concatenate(wave, axis=1) for wave in waves], axis=0)
        back = two_sided(rows, tables, 2, 0)
        for n, acc in ((0, even_ref), (1, odd_ref)):
            first = conj_times(
                probe_re,
                probe_im,
                back[:SIDE, n * SIDE : (n + 1) * SIDE],
                back[SIDE:, n * SIDE : (n + 1) * SIDE],
            )
            for comp, value in enumerate(first + grads[n]):
                at = (comp, slice(None), slice(pair * SIDE, (pair + 1) * SIDE))
                acc[comp, :BLOCK, at[2]] = acc[comp, BLOCK:, at[2]] + value[:BLOCK]
                acc[comp, BLOCK:, at[2]] = value[BLOCK:]

    def merged(comp, rows, col):
        here = odd_ref[comp, rows, col : col + SIDE] if col < pairs * SIDE else None
        before = odd_ref[comp, rows, col - SIDE : col] if col > 0 else None
        if here is None:
            here = jnp.zeros_like(before)
        if before is None:
            before = jnp.zeros_like(here)
        mixed = jnp.where(low_lanes(here.shape), here, before)
        shifted = pltpu.roll(mixed, BLOCK, 1)
        if col < pairs * SIDE:
            shifted = shifted + even_ref[comp, rows, col : col + SIDE]
        return shifted

    top = slice(0, BLOCK)
    for comp in range(4):
        for col in range(0, pairs * SIDE, SIDE):
            out_ref[comp, :, col : col + SIDE] = merged(comp, top, col)
        out_right_ref[comp] = merged(comp, top, pairs * SIDE)

    @pl.when(step == pl.num_programs(0) - 1)
    def _():
        bottom = slice(BLOCK, 2 * BLOCK)
        for comp in range(4):
            for col in range(0, pairs * SIDE, SIDE):
                out_below_ref[comp, :, col : col + SIDE] = merged(comp, bottom, col)
            out_diag_ref[comp] = merged(comp, bottom, pairs * SIDE)


def backward(corner, recv, tile, below, right, diag, probe, tables, far, enter):
    steps = tile.shape[1] // BLOCK
    pairs = tile.shape[2] // SIDE
    comps, rows, cols = tile.shape
    whole = pl.BlockSpec(memory_space=pl.ANY)
    block = pl.BlockSpec((pairs, 2 * SIDE, 2 * SIDE), lambda step: (step, 0, 0))

    def full(shape):
        return pl.BlockSpec(shape, lambda step: (0, 0, 0))

    return pl.pallas_call(
        backward_kernel,
        out_shape=(
            jax.ShapeDtypeStruct(tile.shape, jnp.float32),
            jax.ShapeDtypeStruct((comps, rows, SIDE), jnp.float32),
            jax.ShapeDtypeStruct((comps, BLOCK, cols), jnp.float32),
            jax.ShapeDtypeStruct((comps, BLOCK, SIDE), jnp.float32),
        ),
        grid=(steps,),
        in_specs=[
            pl.BlockSpec(memory_space=pltpu.SMEM),
            full(recv.shape),
            whole,
            whole,
            whole,
            whole,
            full(probe.shape),
            full(tables.shape),
            block,
            block,
        ],
        out_specs=(
            pl.BlockSpec((comps, BLOCK, cols), lambda step: (0, step, 0)),
            pl.BlockSpec((comps, BLOCK, SIDE), lambda step: (0, step, 0)),
            full((comps, BLOCK, cols)),
            full((comps, BLOCK, SIDE)),
        ),
        scratch_shapes=[
            pltpu.VMEM((2, rows + BLOCK, cols + SIDE), jnp.float32),
            pltpu.VMEM((steps * pairs * 2, SIDE, SIDE), jnp.float32),
            pltpu.SMEM((steps * pairs * 2,), jnp.int32),
            pltpu.VMEM((comps, SIDE, cols), jnp.float32),
            pltpu.VMEM((comps, SIDE, cols), jnp.float32),
            pltpu.SemaphoreType.DMA((4,)),
        ],
        compiler_params=pltpu.CompilerParams(vmem_limit_bytes=VMEM_LIMIT),
        cost_estimate=stage_cost(steps * pairs),
        name="backward_fields",
    )(corner, recv, tile, below, right, diag, probe, tables, far, enter)


def border_kernel(own_ref, above_ref, left_ref, diag_ref, out_ref, top_ref, side_ref, sems):
    comps, rows, cols = out_ref.shape
    top = out_ref.at[:, pl.ds(0, BLOCK)]
    side = out_ref.at[:, pl.ds(BLOCK, rows - BLOCK), pl.ds(0, SIDE)]
    loads = [
        pltpu.make_async_copy(top, top_ref, sems.at[0]),
        pltpu.make_async_copy(side, side_ref, sems.at[1]),
    ]
    for copy in loads:
        copy.start()
    for copy in loads:
        copy.wait()
    top_ref[...] = top_ref[...] + above_ref[...]
    top_ref[:, :, :SIDE] = top_ref[:, :, :SIDE] + left_ref[:, :BLOCK] + diag_ref[...]
    side_ref[...] = side_ref[...] + left_ref[:, BLOCK:]
    stores = [
        pltpu.make_async_copy(top_ref, top, sems.at[0]),
        pltpu.make_async_copy(side_ref, side, sems.at[1]),
    ]
    for copy in stores:
        copy.start()
    for copy in stores:
        copy.wait()


def add_borders(own, above, left, diag):
    comps, rows, cols = own.shape
    vmem = pl.BlockSpec(memory_space=pltpu.VMEM)
    return pl.pallas_call(
        border_kernel,
        out_shape=jax.ShapeDtypeStruct(own.shape, jnp.float32),
        in_specs=[pl.BlockSpec(memory_space=pl.ANY), vmem, vmem, vmem],
        out_specs=pl.BlockSpec(memory_space=pl.ANY),
        scratch_shapes=[
            pltpu.VMEM((comps, BLOCK, cols), jnp.float32),
            pltpu.VMEM((comps, rows - BLOCK, SIDE), jnp.float32),
            pltpu.SemaphoreType.DMA((2,)),
        ],
        input_output_aliases={0: 0},
        compiler_params=pltpu.CompilerParams(vmem_limit_bytes=VMEM_LIMIT),
        name="add_borders",
    )(own, above, left, diag)


def moved(shard, down, across):
    row_total = lax.axis_size("row")
    col_total = lax.axis_size("col")
    if across == 0:
        pairs = [(r, r + down) for r in range(row_total) if 0 <= r + down < row_total]
        return lax.ppermute(shard, "row", pairs)
    if down == 0:
        pairs = [(c, c + across) for c in range(col_total) if 0 <= c + across < col_total]
        return lax.ppermute(shard, "col", pairs)
    pairs = [
        (r * col_total + c, (r + down) * col_total + c + across)
        for r in range(row_total)
        for c in range(col_total)
        if 0 <= r + down < row_total and 0 <= c + across < col_total
    ]
    return lax.ppermute(shard, ("row", "col"), pairs)


def body(object_slices, probe, measured, offsets):
    slices, parts, tile_rows, tile_cols = object_slices.shape
    tile = object_slices.reshape(slices * parts, tile_rows, tile_cols)
    row_total = lax.axis_size("row")
    tables = jnp.asarray(TABLES)
    send = pack(offsets, measured, row_total)
    recv = lax.all_to_all(send, "row", split_axis=0, concat_axis=0, tiled=True)
    below = moved(tile[:, :BLOCK, :], -1, 0)
    right = moved(tile[:, :, :SIDE], 0, -1)
    diag = moved(tile[:, :BLOCK, :SIDE], -1, -1)
    far, enter = forward(tile, below, right, diag, probe, tables)
    corner = recv[:, CAP * SIDE : CAP * SIDE + CAP, 0].astype(jnp.int32)
    own, to_right, to_below, to_diag = backward(
        corner, recv, tile, below, right, diag, probe, tables, far, enter
    )
    above = moved(to_below, 1, 0)
    left = moved(to_right, 0, 1)
    corner_part = moved(to_diag, 1, 1)
    result = add_borders(own, above, left, corner_part)
    return result.reshape(object_slices.shape)


def solution(mesh):
    placed = (
        P(None, None, "row", "col"),
        P(),
        P(("row", "col"), None, None),
        P(None, ("row", "col")),
    )
    return jax.shard_map(
        body, mesh=mesh, in_specs=placed, out_specs=P(None, None, "row", "col"), check_vma=False
    )
```

time: 747 us -> 147 us (0.20); the launches traced: 736 us -> 144 us
  local copies, waits for them, and re-layouts: 235 us -> 1.55 us
  waiting for transfers between devices: 259 us -> 40.7 us
  matrix products: 117 us -> 0 us
  Pallas kernels: 0 us -> 73.2 us
  starting transfers between devices: 99.2 us -> 27.3 us
  other arithmetic: 25.4 us -> 0.85 us
    all_to_all x3 -> x1, waiting for transfers between devices: 239 us -> 0.01 us  [body(): recv = lax.all_to_all(send, 'row', split_axis=0, concat_axis=0, tiled=True)]
    gather x100 -> x0, local copies, waits for them, and re-layouts: 140 us -> none
    dot_general x49 -> x0, matrix products: 117 us -> none  [the longest x1 19.5 us: accumulate(): summed = jnp.einsum('mb,mk->bk', onehot, pieces, precision=HIGHEST)]
    pallas_call x0 -> x4, Pallas kernels: none -> 73.2 us  [the longest x1 33.7 us: pack(): pl.pallas_call(pack_kernel, out_shape=jax.ShapeDtypeStruct((owners, CAP *...]
    ppermute x4 -> x6, starting transfers between devices: 75.9 us -> 19.4 us  [the longest x2 8.34 us: moved(): return lax.ppermute(shard, 'col', pairs)]
    reshape x7 -> x0, local copies, waits for them, and re-layouts: 25.8 us -> none  [the longest x1 12.9 us: accumulate(): pieces = pieces.reshape(items * 4, slices * 2 * block * block)]
    transpose x3 -> x0, local copies, waits for them, and re-layouts: 25.4 us -> none  [the longest x1 12.6 us: accumulate(): grads.reshape(items, slices, 2, 2, block, 2, block)]
    ppermute x4 -> x6, waiting for transfers between devices: 19.7 us -> 40.7 us  [the longest x2 40.6 us: moved(): return lax.ppermute(shard, ('row', 'col'), pairs)]
  transfers between devices with their start and end apart: 7 -> 7, of which waited for: 6 -> 3; matrix products, arithmetic and copies ran while one was open for 2% -> 0% of each run, Pallas kernels for 0% -> 12%
where the time goes in v1:
time: 147 us; the launch traced here: 144 us
  Pallas kernels  73.2 us (50%)
  waiting for transfers between devices  40.7 us (28%)
  starting transfers between devices  27.3 us (19%)
  local copies, waits for them, and re-layouts  1.55 us (1%)
    ppermute x2, waiting for transfers between devices, moved(): return lax.ppermute(shard, ('row', 'col'), pairs)  40.6 us
    pallas_call x1, Pallas kernels, pack(): pl.pallas_call(pack_kernel, out_shape=jax.ShapeDtypeStruct((owners, CAP *...  33.7 us
    pallas_call x1, Pallas kernels, backward(): pl.pallas_call(backward_kernel, out_shape=(jax.ShapeDtypeStruct(tile.shap...  20.5 us
    pallas_call x1, Pallas kernels, forward(): pl.pallas_call(forward_kernel, out_shape=(field, field), grid=(steps,), i...  16.8 us
    ppermute x2, starting transfers between devices, moved(): return lax.ppermute(shard, 'col', pairs)  8.34 us
    all_to_all x1, starting transfers between devices, body(): recv = lax.all_to_all(send, 'row', split_axis=0, concat_axis=0, tiled=True)  7.85 us
    ppermute x2, starting transfers between devices, moved(): return lax.ppermute(shard, 'row', pairs)  6.65 us
    ppermute x2, starting transfers between devices, moved(): return lax.ppermute(shard, ('row', 'col'), pairs)  4.44 us
  transfers between devices with their start and end apart: 7, of which 3 were waited for; matrix products, arithmetic and copies ran while one was open for 0% of the time, Pallas kernels for 12%

profile of v1, /device:TPU:7, one launch (start us, length us, event | category | flops | bytes accessed | tf_op | source)
XLA Modules:
  0.0 143.7 jit_solution(14386989635624660454)
XLA Ops:
  0.0 33.7 %pack_measured.1 = f32[16,264,128]{2,1,0:T(8,128)} custom-call(s32[2,16]{1,0:T(2,128)} %off_ref.1, f32[16,128,128]{2,1,0:T(8,128)} %meas_ref.1), custom_call_target="tpu_custom_call" | custom-call | tf_op jit(solution)/shard_map/pack_measured/pallas_call | solution.py:152
  33.7 0.0 copy-start
  33.8 7.9 %all-to-all-start = ((f32[16,264,128]{2,1,0:T(8,128)}), f32[16,264,128]{2,1,0:T(8,128)}, u32[]{:S(2)}, u32[]{:S(2)}) async-start(f32[16,264,128]{2,1,0:T(8,128)} %pack_measured.1), calls=%async_computation | async-start | bytes 4325376 | tf_op jit(solution)/shard_map/all_to_all | solution.py:479
  41.6 0.0 copy-start.1
  41.6 0.0 copy-start.2
  41.6 0.0 copy-done
  41.7 4.7 %collective-permute-start = (f32[4,64,512]{2,1,0:T(8,128)S(1)}, f32[4,64,512]{2,1,0:T(8,128)S(1)}, u32[]{:S(2)}, u32[]{:S(2)}) collective-permute-start(f32[4,64,512]{2,1,0:T(8,128)S(1)} %slice.17), channel_id=1, source_target_pairs={{8,0},{16,8},{24,16},{32,24},{40,32},{48,40},{56,48},{64,56},{72,6... | collective-permute-start | bytes 1572872 | tf_op jit(solution)/shard_map/ppermute | solution.py:460
  46.4 0.1 slice.18
  46.5 3.4 %collective-permute-start.1 = (f32[4,256,128]{2,1,0:T(8,128)S(1)}, f32[4,256,128]{2,1,0:T(8,128)S(1)}, u32[]{:S(2)}, u32[]{:S(2)}) collective-permute-start(f32[4,256,128]{2,1,0:T(8,128)S(1)} %slice.18), channel_id=1, source_target_pairs={{1,0},{2,1},{3,2},{4,3},{5,4},{6,5},{7,6},{9,8},{10,9},{11,10},{12... | collective-permute-start | bytes 1572872 | tf_op jit(solution)/shard_map/ppermute | solution.py:463
  50.0 1.9 %collective-permute-start.2 = (f32[4,64,128]{2,1,0:T(8,128)S(1)}, f32[4,64,128]{2,1,0:T(8,128)S(1)}, u32[]{:S(2)}, u32[]{:S(2)}) collective-permute-start(f32[4,64,128]{2,1,0:T(8,128)S(1)} %slice.19), channel_id=1, source_target_pairs={{9,0},{10,1},{11,2},{12,3},{13,4},{14,5},{15,6},{17,8},{18,9},{19,... | collective-permute-start | bytes 393224 | tf_op jit(solution)/shard_map/ppermute | solution.py:470
  51.9 29.6 %collective-permute-done.2.diag_ref = f32[4,64,128]{2,1,0:T(8,128)S(1)} collective-permute-done((f32[4,64,128]{2,1,0:T(8,128)S(1)}, f32[4,64,128]{2,1,0:T(8,128)S(1)}, u32[]{:S(2)}, u32[]{:S(2)}) %collective-permute-start.2) | collective-permute-done | bytes 131104 | tf_op jit(solution)/shard_map/ppermute | solution.py:470
  81.5 0.0 collective-permute-done.below_ref
  81.5 0.0 collective-permute-done.1.right_ref
  81.5 0.0 copy-done.1
  81.5 0.0 copy-done.2
  81.6 16.8 %forward_fields.1 = (f32[16,256,256]{2,1,0:T(8,128)}, f32[16,256,256]{2,1,0:T(8,128)}) custom-call(f32[4,256,512]{2,1,0:T(8,128)S(1)} %bitcast.6, f32[4,64,512]{2,1,0:T(8,128)S(1)} %collective-permute-done.below_ref, f32[4,256,128]{2,1,0:T(8,128)S(1)} %collective-permute-done.1.right_ref, f32[4,64,128]{2,1,0:T(8,128)S(1)} %collective-permute-done.2.diag_ref, ...), custom_call_target="tpu_custom_call" | custom-call | flops 6442450944 | bytes 14680064 | tf_op jit(solution)/shard_map/forward_fields/pallas_call | solution.py:219
  98.4 0.0 all-to-all-done.recv_ref
  98.4 0.8 slice_convert_fusion
  99.2 0.1 copy.9
  99.3 0.1 copy.10.corner_ref
  99.4 0.0 copy-start.3
  99.4 1.2 copy-done.3
  100.6 20.5 %backward_fields.1 = (f32[4,256,512]{2,1,0:T(8,128)}, f32[4,256,128]{2,1,0:T(8,128)S(1)}, f32[4,64,512]{2,1,0:T(8,128)S(1)}, f32[4,64,128]{2,1,0:T(8,128)S(1)}) custom-call(s32[16,2]{1,0:T(8,128)S(1)} %copy.10.corner_ref, f32[16,264,128]{2,1,0:T(8,128)} %all-to-all-done.recv_ref, f32[4,256,512]{2,1,0:T(8,128)S(1)} %bitcast.7, ...), custom_call_target="tpu_custom_call" | custom-call | flops 6442450944 | bytes 14680064 | tf_op jit(solution)/shard_map/backward_fields/pallas_call | solution.py:370
  121.1 1.9 %collective-permute-start.3 = (f32[4,64,512]{2,1,0:T(8,128)S(1)}, f32[4,64,512]{2,1,0:T(8,128)S(1)}, u32[]{:S(2)}, u32[]{:S(2)}) collective-permute-start(f32[4,64,512]{2,1,0:T(8,128)S(1)} %get-tuple-element.14), channel_id=1, source_target_pairs={{0,8},{8,16},{16,24},{24,32},{32,40},{40,48},{48,56},{56,64},{64,7... | collective-permute-start | bytes 1572872 | tf_op jit(solution)/shard_map/ppermute | solution.py:460
  123.0 4.9 %collective-permute-start.4 = (f32[4,256,128]{2,1,0:T(8,128)S(1)}, f32[4,256,128]{2,1,0:T(8,128)S(1)}, u32[]{:S(2)}, u32[]{:S(2)}) collective-permute-start(f32[4,256,128]{2,1,0:T(8,128)S(1)} %get-tuple-element.15), channel_id=1, source_target_pairs={{0,1},{1,2},{2,3},{3,4},{4,5},{5,6},{6,7},{8,9},{9,10},{10,11},{11... | collective-permute-start | bytes 1572872 | tf_op jit(solution)/shard_map/ppermute | solution.py:463
  128.0 2.5 %collective-permute-start.5 = (f32[4,64,128]{2,1,0:T(8,128)S(1)}, f32[4,64,128]{2,1,0:T(8,128)S(1)}, u32[]{:S(2)}, u32[]{:S(2)}) collective-permute-start(f32[4,64,128]{2,1,0:T(8,128)S(1)} %get-tuple-element.16), channel_id=1, source_target_pairs={{0,9},{1,10},{2,11},{3,12},{4,13},{5,14},{6,15},{8,17},{9,18},{10,... | collective-permute-start | bytes 393224 | tf_op jit(solution)/shard_map/ppermute | solution.py:470
  130.5 10.9 %collective-permute-done.5.diag_ref = f32[4,64,128]{2,1,0:T(8,128)S(1)} collective-permute-done((f32[4,64,128]{2,1,0:T(8,128)S(1)}, f32[4,64,128]{2,1,0:T(8,128)S(1)}, u32[]{:S(2)}, u32[]{:S(2)}) %collective-permute-start.5) | collective-permute-done | bytes 131104 | tf_op jit(solution)/shard_map/ppermute | solution.py:470
  141.4 0.2 collective-permute-done.3.above_ref
  141.6 0.0 collective-permute-done.4.left_ref
  141.6 2.2 %add_borders.1 = f32[4,256,512]{2,1,0:T(8,128)} custom-call(f32[4,256,512]{2,1,0:T(8,128)} %get-tuple-element.13.own_ref, f32[4,64,512]{2,1,0:T(8,128)S(1)} %collective-permute-done.3.above_ref, f32[4,256,128]{2,1,0:T(8,128)S(1)} %collective-permute-done.4.left_ref, f32[4,64,128]{2,1,0:T(8,128)S(1)} %collective-permute-done.5.diag_ref), custom_call_target="tpu_custom_call", output_to_operand_aliasing={{}: (0, {})} | custom-call | tf_op jit(solution)/shard_map/add_borders/pallas_call | solution.py:439
  (2 shorter events, 0.1 us)
Async XLA Ops:
  33.7 7.9 %copy-start = (f32[2,2,256,512]{3,2,1,0:T(8,128)S(1)}, f32[2,2,256,512]{3,2,1,0:T(8,128)}, u32[]{:S(2)}) copy-start(f32[2,2,256,512]{3,2,1,0:T(8,128)} %param.5) | copy-start | bytes 6291460
  33.8 64.6 %all-to-all-start = ((f32[16,264,128]{2,1,0:T(8,128)}), f32[16,264,128]{2,1,0:T(8,128)}, u32[]{:S(2)}, u32[]{:S(2)}) async-start(f32[16,264,128]{2,1,0:T(8,128)} %pack_measured.1), calls=%async_computation | async-start | bytes 4325376 | tf_op jit(solution)/shard_map/all_to_all | solution.py:479
  41.6 39.9 %copy-start.1 = (f32[2,128,128]{2,1,0:T(8,128)S(1)}, f32[2,128,128]{2,1,0:T(8,128)}, u32[]{:S(2)}) copy-start(f32[2,128,128]{2,1,0:T(8,128)} %probe_ref.3) | copy-start | bytes 393220
  41.6 39.9 %copy-start.2 = (bf16[8,256,256]{2,1,0:T(8,128)(2,1)S(1)}, bf16[8,256,256]{2,1,0:T(8,128)(2,1)}, u32[]{:S(2)}) copy-start(bf16[8,256,256]{2,1,0:T(8,128)(2,1)} %constant.2.clone.tables) | copy-start | bytes 3145732
  41.7 39.9 %collective-permute-start = (f32[4,64,512]{2,1,0:T(8,128)S(1)}, f32[4,64,512]{2,1,0:T(8,128)S(1)}, u32[]{:S(2)}, u32[]{:S(2)}) collective-permute-start(f32[4,64,512]{2,1,0:T(8,128)S(1)} %slice.17), channel_id=1, source_target_pairs={{8,0},{16,8},{24,16},{32,24},{40,32},{48,40},{56,48},{64,56},{72,6... | collective-permute-start | bytes 1572872 | tf_op jit(solution)/shard_map/ppermute | solution.py:460
  46.5 35.0 %collective-permute-start.1 = (f32[4,256,128]{2,1,0:T(8,128)S(1)}, f32[4,256,128]{2,1,0:T(8,128)S(1)}, u32[]{:S(2)}, u32[]{:S(2)}) collective-permute-start(f32[4,256,128]{2,1,0:T(8,128)S(1)} %slice.18), channel_id=1, source_target_pairs={{1,0},{2,1},{3,2},{4,3},{5,4},{6,5},{7,6},{9,8},{10,9},{11,10},{12... | collective-permute-start | bytes 1572872 | tf_op jit(solution)/shard_map/ppermute | solution.py:463
  50.0 31.6 %collective-permute-start.2 = (f32[4,64,128]{2,1,0:T(8,128)S(1)}, f32[4,64,128]{2,1,0:T(8,128)S(1)}, u32[]{:S(2)}, u32[]{:S(2)}) collective-permute-start(f32[4,64,128]{2,1,0:T(8,128)S(1)} %slice.19), channel_id=1, source_target_pairs={{9,0},{10,1},{11,2},{12,3},{13,4},{14,5},{15,6},{17,8},{18,9},{19,... | collective-permute-start | bytes 393224 | tf_op jit(solution)/shard_map/ppermute | solution.py:470
  99.4 1.2 copy-start.3
  121.1 20.5 %collective-permute-start.3 = (f32[4,64,512]{2,1,0:T(8,128)S(1)}, f32[4,64,512]{2,1,0:T(8,128)S(1)}, u32[]{:S(2)}, u32[]{:S(2)}) collective-permute-start(f32[4,64,512]{2,1,0:T(8,128)S(1)} %get-tuple-element.14), channel_id=1, source_target_pairs={{0,8},{8,16},{16,24},{24,32},{32,40},{40,48},{48,56},{56,64},{64,7... | collective-permute-start | bytes 1572872 | tf_op jit(solution)/shard_map/ppermute | solution.py:460
  123.0 18.5 %collective-permute-start.4 = (f32[4,256,128]{2,1,0:T(8,128)S(1)}, f32[4,256,128]{2,1,0:T(8,128)S(1)}, u32[]{:S(2)}, u32[]{:S(2)}) collective-permute-start(f32[4,256,128]{2,1,0:T(8,128)S(1)} %get-tuple-element.15), channel_id=1, source_target_pairs={{0,1},{1,2},{2,3},{3,4},{4,5},{5,6},{6,7},{8,9},{9,10},{10,11},{11... | collective-permute-start | bytes 1572872 | tf_op jit(solution)/shard_map/ppermute | solution.py:463
  128.0 13.5 %collective-permute-start.5 = (f32[4,64,128]{2,1,0:T(8,128)S(1)}, f32[4,64,128]{2,1,0:T(8,128)S(1)}, u32[]{:S(2)}, u32[]{:S(2)}) collective-permute-start(f32[4,64,128]{2,1,0:T(8,128)S(1)} %get-tuple-element.16), channel_id=1, source_target_pairs={{0,9},{1,10},{2,11},{3,12},{4,13},{5,14},{6,15},{8,17},{9,18},{10,... | collective-permute-start | bytes 393224 | tf_op jit(solution)/shard_map/ppermute | solution.py:470

commit v2 on v1

v2 whole, which is shorter than its diff:
```python
import functools
import math

import jax
import jax.numpy as jnp
import ml_dtypes
import numpy as np
from jax import lax
from jax.experimental import pallas as pl
from jax.experimental.pallas import tpu as pltpu
from jax.sharding import PartitionSpec as P

PHASE = 40.0
SIDE = 128
BLOCK = 64
CAP = 2
META = 8
VMEM_LIMIT = 48 * 1024 * 1024


def dft_matrix():
    index = np.arange(SIDE)
    angle = (index[:, None] * index[None, :] % SIDE) * (-2.0 * math.pi / SIDE)
    return np.exp(1j * angle) / math.sqrt(SIDE)


def propagation_matrix():
    index = np.arange(SIDE)
    freq = np.where(index < SIDE // 2, index, index - SIDE) / SIDE
    dft = dft_matrix()
    return np.conj(dft) @ (np.exp(-1j * PHASE * freq * freq)[:, None] * dft)


def real_forms(matrix):
    right = np.block([[matrix.real, matrix.imag], [-matrix.imag, matrix.real]])
    out = []
    for form in (right, right.T):
        form = form.astype(np.float32)
        high = form.astype(ml_dtypes.bfloat16)
        out.append(high)
        out.append((form - high.astype(np.float32)).astype(ml_dtypes.bfloat16))
    return np.stack(out)


TABLES = np.concatenate([real_forms(propagation_matrix()), real_forms(dft_matrix())])


def split(field):
    high = field.astype(jnp.bfloat16)
    low = (field - high.astype(jnp.float32)).astype(jnp.bfloat16)
    return high, low


def from_right(rows, tables, at):
    high, low = split(rows)
    left = jnp.concatenate([high, low, high], axis=1)
    right = jnp.concatenate([tables[at], tables[at], tables[at + 1]], axis=0)
    return jnp.dot(left, right, preferred_element_type=jnp.float32)


def from_left(columns, tables, at):
    high, low = split(columns)
    left = jnp.concatenate([tables[at], tables[at], tables[at + 1]], axis=1)
    right = jnp.concatenate([high, low, high], axis=0)
    return jnp.dot(left, right, preferred_element_type=jnp.float32)


def swap(pair):
    top = jnp.concatenate([pair[:SIDE, :SIDE], pair[SIDE:, :SIDE]], axis=1)
    bottom = jnp.concatenate([pair[:SIDE, SIDE:], pair[SIDE:, SIDE:]], axis=1)
    return jnp.concatenate([top, bottom], axis=0)


def two_sided(pairs, tables, right_at, left_at):
    pairs = [from_right(rows, tables, right_at) for rows in pairs]
    return [from_left(swap(rows), tables, left_at) for rows in pairs]


def stacked(fields):
    return jnp.concatenate([jnp.concatenate(field, axis=1) for field in fields], axis=0)


def halves(pair, n):
    return pair[:SIDE, n * SIDE : (n + 1) * SIDE], pair[SIDE:, n * SIDE : (n + 1) * SIDE]


def low_lanes(shape):
    return lax.broadcasted_iota(jnp.int32, shape, len(shape) - 1) < BLOCK


def cut_pair(ext_ref, comp, row, col):
    first = ext_ref[comp, row : row + SIDE, col : col + SIDE]
    second = ext_ref[comp, row : row + SIDE, col + SIDE : col + 2 * SIDE]
    mixed = jnp.where(low_lanes(first.shape), second, first)
    return first, pltpu.roll(mixed, BLOCK, 1)


def times(left_re, left_im, right_re, right_im):
    return (left_re * right_re - left_im * right_im, left_re * right_im + left_im * right_re)


def conj_times(left_re, left_im, right_re, right_im):
    return (left_re * right_re + left_im * right_im, left_re * right_im - left_im * right_re)


def pack_kernel(off_ref, meas_ref, send_ref, meta_ref, count_ref, corner_ref, sems):
    owners = send_ref.shape[0]
    positions = meas_ref.shape[0]
    for owner in range(owners):
        count_ref[owner] = 0
        for rank in range(CAP):
            corner_ref[owner * CAP + rank] = -1
    copies = []
    for pos in range(positions):
        y = off_ref[0, pos]
        x = off_ref[1, pos]
        owner = lax.shift_right_logical(y, 8)
        rank = jnp.minimum(count_ref[owner], CAP - 1)
        count_ref[owner] = rank + 1
        corner = (lax.shift_right_logical(y, 6) & 3) * 8 + (lax.shift_right_logical(x, 6) & 7)
        corner_ref[owner * CAP + rank] = corner
        copy = pltpu.make_async_copy(
            meas_ref.at[pos],
            send_ref.at[owner, pl.ds(pl.multiple_of(rank * SIDE, SIDE), SIDE)],
            sems.at[pos],
        )
        copy.start()
        copies.append(copy)
    row = lax.broadcasted_iota(jnp.int32, (META, SIDE), 0)
    for owner in range(owners):
        both = jnp.where(row == 0, corner_ref[owner * CAP], corner_ref[owner * CAP + 1])
        meta_ref[owner] = both.astype(jnp.float32)
    copy = pltpu.make_async_copy(
        meta_ref, send_ref.at[:, pl.ds(CAP * SIDE, META)], sems.at[positions]
    )
    copy.start()
    copies.append(copy)
    for copy in copies:
        copy.wait()


def pack(offsets, measured, owners):
    positions = measured.shape[0]
    return pl.pallas_call(
        pack_kernel,
        out_shape=jax.ShapeDtypeStruct((owners, CAP * SIDE + META, SIDE), jnp.float32),
        in_specs=[
            pl.BlockSpec(memory_space=pltpu.SMEM),
            pl.BlockSpec(memory_space=pltpu.VMEM),
        ],
        out_specs=pl.BlockSpec(memory_space=pl.ANY),
        scratch_shapes=[
            pltpu.VMEM((owners, META, SIDE), jnp.float32),
            pltpu.SMEM((owners,), jnp.int32),
            pltpu.SMEM((owners * CAP,), jnp.int32),
            pltpu.SemaphoreType.DMA((positions + 1,)),
        ],
        cost_estimate=pl.CostEstimate(
            flops=0, bytes_accessed=40 * 1024 * 1024, transcendentals=0
        ),
        name="pack_measured",
    )(offsets, measured)


def pair_places(rows, cols):
    row_blocks = rows // BLOCK
    last = cols - SIDE
    rim = [(row_blocks - 1, col) for col in range(0, cols, SIDE)]
    rim += [(row, last) for row in range(row_blocks - 1)]
    inner = [(row, col) for row in range(row_blocks - 1) for col in range(0, last, SIDE)]
    return rim, inner


def forward_pairs(places, ext_ref, probe_ref, tables, far_ref, enter_ref):
    probe_re = probe_ref[0]
    probe_im = probe_ref[1]
    rows = []
    for row, col in places:
        trans = [cut_pair(ext_ref, comp, row * BLOCK, col) for comp in range(2)]
        rows.append(
            stacked([times(probe_re, probe_im, trans[0][n], trans[1][n]) for n in range(2)])
        )
    enters = two_sided(rows, tables, 0, 2)
    rows = []
    for pair, (row, col) in enumerate(places):
        enter = enters[pair]
        enter_ref[pair] = enter
        trans = [cut_pair(ext_ref, comp, row * BLOCK, col) for comp in range(2, 4)]
        rows.append(
            stacked([times(*halves(enter, n), trans[0][n], trans[1][n]) for n in range(2)])
        )
    fars = two_sided(rows, tables, 4, 6)
    for pair in range(len(places)):
        far_ref[pair] = fars[pair]


def extended_parts(tile_ref, below_ref, right_ref, diag_ref, ext_ref, first):
    rows, cols = tile_ref.shape[1:]
    comps = pl.ds(first, tile_ref.shape[0] - first)
    return [
        (tile_ref.at[comps], ext_ref.at[:, pl.ds(0, rows), pl.ds(0, cols)]),
        (below_ref.at[comps], ext_ref.at[:, pl.ds(rows, BLOCK), pl.ds(0, cols)]),
        (right_ref.at[comps], ext_ref.at[:, pl.ds(0, rows), pl.ds(cols, SIDE)]),
        (diag_ref.at[comps], ext_ref.at[:, pl.ds(rows, BLOCK), pl.ds(cols, SIDE)]),
    ]


def start_copies(parts, sems):
    copies = [
        pltpu.make_async_copy(source, target, sems.at[n])
        for n, (source, target) in enumerate(parts)
    ]
    for copy in copies:
        copy.start()
    return copies


def wait_copies(copies):
    for copy in copies:
        copy.wait()


def forward_inner_kernel(places, tile_ref, probe_ref, tables, far_ref, enter_ref):
    forward_pairs(places, tile_ref, probe_ref, tables, far_ref, enter_ref)


def forward_rim_kernel(
    places,
    tile_ref,
    below_ref,
    right_ref,
    diag_ref,
    probe_ref,
    tables,
    far_ref,
    enter_ref,
    ext_ref,
    sems,
):
    wait_copies(
        start_copies(
            extended_parts(tile_ref, below_ref, right_ref, diag_ref, ext_ref, 0), sems
        )
    )
    forward_pairs(places, ext_ref, probe_ref, tables, far_ref, enter_ref)


def stage_cost(pairs):
    return pl.CostEstimate(
        flops=pairs * 4 * 3 * 2 * 256**3, bytes_accessed=1024 * 1024, transcendentals=0
    )


def fields(places):
    field = jax.ShapeDtypeStruct((len(places), 2 * SIDE, 2 * SIDE), jnp.float32)
    return field, field


def in_vmem(count):
    return [pl.BlockSpec(memory_space=pltpu.VMEM)] * count


def anywhere(count):
    return [pl.BlockSpec(memory_space=pl.ANY)] * count


def forward_inner(places, tile, probe, tables):
    return pl.pallas_call(
        functools.partial(forward_inner_kernel, places),
        out_shape=fields(places),
        in_specs=in_vmem(3),
        out_specs=tuple(in_vmem(2)),
        compiler_params=pltpu.CompilerParams(vmem_limit_bytes=VMEM_LIMIT),
        cost_estimate=stage_cost(8 * len(places)),
        name="forward_inner",
    )(tile, probe, tables)


def extended_shape(tile, comps):
    return pltpu.VMEM((comps, tile.shape[1] + BLOCK, tile.shape[2] + SIDE), jnp.float32)


def forward_rim(places, tile, below, right, diag, probe, tables):
    return pl.pallas_call(
        functools.partial(forward_rim_kernel, places),
        out_shape=fields(places),
        in_specs=anywhere(4) + in_vmem(2),
        out_specs=tuple(in_vmem(2)),
        scratch_shapes=[extended_shape(tile, tile.shape[0]), pltpu.SemaphoreType.DMA((4,))],
        compiler_params=pltpu.CompilerParams(vmem_limit_bytes=VMEM_LIMIT),
        cost_estimate=stage_cost(8 * len(places)),
        name="forward_rim",
    )(tile, below, right, diag, probe, tables)


def gather_sums(corner_ref, recv_ref, sum_ref, count_ref):
    sum_ref[...] = jnp.zeros_like(sum_ref)
    for corner in range(sum_ref.shape[0]):
        count_ref[corner] = 0
    for source in range(recv_ref.shape[0]):
        for rank in range(CAP):
            corner = corner_ref[source, rank]

            @pl.when(corner >= 0)
            def _():
                count_ref[corner] = count_ref[corner] + 1
                sum_ref[corner] = (
                    sum_ref[corner] + recv_ref[source, rank * SIDE : (rank + 1) * SIDE]
                )


def backward_pairs(
    places, width, probe_ref, tables, far_ref, enter_ref, ext_ref, sum_ref, count_ref, store
):
    probe_re = probe_ref[0]
    probe_im = probe_ref[1]
    rows = []
    for pair, (row, col) in enumerate(places):
        waves = []
        for n in range(2):
            at = row * width + col // BLOCK + n
            hits = count_ref[at].astype(jnp.float32)
            far_re, far_im = halves(far_ref[pair], n)
            misfit = 2.0 * (hits * (far_re * far_re + far_im * far_im) - sum_ref[at])
            waves.append((misfit * far_re, misfit * far_im))
        rows.append(stacked(waves))
    backs = two_sided(rows, tables, 6, 4)
    rows = []
    for pair, (row, col) in enumerate(places):
        trans = [cut_pair(ext_ref, comp, row * BLOCK, col) for comp in range(2)]
        waves = []
        for n in range(2):
            back = halves(backs[pair], n)
            grad = conj_times(*halves(enter_ref[pair], n), *back)
            store(n, 2, row, col, grad[0])
            store(n, 3, row, col, grad[1])
            waves.append(conj_times(trans[0][n], trans[1][n], *back))
        rows.append(stacked(waves))
    backs = two_sided(rows, tables, 2, 0)
    for pair, (row, col) in enumerate(places):
        for n in range(2):
            grad = conj_times(probe_re, probe_im, *halves(backs[pair], n))
            store(n, 0, row, col, grad[0])
            store(n, 1, row, col, grad[1])


def shifted(low, high):
    if low is None:
        low = jnp.zeros_like(high)
    if high is None:
        high = jnp.zeros_like(low)
    return pltpu.roll(jnp.where(low_lanes(low.shape), high, low), BLOCK, 1)


def backward_rim_kernel(
    places,
    corner_ref,
    recv_ref,
    tile_ref,
    below_ref,
    right_ref,
    diag_ref,
    probe_ref,
    tables,
    far_ref,
    enter_ref,
    row_ref,
    col_ref,
    out_right_ref,
    out_below_ref,
    out_diag_ref,
    ext_ref,
    sum_ref,
    count_ref,
    even_ref,
    odd_ref,
    even_side_ref,
    odd_side_ref,
    sems,
):
    rows, cols = tile_ref.shape[1:]
    last = rows // BLOCK - 1
    copies = start_copies(
        extended_parts(tile_ref, below_ref, right_ref, diag_ref, ext_ref, 2), sems
    )
    gather_sums(corner_ref, recv_ref, sum_ref, count_ref)
    wait_copies(copies)
    bands = (even_ref, odd_ref)
    sides = (even_side_ref, odd_side_ref)

    def store(n, comp, row, col, value):
        if row == last:
            bands[n][comp, :, col : col + SIDE] = value
        else:
            at = row * BLOCK
            top = value[:BLOCK]
            if row > 0:
                top = top + sides[n][comp, at : at + BLOCK]
            sides[n][comp, at : at + BLOCK] = top
            sides[n][comp, at + BLOCK : at + SIDE] = value[BLOCK:]

    backward_pairs(
        places,
        cols // BLOCK,
        probe_ref,
        tables,
        far_ref,
        enter_ref,
        ext_ref,
        sum_ref,
        count_ref,
        store,
    )
    for comp in range(4):
        odd_side = odd_side_ref[comp]
        col_ref[comp] = even_side_ref[comp] + shifted(None, odd_side)
        side = shifted(odd_side, None)
        for out_ref, rim_ref, part in (
            (row_ref, None, slice(0, BLOCK)),
            (out_below_ref, out_diag_ref, slice(BLOCK, SIDE)),
        ):
            before = None
            for col in range(0, cols, SIDE):
                here = odd_ref[comp, part, col : col + SIDE]
                out_ref[comp, :, col : col + SIDE] = even_ref[
                    comp, part, col : col + SIDE
                ] + shifted(before, here)
                before = here
            beyond = shifted(before, None)
            if rim_ref is None:
                out_right_ref[comp, : rows - BLOCK] = side[: rows - BLOCK]
                out_right_ref[comp, rows - BLOCK :] = side[rows - BLOCK :] + beyond
            else:
                rim_ref[comp] = beyond


def backward_inner_kernel(
    places,
    corner_ref,
    recv_ref,
    tile_ref,
    probe_ref,
    tables,
    far_ref,
    enter_ref,
    row_ref,
    col_ref,
    out_ref,
    sum_ref,
    count_ref,
    even_ref,
    odd_ref,
):
    rows, cols = out_ref.shape[1:]
    last = rows - BLOCK
    gather_sums(corner_ref, recv_ref, sum_ref, count_ref)
    acc = (even_ref, odd_ref)

    def store(n, comp, row, col, value):
        at = row * BLOCK
        lanes = slice(col, col + SIDE)
        top = value[:BLOCK]
        if row > 0:
            top = top + acc[n][comp, at : at + BLOCK, lanes]
        acc[n][comp, at : at + BLOCK, lanes] = top
        acc[n][comp, at + BLOCK : at + SIDE, lanes] = value[BLOCK:]

    backward_pairs(
        places,
        cols // BLOCK,
        probe_ref,
        tables,
        far_ref,
        enter_ref,
        tile_ref.at[pl.ds(2, 2)],
        sum_ref,
        count_ref,
        store,
    )
    for comp in range(4):
        before = None
        for col in range(0, cols, SIDE):
            lanes = slice(col, col + SIDE)
            if col < cols - SIDE:
                here = odd_ref[comp, :, lanes]
                value = even_ref[comp, :, lanes] + shifted(before, here)
                before = here
            else:
                value = col_ref[comp] + shifted(before, None)
            out_ref[comp, :last, lanes] = value[:last]
            out_ref[comp, last:, lanes] = value[last:] + row_ref[comp, :, lanes]


def backward_rim(places, corner, recv, tile, below, right, diag, probe, tables, far, enter):
    comps, rows, cols = tile.shape
    corners = (rows // BLOCK) * (cols // BLOCK)
    shapes = (
        (comps, BLOCK, cols),
        (comps, rows, SIDE),
        (comps, rows, SIDE),
        (comps, BLOCK, cols),
        (comps, BLOCK, SIDE),
    )
    return pl.pallas_call(
        functools.partial(backward_rim_kernel, places),
        out_shape=tuple(jax.ShapeDtypeStruct(shape, jnp.float32) for shape in shapes),
        in_specs=[pl.BlockSpec(memory_space=pltpu.SMEM)] + in_vmem(1) + anywhere(4) + in_vmem(4),
        out_specs=tuple(in_vmem(5)),
        scratch_shapes=[
            extended_shape(tile, 2),
            pltpu.VMEM((corners, SIDE, SIDE), jnp.float32),
            pltpu.SMEM((corners,), jnp.int32),
            pltpu.VMEM((comps, SIDE, cols), jnp.float32),
            pltpu.VMEM((comps, SIDE, cols), jnp.float32),
            pltpu.VMEM((comps, rows, SIDE), jnp.float32),
            pltpu.VMEM((comps, rows, SIDE), jnp.float32),
            pltpu.SemaphoreType.DMA((4,)),
        ],
        compiler_params=pltpu.CompilerParams(vmem_limit_bytes=VMEM_LIMIT),
        cost_estimate=stage_cost(len(places)),
        name="backward_rim",
    )(corner, recv, tile, below, right, diag, probe, tables, far, enter)


def backward_inner(places, corner, recv, tile, probe, tables, far, enter, row, col):
    comps, rows, cols = tile.shape
    corners = (rows // BLOCK) * (cols // BLOCK)
    return pl.pallas_call(
        functools.partial(backward_inner_kernel, places),
        out_shape=jax.ShapeDtypeStruct(tile.shape, jnp.float32),
        in_specs=[pl.BlockSpec(memory_space=pltpu.SMEM)] + in_vmem(8),
        out_specs=pl.BlockSpec(memory_space=pltpu.VMEM),
        scratch_shapes=[
            pltpu.VMEM((corners, SIDE, SIDE), jnp.float32),
            pltpu.SMEM((corners,), jnp.int32),
            pltpu.VMEM((comps, rows, cols - SIDE), jnp.float32),
            pltpu.VMEM((comps, rows, cols - SIDE), jnp.float32),
        ],
        compiler_params=pltpu.CompilerParams(vmem_limit_bytes=VMEM_LIMIT),
        cost_estimate=stage_cost(8 * len(places)),
        name="backward_inner",
    )(corner, recv, tile, probe, tables, far, enter, row, col)


def border_kernel(own_ref, above_ref, left_ref, diag_ref, out_ref, top_ref, side_ref, sems):
    comps, rows, cols = out_ref.shape
    top = out_ref.at[:, pl.ds(0, BLOCK)]
    side = out_ref.at[:, pl.ds(BLOCK, rows - BLOCK), pl.ds(0, SIDE)]
    loads = [
        pltpu.make_async_copy(top, top_ref, sems.at[0]),
        pltpu.make_async_copy(side, side_ref, sems.at[1]),
    ]
    for copy in loads:
        copy.start()
    for copy in loads:
        copy.wait()
    top_ref[...] = top_ref[...] + above_ref[...]
    top_ref[:, :, :SIDE] = top_ref[:, :, :SIDE] + left_ref[:, :BLOCK] + diag_ref[...]
    side_ref[...] = side_ref[...] + left_ref[:, BLOCK:]
    stores = [
        pltpu.make_async_copy(top_ref, top, sems.at[0]),
        pltpu.make_async_copy(side_ref, side, sems.at[1]),
    ]
    for copy in stores:
        copy.start()
    for copy in stores:
        copy.wait()


def add_borders(own, above, left, diag):
    comps, rows, cols = own.shape
    vmem = pl.BlockSpec(memory_space=pltpu.VMEM)
    return pl.pallas_call(
        border_kernel,
        out_shape=jax.ShapeDtypeStruct(own.shape, jnp.float32),
        in_specs=[pl.BlockSpec(memory_space=pl.ANY), vmem, vmem, vmem],
        out_specs=pl.BlockSpec(memory_space=pl.ANY),
        scratch_shapes=[
            pltpu.VMEM((comps, BLOCK, cols), jnp.float32),
            pltpu.VMEM((comps, rows - BLOCK, SIDE), jnp.float32),
            pltpu.SemaphoreType.DMA((2,)),
        ],
        input_output_aliases={0: 0},
        compiler_params=pltpu.CompilerParams(vmem_limit_bytes=VMEM_LIMIT),
        name="add_borders",
    )(own, above, left, diag)


def moved(shard, down, across):
    row_total = lax.axis_size("row")
    col_total = lax.axis_size("col")
    if across == 0:
        pairs = [(r, r + down) for r in range(row_total) if 0 <= r + down < row_total]
        return lax.ppermute(shard, "row", pairs)
    if down == 0:
        pairs = [(c, c + across) for c in range(col_total) if 0 <= c + across < col_total]
        return lax.ppermute(shard, "col", pairs)
    pairs = [
        (r * col_total + c, (r + down) * col_total + c + across)
        for r in range(row_total)
        for c in range(col_total)
        if 0 <= r + down < row_total and 0 <= c + across < col_total
    ]
    return lax.ppermute(shard, ("row", "col"), pairs)


def body(object_slices, probe, measured, offsets):
    slices, parts, tile_rows, tile_cols = object_slices.shape
    tile = object_slices.reshape(slices * parts, tile_rows, tile_cols)
    row_total = lax.axis_size("row")
    tables = jnp.asarray(TABLES)
    send = pack(offsets, measured, row_total)
    recv = lax.all_to_all(send, "row", split_axis=0, concat_axis=0, tiled=True)
    below = moved(tile[:, :BLOCK, :], -1, 0)
    right = moved(tile[:, :, :SIDE], 0, -1)
    diag = moved(tile[:, :BLOCK, :SIDE], -1, -1)
    rim, inner = pair_places(tile_rows, tile_cols)
    far_inner, enter_inner = forward_inner(inner, tile, probe, tables)
    far_rim, enter_rim = forward_rim(rim, tile, below, right, diag, probe, tables)
    corner = recv[:, CAP * SIDE : CAP * SIDE + CAP, 0].astype(jnp.int32)
    row, col, to_right, to_below, to_diag = backward_rim(
        rim, corner, recv, tile, below, right, diag, probe, tables, far_rim, enter_rim
    )
    above = moved(to_below, 1, 0)
    left = moved(to_right, 0, 1)
    corner_part = moved(to_diag, 1, 1)
    own = backward_inner(
        inner, corner, recv, tile, probe, tables, far_inner, enter_inner, row, col
    )
    result = add_borders(own, above, left, corner_part)
    return result.reshape(object_slices.shape)


def solution(mesh):
    placed = (
        P(None, None, "row", "col"),
        P(),
        P(("row", "col"), None, None),
        P(None, ("row", "col")),
    )
    return jax.shard_map(
        body, mesh=mesh, in_specs=placed, out_specs=P(None, None, "row", "col"), check_vma=False
    )
```

time: 147 us -> 86.3 us (0.59); the launches traced: 144 us -> 84.8 us
  Pallas kernels: 73.2 us -> 31 us
  waiting for transfers between devices: 40.7 us -> 16.5 us
  local copies, waits for them, and re-layouts: 1.55 us -> 11.2 us
  starting transfers between devices: 27.3 us -> 25 us
    ppermute x2, waiting for transfers between devices: 40.6 us -> 0.01 us  [moved(): return lax.ppermute(shard, ('row', 'col'), pairs)]
    pallas_call x1, Pallas kernels: 33.7 us -> 2.41 us  [pack(): pl.pallas_call(pack_kernel, out_shape=jax.ShapeDtypeStruct((owners, CAP *...]
    all_to_all x1, waiting for transfers between devices: 0.01 us -> 13.6 us  [body(): recv = lax.all_to_all(send, 'row', split_axis=0, concat_axis=0, tiled=True)]
    pallas_call x2 -> x4, Pallas kernels: 37.3 us -> 26.4 us  [the longest x1 9.51 us: backward_inner(): pl.pallas_call(functools.partial(backward_inner_kernel, places), out_shap...]
    ppermute x2, starting transfers between devices: 4.44 us -> 11.6 us  [moved(): return lax.ppermute(shard, ('row', 'col'), pairs)]
    unnamed x8 -> x18, local copies, waits for them, and re-layouts: 1.24 us -> 6.33 us
    ppermute x2, starting transfers between devices: 8.34 us -> 4.38 us  [moved(): return lax.ppermute(shard, 'col', pairs)]
    ppermute x2, waiting for transfers between devices: 0.16 us -> 2.91 us  [moved(): return lax.ppermute(shard, 'row', pairs)]
  transfers between devices with their start and end apart: 7 -> 7, of which waited for: 3 -> 2; matrix products, arithmetic and copies ran while one was open for 0% -> 4% of each run, Pallas kernels for 12% -> 25%
where the time goes in v2:
time: 86.3 us; the launch traced here: 84.8 us
  Pallas kernels  31 us (36%)
  starting transfers between devices  25 us (29%)
  waiting for transfers between devices  16.5 us (19%)
  local copies, waits for them, and re-layouts  11.2 us (13%)
    all_to_all x1, waiting for transfers between devices, body(): recv = lax.all_to_all(send, 'row', split_axis=0, concat_axis=0, tiled=True)  13.6 us
    ppermute x2, starting transfers between devices, moved(): return lax.ppermute(shard, ('row', 'col'), pairs)  11.6 us
    pallas_call x1, Pallas kernels, backward_inner(): pl.pallas_call(functools.partial(backward_inner_kernel, places), out_shap...  9.51 us
    pallas_call x1, Pallas kernels, backward_rim(): pl.pallas_call(functools.partial(backward_rim_kernel, places), out_shape=...  7.74 us
    unnamed x18, local copies, waits for them, and re-layouts  6.33 us
    all_to_all x1, starting transfers between devices, body(): recv = lax.all_to_all(send, 'row', split_axis=0, concat_axis=0, tiled=True)  5.17 us
    pallas_call x1, Pallas kernels, forward_rim(): pl.pallas_call(functools.partial(forward_rim_kernel, places), out_shape=f...  4.92 us
    ppermute x2, starting transfers between devices, moved(): return lax.ppermute(shard, 'col', pairs)  4.38 us
  transfers between devices with their start and end apart: 7, of which 2 were waited for; matrix products, arithmetic and copies ran while one was open for 4% of the time, Pallas kernels for 25%

profile of v2, /device:TPU:7, one launch (start us, length us, event | category | flops | bytes accessed | tf_op | source)
XLA Modules:
  0.0 84.8 jit_solution(12017999190218320279)
XLA Ops:
  0.0 0.9 %slice.19 = f32[4,64,128]{2,1,0:T(8,128)S(1)} slice(f32[4,256,512]{2,1,0:T(8,128)} %bitcast.3), slice={[0:4], [0:64], [0:128]} | slice | bytes 262144 | tf_op jit(solution)/shard_map/slice | solution.py:616
  0.9 6.5 %collective-permute-start.2 = (f32[4,64,128]{2,1,0:T(8,128)S(1)}, f32[4,64,128]{2,1,0:T(8,128)S(1)}, u32[]{:S(2)}, u32[]{:S(2)}) collective-permute-start(f32[4,64,128]{2,1,0:T(8,128)S(1)} %slice.19), channel_id=1, source_target_pairs={{9,0},{10,1},{11,2},{12,3},{13,4},{14,5},{15,6},{17,8},{18,9},{19,... | collective-permute-start | bytes 393224 | tf_op jit(solution)/shard_map/ppermute | solution.py:604
  7.4 1.9 %slice.17 = f32[4,64,512]{2,1,0:T(8,128)} slice(f32[4,256,512]{2,1,0:T(8,128)} %bitcast.4), slice={[0:4], [0:64], [0:512]} | slice | bytes 1048576 | tf_op jit(solution)/shard_map/slice | solution.py:614
  9.3 2.0 %collective-permute-start = (f32[4,64,512]{2,1,0:T(8,128)}, f32[4,64,512]{2,1,0:T(8,128)S(1)}, u32[]{:S(2)}, u32[]{:S(2)}) collective-permute-start(f32[4,64,512]{2,1,0:T(8,128)} %slice.17), channel_id=1, source_target_pairs={{8,0},{16,8},{24,16},{32,24},{40,32},{48,40},{56,48},{64,56},{72,6... | collective-permute-start | bytes 1572872 | tf_op jit(solution)/shard_map/ppermute | solution.py:594
  11.3 1.9 %slice.18 = f32[4,256,128]{2,1,0:T(8,128)} slice(f32[4,256,512]{2,1,0:T(8,128)} %bitcast.5), slice={[0:4], [0:256], [0:128]} | slice | bytes 1048576 | tf_op jit(solution)/shard_map/slice | solution.py:615
  13.2 1.9 %collective-permute-start.1 = (f32[4,256,128]{2,1,0:T(8,128)}, f32[4,256,128]{2,1,0:T(8,128)S(1)}, u32[]{:S(2)}, u32[]{:S(2)}) collective-permute-start(f32[4,256,128]{2,1,0:T(8,128)} %slice.18), channel_id=1, source_target_pairs={{1,0},{2,1},{3,2},{4,3},{5,4},{6,5},{7,6},{9,8},{10,9},{11,10},{12... | collective-permute-start | bytes 1572872 | tf_op jit(solution)/shard_map/ppermute | solution.py:597
  15.1 2.4 %pack_measured.1 = f32[16,264,128]{2,1,0:T(8,128)} custom-call(s32[2,16]{1,0:T(2,128)} %off_ref.1, f32[16,128,128]{2,1,0:T(8,128)} %meas_ref.1), custom_call_target="tpu_custom_call" | custom-call | bytes 41943040 | tf_op jit(solution)/shard_map/pack_measured/pallas_call | solution.py:144
  17.5 0.0 copy-start
  17.5 0.0 copy-start.2
  17.6 5.2 %all-to-all-start = ((f32[16,264,128]{2,1,0:T(8,128)}), f32[16,264,128]{2,1,0:T(8,128)}, u32[]{:S(2)}, u32[]{:S(2)}) async-start(f32[16,264,128]{2,1,0:T(8,128)} %pack_measured.1), calls=%async_computation | async-start | bytes 4325376 | tf_op jit(solution)/shard_map/all_to_all | solution.py:613
  22.7 0.0 copy-start.3
  22.8 1.2 %copy-done.3 = bf16[8,256,256]{2,1,0:T(8,128)(2,1)S(1)} copy-done((bf16[8,256,256]{2,1,0:T(8,128)(2,1)S(1)}, bf16[8,256,256]{2,1,0:T(8,128)(2,1)}, u32[]{:S(2)}) %copy-start.3) | copy-done | bytes 1048600
  24.0 4.2 %forward_inner.1 = (f32[9,256,256]{2,1,0:T(8,128)S(1)}, f32[9,256,256]{2,1,0:T(8,128)}) custom-call(f32[4,256,512]{2,1,0:T(8,128)S(1)} %bitcast.8, f32[2,128,128]{2,1,0:T(8,128)S(1)} %copy-done.2, bf16[8,256,256]{2,1,0:T(8,128)(2,1)S(1)} %copy-done.3), custom_call_target="tpu_custom_call" | custom-call | flops 28991029248 | bytes 1048576 | tf_op jit(solution)/shard_map/forward_inner/pallas_call | solution.py:268
  28.2 1.4 %copy-done.8 = f32[9,256,256]{2,1,0:T(8,128)} copy-done((f32[9,256,256]{2,1,0:T(8,128)}, f32[9,256,256]{2,1,0:T(8,128)S(1)}, u32[]{:S(2)}) %copy-start.8) | copy-done | bytes 2359320
  29.6 0.0 collective-permute-done.1.right_ref
  29.6 4.9 %forward_rim.1 = (f32[7,256,256]{2,1,0:T(8,128)S(1)}, f32[7,256,256]{2,1,0:T(8,128)S(1)}) custom-call(f32[4,256,512]{2,1,0:T(8,128)} %bitcast.6, f32[4,64,512]{2,1,0:T(8,128)S(1)} %collective-permute-done.below_ref, f32[4,256,128]{2,1,0:T(8,128)S(1)} %collective-permute-done.1.right_ref, f32[4,64,128]{2,1,0:T(8,128)S(1)} %collective-permute-done.2.diag_ref, ...), custom_call_target="tpu_custom_call" | custom-call | flops 22548578304 | bytes 1048576 | tf_op jit(solution)/shard_map/forward_rim/pallas_call | solution.py:284
  34.5 0.0 copy-start.6
  34.6 1.2 %copy-done.6 = f32[7,256,256]{2,1,0:T(8,128)} copy-done((f32[7,256,256]{2,1,0:T(8,128)}, f32[7,256,256]{2,1,0:T(8,128)S(1)}, u32[]{:S(2)}) %copy-start.6) | copy-done | bytes 1835032
  35.8 1.2 %copy-done.7 = f32[7,256,256]{2,1,0:T(8,128)} copy-done((f32[7,256,256]{2,1,0:T(8,128)}, f32[7,256,256]{2,1,0:T(8,128)S(1)}, u32[]{:S(2)}) %copy-start.7) | copy-done | bytes 1835032
  37.0 13.6 %all-to-all-done.recv_ref = f32[16,264,128]{2,1,0:T(8,128)} async-done(((f32[16,264,128]{2,1,0:T(8,128)}), f32[16,264,128]{2,1,0:T(8,128)}, u32[]{:S(2)}, u32[]{:S(2)}) %all-to-all-start) | async-done | bytes 2162720 | tf_op jit(solution)/shard_map/all_to_all | solution.py:613
  50.6 0.8 slice_convert_fusion
  51.4 0.1 copy.10
  51.5 0.1 copy.12.corner_ref
  51.6 1.2 %copy-done.4 = bf16[8,256,256]{2,1,0:T(8,128)(2,1)S(1)} copy-done((bf16[8,256,256]{2,1,0:T(8,128)(2,1)S(1)}, bf16[8,256,256]{2,1,0:T(8,128)(2,1)}, u32[]{:S(2)}) %copy-start.4) | copy-done | bytes 1048600
  52.8 7.7 %backward_rim.1 = (f32[4,64,512]{2,1,0:T(8,128)S(1)}, f32[4,256,128]{2,1,0:T(8,128)S(1)}, f32[4,256,128]{2,1,0:T(8,128)S(1)}, f32[4,64,512]{2,1,0:T(8,128)S(1)}, f32[4,64,128]{2,1,0:T(8,128)S(1)}) custom-call(s32[16,2]{1,0:T(8,128)S(1)} %copy.12.corner_ref, f32[16,264,128]{2,1,0:T(8,128)} %all-to-all-done.recv_ref, f32[4,256,512]{2,1,0:T(8,128)} %bitcast.7, ...), custom_call_target="tpu_custom_call" | custom-call | flops 2818572288 | bytes 1048576 | tf_op jit(solution)/shard_map/backward_rim/pallas_call | solution.py:504
  60.6 5.1 %collective-permute-start.5 = (f32[4,64,128]{2,1,0:T(8,128)S(1)}, f32[4,64,128]{2,1,0:T(8,128)S(1)}, u32[]{:S(2)}, u32[]{:S(2)}) collective-permute-start(f32[4,64,128]{2,1,0:T(8,128)S(1)} %get-tuple-element.22), channel_id=1, source_target_pairs={{0,9},{1,10},{2,11},{3,12},{4,13},{5,14},{6,15},{8,17},{9,18},{10,... | collective-permute-start | bytes 393224 | tf_op jit(solution)/shard_map/ppermute | solution.py:604
  65.6 1.9 %collective-permute-start.3 = (f32[4,64,512]{2,1,0:T(8,128)S(1)}, f32[4,64,512]{2,1,0:T(8,128)S(1)}, u32[]{:S(2)}, u32[]{:S(2)}) collective-permute-start(f32[4,64,512]{2,1,0:T(8,128)S(1)} %get-tuple-element.20), channel_id=1, source_target_pairs={{0,8},{8,16},{16,24},{24,32},{32,40},{40,48},{48,56},{56,64},{64,7... | collective-permute-start | bytes 1572872 | tf_op jit(solution)/shard_map/ppermute | solution.py:594
  67.6 2.5 %collective-permute-start.4 = (f32[4,256,128]{2,1,0:T(8,128)S(1)}, f32[4,256,128]{2,1,0:T(8,128)S(1)}, u32[]{:S(2)}, u32[]{:S(2)}) collective-permute-start(f32[4,256,128]{2,1,0:T(8,128)S(1)} %get-tuple-element.21), channel_id=1, source_target_pairs={{0,1},{1,2},{2,3},{3,4},{4,5},{5,6},{6,7},{8,9},{9,10},{10,11},{11... | collective-permute-start | bytes 1572872 | tf_op jit(solution)/shard_map/ppermute | solution.py:597
  70.1 9.5 %backward_inner.1.own_ref = f32[4,256,512]{2,1,0:T(8,128)} custom-call(s32[16,2]{1,0:T(8,128)S(1)} %copy.12.corner_ref, f32[16,264,128]{2,1,0:T(8,128)} %all-to-all-done.recv_ref, f32[4,256,512]{2,1,0:T(8,128)S(1)} %bitcast.9, f32[2,128,128]{2,1,0:T(8,128)S(1)} %copy-done.2, bf16[8,256,256]{2,1,0:T(8,128)(2,1)S(1)} %copy-done.5, f32[9,256,256]{2,1,0:T(8,128)} %copy-done.8, ...), custom_call_target="tpu_custom_call" | custom-call | flops 28991029248 | bytes 1048576 | tf_op jit(solution)/shard_map/backward_inner/pallas_call | solution.py:528
  79.6 0.0 collective-permute-done.5.diag_ref
  79.6 2.9 %collective-permute-done.3.above_ref = f32[4,64,512]{2,1,0:T(8,128)S(1)} collective-permute-done((f32[4,64,512]{2,1,0:T(8,128)S(1)}, f32[4,64,512]{2,1,0:T(8,128)S(1)}, u32[]{:S(2)}, u32[]{:S(2)}) %collective-permute-start.3) | collective-permute-done | bytes 524320 | tf_op jit(solution)/shard_map/ppermute | solution.py:594
  82.5 2.2 %add_borders.1 = f32[4,256,512]{2,1,0:T(8,128)} custom-call(f32[4,256,512]{2,1,0:T(8,128)} %backward_inner.1.own_ref, f32[4,64,512]{2,1,0:T(8,128)S(1)} %collective-permute-done.3.above_ref, f32[4,256,128]{2,1,0:T(8,128)S(1)} %collective-permute-done.4.left_ref, f32[4,64,128]{2,1,0:T(8,128)S(1)} %collective-permute-done.5.diag_ref), custom_call_target="tpu_custom_call", output_to_operand_aliasing={{}: (0, {})} | custom-call | tf_op jit(solution)/shard_map/add_borders/pallas_call | solution.py:573
  (12 shorter events, 0.0 us)
Async XLA Ops:
  0.9 28.7 %collective-permute-start.2 = (f32[4,64,128]{2,1,0:T(8,128)S(1)}, f32[4,64,128]{2,1,0:T(8,128)S(1)}, u32[]{:S(2)}, u32[]{:S(2)}) collective-permute-start(f32[4,64,128]{2,1,0:T(8,128)S(1)} %slice.19), channel_id=1, source_target_pairs={{9,0},{10,1},{11,2},{12,3},{13,4},{14,5},{15,6},{17,8},{18,9},{19,... | collective-permute-start | bytes 393224 | tf_op jit(solution)/shard_map/ppermute | solution.py:604
  9.3 20.3 %collective-permute-start = (f32[4,64,512]{2,1,0:T(8,128)}, f32[4,64,512]{2,1,0:T(8,128)S(1)}, u32[]{:S(2)}, u32[]{:S(2)}) collective-permute-start(f32[4,64,512]{2,1,0:T(8,128)} %slice.17), channel_id=1, source_target_pairs={{8,0},{16,8},{24,16},{32,24},{40,32},{48,40},{56,48},{64,56},{72,6... | collective-permute-start | bytes 1572872 | tf_op jit(solution)/shard_map/ppermute | solution.py:594
  13.2 16.4 %collective-permute-start.1 = (f32[4,256,128]{2,1,0:T(8,128)}, f32[4,256,128]{2,1,0:T(8,128)S(1)}, u32[]{:S(2)}, u32[]{:S(2)}) collective-permute-start(f32[4,256,128]{2,1,0:T(8,128)} %slice.18), channel_id=1, source_target_pairs={{1,0},{2,1},{3,2},{4,3},{5,4},{6,5},{7,6},{9,8},{10,9},{11,10},{12... | collective-permute-start | bytes 1572872 | tf_op jit(solution)/shard_map/ppermute | solution.py:597
  17.5 5.2 %copy-start = (f32[2,2,256,512]{3,2,1,0:T(8,128)S(1)}, f32[2,2,256,512]{3,2,1,0:T(8,128)}, u32[]{:S(2)}) copy-start(f32[2,2,256,512]{3,2,1,0:T(8,128)} %param.5) | copy-start | bytes 6291460
  17.5 5.2 %copy-start.2 = (f32[2,128,128]{2,1,0:T(8,128)S(1)}, f32[2,128,128]{2,1,0:T(8,128)}, u32[]{:S(2)}) copy-start(f32[2,128,128]{2,1,0:T(8,128)} %probe_ref.7) | copy-start | bytes 393220
  17.6 33.0 %all-to-all-start = ((f32[16,264,128]{2,1,0:T(8,128)}), f32[16,264,128]{2,1,0:T(8,128)}, u32[]{:S(2)}, u32[]{:S(2)}) async-start(f32[16,264,128]{2,1,0:T(8,128)} %pack_measured.1), calls=%async_computation | async-start | bytes 4325376 | tf_op jit(solution)/shard_map/all_to_all | solution.py:613
  22.7 1.2 %copy-start.3 = (bf16[8,256,256]{2,1,0:T(8,128)(2,1)S(1)}, bf16[8,256,256]{2,1,0:T(8,128)(2,1)}, u32[]{:S(2)}) copy-start(bf16[8,256,256]{2,1,0:T(8,128)(2,1)} %constant.2.clone.tables) | copy-start | bytes 3145732
  28.2 1.4 %copy-start.8 = (f32[9,256,256]{2,1,0:T(8,128)}, f32[9,256,256]{2,1,0:T(8,128)S(1)}, u32[]{:S(2)}) copy-start(f32[9,256,256]{2,1,0:T(8,128)S(1)} %get-tuple-element.14.far_ref) | copy-start | bytes 7077892
  34.5 1.2 %copy-start.6 = (f32[7,256,256]{2,1,0:T(8,128)}, f32[7,256,256]{2,1,0:T(8,128)S(1)}, u32[]{:S(2)}) copy-start(f32[7,256,256]{2,1,0:T(8,128)S(1)} %get-tuple-element.16.far_ref) | copy-start | bytes 5505028
  35.8 1.2 %copy-start.7 = (f32[7,256,256]{2,1,0:T(8,128)}, f32[7,256,256]{2,1,0:T(8,128)S(1)}, u32[]{:S(2)}) copy-start(f32[7,256,256]{2,1,0:T(8,128)S(1)} %get-tuple-element.17.enter_ref) | copy-start | bytes 5505028
  51.6 1.2 %copy-start.4 = (bf16[8,256,256]{2,1,0:T(8,128)(2,1)S(1)}, bf16[8,256,256]{2,1,0:T(8,128)(2,1)}, u32[]{:S(2)}) copy-start(bf16[8,256,256]{2,1,0:T(8,128)(2,1)} %constant.2.clone.tables) | copy-start | bytes 3145732
  52.8 17.2 %copy-start.1 = (f32[2,2,256,512]{3,2,1,0:T(8,128)S(1)}, f32[2,2,256,512]{3,2,1,0:T(8,128)}, u32[]{:S(2)}) copy-start(f32[2,2,256,512]{3,2,1,0:T(8,128)} %param.5) | copy-start | bytes 6291460
  52.8 17.2 %copy-start.5 = (bf16[8,256,256]{2,1,0:T(8,128)(2,1)S(1)}, bf16[8,256,256]{2,1,0:T(8,128)(2,1)}, u32[]{:S(2)}) copy-start(bf16[8,256,256]{2,1,0:T(8,128)(2,1)} %constant.2.clone.tables) | copy-start | bytes 3145732
  60.6 19.0 %collective-permute-start.5 = (f32[4,64,128]{2,1,0:T(8,128)S(1)}, f32[4,64,128]{2,1,0:T(8,128)S(1)}, u32[]{:S(2)}, u32[]{:S(2)}) collective-permute-start(f32[4,64,128]{2,1,0:T(8,128)S(1)} %get-tuple-element.22), channel_id=1, source_target_pairs={{0,9},{1,10},{2,11},{3,12},{4,13},{5,14},{6,15},{8,17},{9,18},{10,... | collective-permute-start | bytes 393224 | tf_op jit(solution)/shard_map/ppermute | solution.py:604
  65.6 16.9 %collective-permute-start.3 = (f32[4,64,512]{2,1,0:T(8,128)S(1)}, f32[4,64,512]{2,1,0:T(8,128)S(1)}, u32[]{:S(2)}, u32[]{:S(2)}) collective-permute-start(f32[4,64,512]{2,1,0:T(8,128)S(1)} %get-tuple-element.20), channel_id=1, source_target_pairs={{0,8},{8,16},{16,24},{24,32},{32,40},{40,48},{48,56},{56,64},{64,7... | collective-permute-start | bytes 1572872 | tf_op jit(solution)/shard_map/ppermute | solution.py:594
  67.6 14.9 %collective-permute-start.4 = (f32[4,256,128]{2,1,0:T(8,128)S(1)}, f32[4,256,128]{2,1,0:T(8,128)S(1)}, u32[]{:S(2)}, u32[]{:S(2)}) collective-permute-start(f32[4,256,128]{2,1,0:T(8,128)S(1)} %get-tuple-element.21), channel_id=1, source_target_pairs={{0,1},{1,2},{2,3},{3,4},{4,5},{5,6},{6,7},{8,9},{9,10},{10,11},{11... | collective-permute-start | bytes 1572872 | tf_op jit(solution)/shard_map/ppermute | solution.py:597

commit v3 on v2

--- a/solution.py
+++ b/solution.py
@@ -15,7 +15,7 @@
 BLOCK = 64
 CAP = 2
 META = 8
-VMEM_LIMIT = 48 * 1024 * 1024
+VMEM_LIMIT = 28 * 1024 * 1024
 
 
 def dft_matrix():
@@ -126,9 +126,9 @@
         )
         copy.start()
         copies.append(copy)
-    row = lax.broadcasted_iota(jnp.int32, (META, SIDE), 0)
+    first = low_lanes((META, SIDE))
     for owner in range(owners):
-        both = jnp.where(row == 0, corner_ref[owner * CAP], corner_ref[owner * CAP + 1])
+        both = jnp.where(first, corner_ref[owner * CAP], corner_ref[owner * CAP + 1])
         meta_ref[owner] = both.astype(jnp.float32)
     copy = pltpu.make_async_copy(
         meta_ref, send_ref.at[:, pl.ds(CAP * SIDE, META)], sems.at[positions]
@@ -164,14 +164,14 @@
 
 def pair_places(rows, cols):
     row_blocks = rows // BLOCK
-    last = cols - SIDE
-    rim = [(row_blocks - 1, col) for col in range(0, cols, SIDE)]
-    rim += [(row, last) for row in range(row_blocks - 1)]
-    inner = [(row, col) for row in range(row_blocks - 1) for col in range(0, last, SIDE)]
-    return rim, inner
-
-
-def forward_pairs(places, ext_ref, probe_ref, tables, far_ref, enter_ref):
+    edge = cols - SIDE
+    last = tuple((row_blocks - 1, col) for col in range(0, cols, SIDE))
+    side = tuple((row, edge) for row in range(row_blocks - 1))
+    inner = tuple((row, col) for row in range(row_blocks - 1) for col in range(0, edge, SIDE))
+    return last, side, inner
+
+
+def forward_pairs(places, ext_ref, probe_ref, tables, far_refs, enter_refs):
     probe_re = probe_ref[0]
     probe_im = probe_ref[1]
     rows = []
@@ -184,14 +184,18 @@
     rows = []
     for pair, (row, col) in enumerate(places):
         enter = enters[pair]
-        enter_ref[pair] = enter
+        enter_refs[pair][...] = enter
         trans = [cut_pair(ext_ref, comp, row * BLOCK, col) for comp in range(2, 4)]
         rows.append(
             stacked([times(*halves(enter, n), trans[0][n], trans[1][n]) for n in range(2)])
         )
     fars = two_sided(rows, tables, 4, 6)
-    for pair in range(len(places)):
-        far_ref[pair] = fars[pair]
+    for far_ref, far in zip(far_refs, fars):
+        far_ref[...] = far
+
+
+def each(ref):
+    return [ref.at[pair] for pair in range(ref.shape[0])]
 
 
 def extended_parts(tile_ref, below_ref, right_ref, diag_ref, ext_ref, first):
@@ -221,7 +225,7 @@
 
 
 def forward_inner_kernel(places, tile_ref, probe_ref, tables, far_ref, enter_ref):
-    forward_pairs(places, tile_ref, probe_ref, tables, far_ref, enter_ref)
+    forward_pairs(places, tile_ref, probe_ref, tables, each(far_ref), each(enter_ref))
 
 
 def forward_rim_kernel(
@@ -232,8 +236,10 @@
     diag_ref,
     probe_ref,
     tables,
-    far_ref,
-    enter_ref,
+    far_last_ref,
+    enter_last_ref,
+    far_side_ref,
+    enter_side_ref,
     ext_ref,
     sems,
 ):
@@ -242,7 +248,14 @@
             extended_parts(tile_ref, below_ref, right_ref, diag_ref, ext_ref, 0), sems
         )
     )
-    forward_pairs(places, ext_ref, probe_ref, tables, far_ref, enter_ref)
+    forward_pairs(
+        places,
+        ext_ref,
+        probe_ref,
+        tables,
+        each(far_last_ref) + each(far_side_ref),
+        each(enter_last_ref) + each(enter_side_ref),
+    )
 
 
 def stage_cost(pairs):
@@ -280,12 +293,13 @@
     return pltpu.VMEM((comps, tile.shape[1] + BLOCK, tile.shape[2] + SIDE), jnp.float32)
 
 
-def forward_rim(places, tile, below, right, diag, probe, tables):
+def forward_rim(last, side, tile, below, right, diag, probe, tables):
+    places = last + side
     return pl.pallas_call(
         functools.partial(forward_rim_kernel, places),
-        out_shape=fields(places),
+        out_shape=fields(last) + fields(side),
         in_specs=anywhere(4) + in_vmem(2),
-        out_specs=tuple(in_vmem(2)),
+        out_specs=tuple(in_vmem(4)),
         scratch_shapes=[extended_shape(tile, tile.shape[0]), pltpu.SemaphoreType.DMA((4,))],
         compiler_params=pltpu.CompilerParams(vmem_limit_bytes=VMEM_LIMIT),
         cost_estimate=stage_cost(8 * len(places)),
@@ -293,24 +307,23 @@
     )(tile, below, right, diag, probe, tables)
 
 
-def gather_sums(corner_ref, recv_ref, sum_ref, count_ref):
+def gather_sums(corner_ref, recv_ref, sum_ref, count_ref, first):
+    corners = sum_ref.shape[0]
     sum_ref[...] = jnp.zeros_like(sum_ref)
-    for corner in range(sum_ref.shape[0]):
+    for corner in range(corners):
         count_ref[corner] = 0
     for source in range(recv_ref.shape[0]):
         for rank in range(CAP):
-            corner = corner_ref[source, rank]
-
-            @pl.when(corner >= 0)
+            at = corner_ref[source, rank] - first
+
+            @pl.when(jnp.logical_and(at >= 0, at < corners))
             def _():
-                count_ref[corner] = count_ref[corner] + 1
-                sum_ref[corner] = (
-                    sum_ref[corner] + recv_ref[source, rank * SIDE : (rank + 1) * SIDE]
-                )
+                count_ref[at] = count_ref[at] + 1
+                sum_ref[at] = sum_ref[at] + recv_ref[source, rank * SIDE : (rank + 1) * SIDE]
 
 
 def backward_pairs(
-    places, width, probe_ref, tables, far_ref, enter_ref, ext_ref, sum_ref, count_ref, store
+    places, corner_of, probe_ref, tables, far_ref, enter_ref, ext_ref, sum_ref, count_ref, store
 ):
     probe_re = probe_ref[0]
     probe_im = probe_ref[1]
@@ -318,7 +331,7 @@
     for pair, (row, col) in enumerate(places):
         waves = []
         for n in range(2):
-            at = row * width + col // BLOCK + n
+            at = corner_of(row, col) + n
             hits = count_ref[at].astype(jnp.float32)
             far_re, far_im = halves(far_ref[pair], n)
             misfit = 2.0 * (hits * (far_re * far_re + far_im * far_im) - sum_ref[at])
@@ -352,71 +365,86 @@
     return pltpu.roll(jnp.where(low_lanes(low.shape), high, low), BLOCK, 1)
 
 
-def backward_rim_kernel(
+def backward_last_kernel(
     places,
-    corner_ref,
     recv_ref,
     tile_ref,
     below_ref,
     right_ref,
     diag_ref,
     probe_ref,
-    tables,
+    tables_ref,
     far_ref,
     enter_ref,
     row_ref,
-    col_ref,
-    out_right_ref,
+    right_part_ref,
     out_below_ref,
     out_diag_ref,
+    corner_ref,
+    items_ref,
+    table_buf,
+    probe_buf,
+    far_buf,
+    enter_buf,
     ext_ref,
     sum_ref,
     count_ref,
+    meta_ref,
     even_ref,
     odd_ref,
-    even_side_ref,
-    odd_side_ref,
     sems,
 ):
     rows, cols = tile_ref.shape[1:]
-    last = rows // BLOCK - 1
+    corners = sum_ref.shape[0]
+    start = rows - BLOCK
+    two = pl.ds(2, 2)
+    above = pl.ds(0, BLOCK)
+    under = pl.ds(BLOCK, BLOCK)
+    wide = pl.ds(0, cols)
+    beyond = pl.ds(cols, SIDE)
+    low = pl.ds(start, BLOCK)
     copies = start_copies(
-        extended_parts(tile_ref, below_ref, right_ref, diag_ref, ext_ref, 2), sems
-    )
-    gather_sums(corner_ref, recv_ref, sum_ref, count_ref)
-    wait_copies(copies)
+        [
+            (recv_ref.at[:, CAP * SIDE], meta_ref),
+            (recv_ref.at[:, pl.ds(0, CAP * SIDE)], items_ref),
+            (far_ref, far_buf),
+            (tables_ref, table_buf),
+            (tile_ref.at[two, low], ext_ref.at[:, above, wide]),
+            (below_ref.at[two], ext_ref.at[:, under, wide]),
+            (right_ref.at[two, low], ext_ref.at[:, above, beyond]),
+            (diag_ref.at[two], ext_ref.at[:, under, beyond]),
+            (enter_ref, enter_buf),
+            (probe_ref, probe_buf),
+        ],
+        sems,
+    )
+    wait_copies(copies[:1])
+    for source in range(corner_ref.shape[0]):
+        for rank in range(CAP):
+            corner_ref[source, rank] = meta_ref[source, rank * BLOCK].astype(jnp.int32)
+    wait_copies(copies[1:2])
+    gather_sums(corner_ref, items_ref, sum_ref, count_ref, start // BLOCK * corners)
+    wait_copies(copies[2:])
     bands = (even_ref, odd_ref)
-    sides = (even_side_ref, odd_side_ref)
 
     def store(n, comp, row, col, value):
-        if row == last:
-            bands[n][comp, :, col : col + SIDE] = value
-        else:
-            at = row * BLOCK
-            top = value[:BLOCK]
-            if row > 0:
-                top = top + sides[n][comp, at : at + BLOCK]
-            sides[n][comp, at : at + BLOCK] = top
-            sides[n][comp, at + BLOCK : at + SIDE] = value[BLOCK:]
+        bands[n][comp, :, col : col + SIDE] = value
 
     backward_pairs(
-        places,
-        cols // BLOCK,
-        probe_ref,
-        tables,
-        far_ref,
-        enter_ref,
+        [(0, col) for _, col in places],
+        lambda row, col: col // BLOCK,
+        probe_buf,
+        table_buf,
+        far_buf,
+        enter_buf,
         ext_ref,
         sum_ref,
         count_ref,
         store,
     )
     for comp in range(4):
-        odd_side = odd_side_ref[comp]
-        col_ref[comp] = even_side_ref[comp] + shifted(None, odd_side)
-        side = shifted(odd_side, None)
-        for out_ref, rim_ref, part in (
-            (row_ref, None, slice(0, BLOCK)),
+        for out_ref, side_ref, part in (
+            (row_ref, right_part_ref, slice(0, BLOCK)),
             (out_below_ref, out_diag_ref, slice(BLOCK, SIDE)),
         ):
             before = None
@@ -426,18 +454,80 @@
                     comp, part, col : col + SIDE
                 ] + shifted(before, here)
                 before = here
-            beyond = shifted(before, None)
-            if rim_ref is None:
-                out_right_ref[comp, : rows - BLOCK] = side[: rows - BLOCK]
-                out_right_ref[comp, rows - BLOCK :] = side[rows - BLOCK :] + beyond
-            else:
-                rim_ref[comp] = beyond
-
-
-def backward_inner_kernel(
+            side_ref[comp] = shifted(before, None)
+
+
+def backward_side_kernel(
     places,
     corner_ref,
     recv_ref,
+    tile_ref,
+    right_ref,
+    probe_ref,
+    tables,
+    far_ref,
+    enter_ref,
+    right_part_ref,
+    col_ref,
+    out_right_ref,
+    sum_ref,
+    count_ref,
+    ext_ref,
+    even_ref,
+    odd_ref,
+    sems,
+):
+    rows, cols = tile_ref.shape[1:]
+    edge = cols - SIDE
+    last = rows - BLOCK
+    width = cols // BLOCK
+    two = pl.ds(2, 2)
+    copies = start_copies(
+        [
+            (tile_ref.at[two, :, pl.ds(edge, SIDE)], ext_ref.at[:, :, pl.ds(0, SIDE)]),
+            (right_ref.at[two], ext_ref.at[:, :, pl.ds(SIDE, SIDE)]),
+        ],
+        sems,
+    )
+    gather_sums(corner_ref, recv_ref, sum_ref, count_ref, 0)
+    wait_copies(copies)
+    acc = (even_ref, odd_ref)
+
+    def store(n, comp, row, col, value):
+        at = row * BLOCK
+        top = value[:BLOCK]
+        if row > 0:
+            top = top + acc[n][comp, at : at + BLOCK]
+        acc[n][comp, at : at + BLOCK] = top
+        acc[n][comp, at + BLOCK : at + SIDE] = value[BLOCK:]
+
+    backward_pairs(
+        [(row, 0) for row, _ in places],
+        lambda row, col: row * width + edge // BLOCK,
+        probe_ref,
+        tables,
+        far_ref,
+        enter_ref,
+        ext_ref,
+        sum_ref,
+        count_ref,
+        store,
+    )
+    half = rows // 2
+    for comp in range(4):
+        col_ref[comp] = even_ref[comp] + shifted(None, odd_ref[comp])
+        side = shifted(odd_ref[comp], None)
+        first = side[:half]
+        second = jnp.concatenate(
+            [side[half:last], side[last:] + right_part_ref[comp]], axis=0
+        )
+        out_right_ref[comp] = first + pltpu.roll(second, BLOCK, 1)
+
+
+def backward_inner_kernel(
+    places,
+    count_ref,
+    sum_ref,
     tile_ref,
     probe_ref,
     tables,
@@ -446,14 +536,12 @@
     row_ref,
     col_ref,
     out_ref,
-    sum_ref,
-    count_ref,
     even_ref,
     odd_ref,
 ):
     rows, cols = out_ref.shape[1:]
     last = rows - BLOCK
-    gather_sums(corner_ref, recv_ref, sum_ref, count_ref)
+    width = cols // BLOCK
     acc = (even_ref, odd_ref)
 
     def store(n, comp, row, col, value):
@@ -467,7 +555,7 @@
 
     backward_pairs(
         places,
-        cols // BLOCK,
+        lambda row, col: row * width + col // BLOCK,
         probe_ref,
         tables,
         far_ref,
@@ -491,99 +579,162 @@
             out_ref[comp, last:, lanes] = value[last:] + row_ref[comp, :, lanes]
 
 
-def backward_rim(places, corner, recv, tile, below, right, diag, probe, tables, far, enter):
+def shapes_of(*shapes):
+    return tuple(jax.ShapeDtypeStruct(shape, jnp.float32) for shape in shapes)
+
+
+def backward_last(places, recv, tile, below, right, diag, probe, tables, far, enter):
     comps, rows, cols = tile.shape
-    corners = (rows // BLOCK) * (cols // BLOCK)
-    shapes = (
-        (comps, BLOCK, cols),
-        (comps, rows, SIDE),
-        (comps, rows, SIDE),
-        (comps, BLOCK, cols),
-        (comps, BLOCK, SIDE),
-    )
+    corners = cols // BLOCK
+    sources = recv.shape[0]
+    edge = (comps, BLOCK, cols)
+    side = (comps, BLOCK, SIDE)
     return pl.pallas_call(
-        functools.partial(backward_rim_kernel, places),
-        out_shape=tuple(jax.ShapeDtypeStruct(shape, jnp.float32) for shape in shapes),
-        in_specs=[pl.BlockSpec(memory_space=pltpu.SMEM)] + in_vmem(1) + anywhere(4) + in_vmem(4),
-        out_specs=tuple(in_vmem(5)),
+        functools.partial(backward_last_kernel, places),
+        out_shape=shapes_of(edge, side, edge, side)
+        + (jax.ShapeDtypeStruct((sources, CAP), jnp.int32),),
+        in_specs=anywhere(9),
+        out_specs=tuple(in_vmem(4)) + (pl.BlockSpec(memory_space=pltpu.SMEM),),
         scratch_shapes=[
-            extended_shape(tile, 2),
+            pltpu.VMEM((sources, CAP * SIDE, SIDE), jnp.float32),
+            pltpu.VMEM(tables.shape, tables.dtype),
+            pltpu.VMEM(probe.shape, jnp.float32),
+            pltpu.VMEM(far.shape, jnp.float32),
+            pltpu.VMEM(enter.shape, jnp.float32),
+            pltpu.VMEM((2, SIDE, cols + SIDE), jnp.float32),
             pltpu.VMEM((corners, SIDE, SIDE), jnp.float32),
             pltpu.SMEM((corners,), jnp.int32),
+            pltpu.SMEM((sources, SIDE), jnp.float32),
             pltpu.VMEM((comps, SIDE, cols), jnp.float32),
             pltpu.VMEM((comps, SIDE, cols), jnp.float32),
+            pltpu.SemaphoreType.DMA((10,)),
+        ],
+        compiler_params=pltpu.CompilerParams(vmem_limit_bytes=VMEM_LIMIT),
+        cost_estimate=stage_cost(len(places)),
+        name="backward_last_row",
+    )(recv, tile, below, right, diag, probe, tables, far, enter)
+
+
+def backward_side(places, corner, recv, tile, right, probe, tables, far, enter, right_part):
+    comps, rows, cols = tile.shape
+    corners = (rows // BLOCK - 1) * (cols // BLOCK)
+    return pl.pallas_call(
+        functools.partial(backward_side_kernel, places),
+        out_shape=shapes_of(
+            (comps, rows, SIDE), (comps, rows // 2, SIDE), (corners, SIDE, SIDE)
+        )
+        + (jax.ShapeDtypeStruct((corners,), jnp.int32),),
+        in_specs=[pl.BlockSpec(memory_space=pltpu.SMEM)]
+        + in_vmem(1)
+        + anywhere(2)
+        + in_vmem(5),
+        out_specs=tuple(in_vmem(3)) + (pl.BlockSpec(memory_space=pltpu.SMEM),),
+        scratch_shapes=[
+            pltpu.VMEM((2, rows, 2 * SIDE), jnp.float32),
             pltpu.VMEM((comps, rows, SIDE), jnp.float32),
             pltpu.VMEM((comps, rows, SIDE), jnp.float32),
-            pltpu.SemaphoreType.DMA((4,)),
+            pltpu.SemaphoreType.DMA((2,)),
         ],
         compiler_params=pltpu.CompilerParams(vmem_limit_bytes=VMEM_LIMIT),
-        cost_estimate=stage_cost(len(places)),
-        name="backward_rim",
-    )(corner, recv, tile, below, right, diag, probe, tables, far, enter)
-
-
-def backward_inner(places, corner, recv, tile, probe, tables, far, enter, row, col):
+        cost_estimate=stage_cost(8 * len(places)),
+        name="backward_last_column",
+    )(corner, recv, tile, right, probe, tables, far, enter, right_part)
+
+
+def backward_inner(places, count, sums, tile, probe, tables, far, enter, row, col):
     comps, rows, cols = tile.shape
-    corners = (rows // BLOCK) * (cols // BLOCK)
     return pl.pallas_call(
         functools.partial(backward_inner_kernel, places),
         out_shape=jax.ShapeDtypeStruct(tile.shape, jnp.float32),
         in_specs=[pl.BlockSpec(memory_space=pltpu.SMEM)] + in_vmem(8),
         out_specs=pl.BlockSpec(memory_space=pltpu.VMEM),
         scratch_shapes=[
-            pltpu.VMEM((corners, SIDE, SIDE), jnp.float32),
-            pltpu.SMEM((corners,), jnp.int32),
             pltpu.VMEM((comps, rows, cols - SIDE), jnp.float32),
             pltpu.VMEM((comps, rows, cols - SIDE), jnp.float32),
         ],
         compiler_params=pltpu.CompilerParams(vmem_limit_bytes=VMEM_LIMIT),
-        cost_estimate=stage_cost(8 * len(places)),
+        cost_estimate=stage_cost(len(places)),
         name="backward_inner",
-    )(corner, recv, tile, probe, tables, far, enter, row, col)
-
-
-def border_kernel(own_ref, above_ref, left_ref, diag_ref, out_ref, top_ref, side_ref, sems):
-    comps, rows, cols = out_ref.shape
+    )(count, sums, tile, probe, tables, far, enter, row, col)
+
+
+def border_kernel(
+    own_ref, above_ref, left_ref, diag_ref, out_ref, top_ref, side_ref, row_buf, col_buf, diag_buf, sems
+):
+    rows = out_ref.shape[1]
+    half = rows // 2
     top = out_ref.at[:, pl.ds(0, BLOCK)]
     side = out_ref.at[:, pl.ds(BLOCK, rows - BLOCK), pl.ds(0, SIDE)]
-    loads = [
-        pltpu.make_async_copy(top, top_ref, sems.at[0]),
-        pltpu.make_async_copy(side, side_ref, sems.at[1]),
-    ]
-    for copy in loads:
-        copy.start()
-    for copy in loads:
-        copy.wait()
-    top_ref[...] = top_ref[...] + above_ref[...]
-    top_ref[:, :, :SIDE] = top_ref[:, :, :SIDE] + left_ref[:, :BLOCK] + diag_ref[...]
-    side_ref[...] = side_ref[...] + left_ref[:, BLOCK:]
-    stores = [
-        pltpu.make_async_copy(top_ref, top, sems.at[0]),
-        pltpu.make_async_copy(side_ref, side, sems.at[1]),
-    ]
-    for copy in stores:
-        copy.start()
-    for copy in stores:
-        copy.wait()
+    loads = start_copies(
+        [
+            (above_ref, row_buf),
+            (top, top_ref),
+            (left_ref, col_buf),
+            (diag_ref, diag_buf),
+            (side, side_ref),
+        ],
+        sems,
+    )
+    wait_copies(loads)
+    left = col_buf[...]
+    low = low_lanes(left.shape)
+    upper = jnp.where(low, left, 0.0)
+    lower = pltpu.roll(jnp.where(low, 0.0, left), BLOCK, 2)
+    top_ref[...] = top_ref[...] + row_buf[...]
+    top_ref[:, :, :SIDE] = top_ref[:, :, :SIDE] + upper[:, :BLOCK] + diag_buf[...]
+    stores = start_copies([(top_ref, top)], sems)
+    side_ref[:, : half - BLOCK] = side_ref[:, : half - BLOCK] + upper[:, BLOCK:]
+    side_ref[:, half - BLOCK :] = side_ref[:, half - BLOCK :] + lower
+    stores += start_copies([(side_ref, side)], sems.at[pl.ds(1, 1)])
+    wait_copies(stores)
 
 
 def add_borders(own, above, left, diag):
     comps, rows, cols = own.shape
-    vmem = pl.BlockSpec(memory_space=pltpu.VMEM)
     return pl.pallas_call(
         border_kernel,
         out_shape=jax.ShapeDtypeStruct(own.shape, jnp.float32),
-        in_specs=[pl.BlockSpec(memory_space=pl.ANY), vmem, vmem, vmem],
+        in_specs=anywhere(4),
         out_specs=pl.BlockSpec(memory_space=pl.ANY),
         scratch_shapes=[
             pltpu.VMEM((comps, BLOCK, cols), jnp.float32),
             pltpu.VMEM((comps, rows - BLOCK, SIDE), jnp.float32),
-            pltpu.SemaphoreType.DMA((2,)),
+            pltpu.VMEM(above.shape, jnp.float32),
+            pltpu.VMEM(left.shape, jnp.float32),
+            pltpu.VMEM(diag.shape, jnp.float32),
+            pltpu.SemaphoreType.DMA((5,)),
         ],
         input_output_aliases={0: 0},
         compiler_params=pltpu.CompilerParams(vmem_limit_bytes=VMEM_LIMIT),
         name="add_borders",
     )(own, above, left, diag)
+
+
+def strip_kernel(tile_ref, below_ref, right_ref, diag_ref, sems):
+    top = pl.ds(0, BLOCK)
+    left = pl.ds(0, SIDE)
+    wait_copies(
+        start_copies(
+            [
+                (tile_ref.at[:, top], below_ref),
+                (tile_ref.at[:, :, left], right_ref),
+                (tile_ref.at[:, top, left], diag_ref),
+            ],
+            sems,
+        )
+    )
+
+
+def strips(tile):
+    comps, rows, cols = tile.shape
+    return pl.pallas_call(
+        strip_kernel,
+        out_shape=shapes_of((comps, BLOCK, cols), (comps, rows, SIDE), (comps, BLOCK, SIDE)),
+        in_specs=anywhere(1),
+        out_specs=tuple(in_vmem(3)),
+        scratch_shapes=[pltpu.SemaphoreType.DMA((3,))],
+        name="halo_strips",
+    )(tile)
 
 
 def moved(shard, down, across):
@@ -609,23 +760,28 @@
     tile = object_slices.reshape(slices * parts, tile_rows, tile_cols)
     row_total = lax.axis_size("row")
     tables = jnp.asarray(TABLES)
+    strip_below, strip_right, strip_diag = strips(tile)
+    below = moved(strip_below, -1, 0)
+    right = moved(strip_right, 0, -1)
+    diag = moved(strip_diag, -1, -1)
     send = pack(offsets, measured, row_total)
     recv = lax.all_to_all(send, "row", split_axis=0, concat_axis=0, tiled=True)
-    below = moved(tile[:, :BLOCK, :], -1, 0)
-    right = moved(tile[:, :, :SIDE], 0, -1)
-    diag = moved(tile[:, :BLOCK, :SIDE], -1, -1)
-    rim, inner = pair_places(tile_rows, tile_cols)
+    last, side, inner = pair_places(tile_rows, tile_cols)
     far_inner, enter_inner = forward_inner(inner, tile, probe, tables)
-    far_rim, enter_rim = forward_rim(rim, tile, below, right, diag, probe, tables)
-    corner = recv[:, CAP * SIDE : CAP * SIDE + CAP, 0].astype(jnp.int32)
-    row, col, to_right, to_below, to_diag = backward_rim(
-        rim, corner, recv, tile, below, right, diag, probe, tables, far_rim, enter_rim
+    far_last, enter_last, far_side, enter_side = forward_rim(
+        last, side, tile, below, right, diag, probe, tables
+    )
+    row, right_part, to_below, to_diag, corner = backward_last(
+        last, recv, tile, below, right, diag, probe, tables, far_last, enter_last
     )
     above = moved(to_below, 1, 0)
+    col, to_right, sums, count = backward_side(
+        side, corner, recv, tile, right, probe, tables, far_side, enter_side, right_part
+    )
     left = moved(to_right, 0, 1)
     corner_part = moved(to_diag, 1, 1)
     own = backward_inner(
-        inner, corner, recv, tile, probe, tables, far_inner, enter_inner, row, col
+        inner, count, sums, tile, probe, tables, far_inner, enter_inner, row, col
     )
     result = add_borders(own, above, left, corner_part)
     return result.reshape(object_slices.shape)

time: 86.3 us -> 84.5 us (0.979)
  the two profiles are of different devices: /device:TPU:7 before, /device:TPU:26 now
where the time goes in v3:
time: 84.5 us; the launch traced here: 84 us
  Pallas kernels  30.3 us (36%)
  starting transfers between devices  22.7 us (27%)
  waiting for transfers between devices  18.3 us (22%)
  local copies, waits for them, and re-layouts  12.3 us (15%)
    all_to_all x1, waiting for transfers between devices, body(): recv = lax.all_to_all(send, 'row', split_axis=0, concat_axis=0, tiled=True)  13.6 us
    unnamed x32, local copies, waits for them, and re-layouts  12.3 us
    ppermute x2, starting transfers between devices, moved(): return lax.ppermute(shard, ('row', 'col'), pairs)  7.46 us
    pallas_call x1, Pallas kernels, backward_inner(): pl.pallas_call(functools.partial(backward_inner_kernel, places), out_shap...  6.58 us
    all_to_all x1, starting transfers between devices, body(): recv = lax.all_to_all(send, 'row', split_axis=0, concat_axis=0, tiled=True)  6.09 us
    pallas_call x1, Pallas kernels, forward_rim(): pl.pallas_call(functools.partial(forward_rim_kernel, places), out_shape=f...  4.8 us
    ppermute x2, starting transfers between devices, moved(): return lax.ppermute(shard, 'row', pairs)  4.73 us
    ppermute x2, waiting for transfers between devices, moved(): return lax.ppermute(shard, 'row', pairs)  4.61 us
  transfers between devices with their start and end apart: 7, of which 2 were waited for; matrix products, arithmetic and copies ran while one was open for 0% of the time, Pallas kernels for 26%

profile of v3, /device:TPU:26, one launch (start us, length us, event | category | flops | bytes accessed | tf_op | source)
XLA Modules:
  0.0 84.0 jit_solution(3945138192422875560)
XLA Ops:
  0.0 2.2 %halo_strips.1 = (f32[4,64,512]{2,1,0:T(8,128)}, f32[4,256,128]{2,1,0:T(8,128)}, f32[4,64,128]{2,1,0:T(8,128)}) custom-call(f32[4,256,512]{2,1,0:T(8,128)} %bitcast.2), custom_call_target="tpu_custom_call" | custom-call | tf_op jit(solution)/shard_map/halo_strips/pallas_call | solution.py:730
  2.3 5.5 %collective-permute-start.2 = (f32[4,64,128]{2,1,0:T(8,128)}, f32[4,64,128]{2,1,0:T(8,128)S(1)}, u32[]{:S(2)}, u32[]{:S(2)}) collective-permute-start(f32[4,64,128]{2,1,0:T(8,128)} %get-tuple-element.25), channel_id=1, source_target_pairs={{9,0},{10,1},{11,2},{12,3},{13,4},{14,5},{15,6},{17,8},{18,9},{19,... | collective-permute-start | bytes 393224 | tf_op jit(solution)/shard_map/ppermute | solution.py:755
  7.8 2.3 %collective-permute-start = (f32[4,64,512]{2,1,0:T(8,128)}, f32[4,64,512]{2,1,0:T(8,128)}, u32[]{:S(2)}, u32[]{:S(2)}) collective-permute-start(f32[4,64,512]{2,1,0:T(8,128)} %get-tuple-element.23), channel_id=1, source_target_pairs={{8,0},{16,8},{24,16},{32,24},{40,32},{48,40},{56,48},{64,56},{72,6... | collective-permute-start | bytes 1572872 | tf_op jit(solution)/shard_map/ppermute | solution.py:745
  10.1 2.5 %collective-permute-start.1 = (f32[4,256,128]{2,1,0:T(8,128)}, f32[4,256,128]{2,1,0:T(8,128)}, u32[]{:S(2)}, u32[]{:S(2)}) collective-permute-start(f32[4,256,128]{2,1,0:T(8,128)} %get-tuple-element.24), channel_id=1, source_target_pairs={{1,0},{2,1},{3,2},{4,3},{5,4},{6,5},{7,6},{9,8},{10,9},{11,10},{12... | collective-permute-start | bytes 1572872 | tf_op jit(solution)/shard_map/ppermute | solution.py:748
  12.6 2.4 %pack_measured.1 = f32[16,264,128]{2,1,0:T(8,128)} custom-call(s32[2,16]{1,0:T(2,128)} %off_ref.1, f32[16,128,128]{2,1,0:T(8,128)} %meas_ref.1), custom_call_target="tpu_custom_call" | custom-call | bytes 41943040 | tf_op jit(solution)/shard_map/pack_measured/pallas_call | solution.py:144
  15.0 0.0 copy-start.2
  15.0 0.0 copy-start.7
  15.1 6.1 %all-to-all-start = ((f32[16,264,128]{2,1,0:T(8,128)}), f32[16,264,128]{2,1,0:T(8,128)S(1)}, u32[]{:S(2)}, u32[]{:S(2)}) async-start(f32[16,264,128]{2,1,0:T(8,128)} %pack_measured.1), calls=%async_computation | async-start | bytes 4325376 | tf_op jit(solution)/shard_map/all_to_all | solution.py:768
  21.2 0.0 copy-start
  21.2 1.6 %copy-done = f32[2,2,256,512]{3,2,1,0:T(8,128)S(1)} copy-done((f32[2,2,256,512]{3,2,1,0:T(8,128)S(1)}, f32[2,2,256,512]{3,2,1,0:T(8,128)}, u32[]{:S(2)}) %copy-start) | copy-done | bytes 2097176
  22.8 4.2 %forward_inner.1 = (f32[9,256,256]{2,1,0:T(8,128)S(1)}, f32[9,256,256]{2,1,0:T(8,128)S(1)}) custom-call(f32[4,256,512]{2,1,0:T(8,128)S(1)} %bitcast.3, f32[2,128,128]{2,1,0:T(8,128)S(1)} %copy-done.7, bf16[8,256,256]{2,1,0:T(8,128)(2,1)S(1)} %copy-done.2), custom_call_target="tpu_custom_call" | custom-call | flops 28991029248 | bytes 1048576 | tf_op jit(solution)/shard_map/forward_inner/pallas_call | solution.py:281
  27.0 1.4 %copy-done.8 = f32[9,256,256]{2,1,0:T(8,128)} copy-done((f32[9,256,256]{2,1,0:T(8,128)}, f32[9,256,256]{2,1,0:T(8,128)S(1)}, u32[]{:S(2)}) %copy-start.8) | copy-done | bytes 2359320
  28.4 1.4 %copy-done.10 = f32[9,256,256]{2,1,0:T(8,128)} copy-done((f32[9,256,256]{2,1,0:T(8,128)}, f32[9,256,256]{2,1,0:T(8,128)S(1)}, u32[]{:S(2)}) %copy-start.10) | copy-done | bytes 2359320
  29.9 0.0 collective-permute-done.2.diag_ref
  29.9 4.8 %forward_rim.1 = (f32[4,256,256]{2,1,0:T(8,128)S(1)}, f32[4,256,256]{2,1,0:T(8,128)S(1)}, f32[3,256,256]{2,1,0:T(8,128)S(1)}, f32[3,256,256]{2,1,0:T(8,128)S(1)}) custom-call(f32[4,256,512]{2,1,0:T(8,128)S(1)} %bitcast.4, f32[4,64,512]{2,1,0:T(8,128)} %collective-permute-done.below_ref, f32[4,256,128]{2,1,0:T(8,128)} %collective-permute-done.1.right_ref, ...), custom_call_target="tpu_custom_call" | custom-call | flops 22548578304 | bytes 1048576 | tf_op jit(solution)/shard_map/forward_rim/pallas_call | solution.py:298
  34.7 0.0 copy-start.3
  34.7 1.0 %copy-done.3 = f32[4,256,256]{2,1,0:T(8,128)} copy-done((f32[4,256,256]{2,1,0:T(8,128)}, f32[4,256,256]{2,1,0:T(8,128)S(1)}, u32[]{:S(2)}) %copy-start.3) | copy-done | bytes 1048600
  35.6 1.0 %copy-done.5 = f32[4,256,256]{2,1,0:T(8,128)} copy-done((f32[4,256,256]{2,1,0:T(8,128)}, f32[4,256,256]{2,1,0:T(8,128)S(1)}, u32[]{:S(2)}) %copy-start.5) | copy-done | bytes 1048600
  36.6 0.9 %copy-done.12 = f32[3,256,256]{2,1,0:T(8,128)} copy-done((f32[3,256,256]{2,1,0:T(8,128)}, f32[3,256,256]{2,1,0:T(8,128)S(1)}, u32[]{:S(2)}) %copy-start.12) | copy-done | bytes 786456
  37.6 0.9 %copy-done.14 = f32[3,256,256]{2,1,0:T(8,128)} copy-done((f32[3,256,256]{2,1,0:T(8,128)}, f32[3,256,256]{2,1,0:T(8,128)S(1)}, u32[]{:S(2)}) %copy-start.14) | copy-done | bytes 786456
  38.5 13.6 %all-to-all-done.recv_ref = f32[16,264,128]{2,1,0:T(8,128)S(1)} async-done(((f32[16,264,128]{2,1,0:T(8,128)}), f32[16,264,128]{2,1,0:T(8,128)S(1)}, u32[]{:S(2)}, u32[]{:S(2)}) %all-to-all-start) | async-done | bytes 2162720 | tf_op jit(solution)/shard_map/all_to_all | solution.py:768
  52.1 1.6 %copy-done.1 = f32[2,2,256,512]{3,2,1,0:T(8,128)S(1)} copy-done((f32[2,2,256,512]{3,2,1,0:T(8,128)S(1)}, f32[2,2,256,512]{3,2,1,0:T(8,128)}, u32[]{:S(2)}) %copy-start.1) | copy-done | bytes 2097176
  53.7 1.2 %copy-done.4 = f32[4,256,256]{2,1,0:T(8,128)S(1)} copy-done((f32[4,256,256]{2,1,0:T(8,128)S(1)}, f32[4,256,256]{2,1,0:T(8,128)}, u32[]{:S(2)}) %copy-start.4) | copy-done | bytes 1048600
  54.9 1.2 %copy-done.6 = f32[4,256,256]{2,1,0:T(8,128)S(1)} copy-done((f32[4,256,256]{2,1,0:T(8,128)S(1)}, f32[4,256,256]{2,1,0:T(8,128)}, u32[]{:S(2)}) %copy-start.6) | copy-done | bytes 1048600
  56.1 3.7 %backward_last_row.1 = (f32[4,64,512]{2,1,0:T(8,128)S(1)}, f32[4,64,128]{2,1,0:T(8,128)S(1)}, f32[4,64,512]{2,1,0:T(8,128)S(1)}, f32[4,64,128]{2,1,0:T(8,128)S(1)}, s32[16,2]{1,0:T(8,128)S(1)}) custom-call(f32[16,264,128]{2,1,0:T(8,128)S(1)} %all-to-all-done.recv_ref, f32[4,256,512]{2,1,0:T(8,128)S(1)} %bitcast.5, ...), custom_call_target="tpu_custom_call" | custom-call | flops 1610612736 | bytes 1048576 | tf_op jit(solution)/shard_map/backward_last_row/pallas_call | solution.py:592
  59.8 1.9 %collective-permute-start.5 = (f32[4,64,128]{2,1,0:T(8,128)S(1)}, f32[4,64,128]{2,1,0:T(8,128)S(1)}, u32[]{:S(2)}, u32[]{:S(2)}) collective-permute-start(f32[4,64,128]{2,1,0:T(8,128)S(1)} %get-tuple-element.40), channel_id=1, source_target_pairs={{0,9},{1,10},{2,11},{3,12},{4,13},{5,14},{6,15},{8,17},{9,18},{10,... | collective-permute-start | bytes 393224 | tf_op jit(solution)/shard_map/ppermute | solution.py:755
  61.8 2.4 %collective-permute-start.3 = (f32[4,64,512]{2,1,0:T(8,128)S(1)}, f32[4,64,512]{2,1,0:T(8,128)S(1)}, u32[]{:S(2)}, u32[]{:S(2)}) collective-permute-start(f32[4,64,512]{2,1,0:T(8,128)S(1)} %get-tuple-element.38), channel_id=1, source_target_pairs={{0,8},{8,16},{16,24},{24,32},{32,40},{40,48},{48,56},{56,64},{64,7... | collective-permute-start | bytes 1572872 | tf_op jit(solution)/shard_map/ppermute | solution.py:745
  64.2 4.1 %backward_last_column.1 = (f32[4,256,128]{2,1,0:T(8,128)S(1)}, f32[4,128,128]{2,1,0:T(8,128)S(1)}, f32[24,128,128]{2,1,0:T(8,128)S(1)}, s32[24]{0:T(128)S(1)}) custom-call(s32[16,2]{1,0:T(8,128)S(1)} %get-tuple-element.28.corner_ref, f32[16,264,128]{2,1,0:T(8,128)S(1)} %all-to-all-done.recv_ref, f32[4,256,512]{2,1,0:T(8,128)S(1)} %bitcast.6, ...), custom_call_target="tpu_custom_call" | custom-call | flops 9663676416 | bytes 1048576 | tf_op jit(solution)/shard_map/backward_last_column/pallas_call | solution.py:621
  68.3 1.9 %collective-permute-start.4 = (f32[4,128,128]{2,1,0:T(8,128)S(1)}, f32[4,128,128]{2,1,0:T(8,128)S(1)}, u32[]{:S(2)}, u32[]{:S(2)}) collective-permute-start(f32[4,128,128]{2,1,0:T(8,128)S(1)} %get-tuple-element.39), channel_id=1, source_target_pairs={{0,1},{1,2},{2,3},{3,4},{4,5},{5,6},{6,7},{8,9},{9,10},{10,11},{11... | collective-permute-start | bytes 786440 | tf_op jit(solution)/shard_map/ppermute | solution.py:748
  70.2 6.6 %backward_inner.1.own_ref = f32[4,256,512]{2,1,0:T(8,128)} custom-call(s32[24]{0:T(128)S(1)} %get-tuple-element.32.count_ref, f32[24,128,128]{2,1,0:T(8,128)S(1)} %get-tuple-element.33.sum_ref, f32[4,256,512]{2,1,0:T(8,128)S(1)} %bitcast.7, f32[2,128,128]{2,1,0:T(8,128)S(1)} %copy-done.7, bf16[8,256,256]{2,1,0:T(8,128)(2,1)S(1)} %copy-done.2, ...), custom_call_target="tpu_custom_call" | custom-call | flops 3623878656 | bytes 1048576 | tf_op jit(solution)/shard_map/backward_inner/pallas_call | solution.py:646
  76.8 4.6 %collective-permute-done.3.above_ref = f32[4,64,512]{2,1,0:T(8,128)S(1)} collective-permute-done((f32[4,64,512]{2,1,0:T(8,128)S(1)}, f32[4,64,512]{2,1,0:T(8,128)S(1)}, u32[]{:S(2)}, u32[]{:S(2)}) %collective-permute-start.3) | collective-permute-done | bytes 524320 | tf_op jit(solution)/shard_map/ppermute | solution.py:745
  81.4 2.3 %add_borders.1 = f32[4,256,512]{2,1,0:T(8,128)} custom-call(f32[4,256,512]{2,1,0:T(8,128)} %backward_inner.1.own_ref, f32[4,64,512]{2,1,0:T(8,128)S(1)} %collective-permute-done.3.above_ref, f32[4,128,128]{2,1,0:T(8,128)S(1)} %collective-permute-done.4.left_ref, f32[4,64,128]{2,1,0:T(8,128)S(1)} %collective-permute-done.5.diag_ref), custom_call_target="tpu_custom_call", output_to_operand_aliasing={{}: (0, {})} | custom-call | tf_op jit(solution)/shard_map/add_borders/pallas_call | solution.py:694
  (22 shorter events, 0.0 us)
Async XLA Ops:
  2.3 27.6 %collective-permute-start.2 = (f32[4,64,128]{2,1,0:T(8,128)}, f32[4,64,128]{2,1,0:T(8,128)S(1)}, u32[]{:S(2)}, u32[]{:S(2)}) collective-permute-start(f32[4,64,128]{2,1,0:T(8,128)} %get-tuple-element.25), channel_id=1, source_target_pairs={{9,0},{10,1},{11,2},{12,3},{13,4},{14,5},{15,6},{17,8},{18,9},{19,... | collective-permute-start | bytes 393224 | tf_op jit(solution)/shard_map/ppermute | solution.py:755
  7.8 22.1 %collective-permute-start = (f32[4,64,512]{2,1,0:T(8,128)}, f32[4,64,512]{2,1,0:T(8,128)}, u32[]{:S(2)}, u32[]{:S(2)}) collective-permute-start(f32[4,64,512]{2,1,0:T(8,128)} %get-tuple-element.23), channel_id=1, source_target_pairs={{8,0},{16,8},{24,16},{32,24},{40,32},{48,40},{56,48},{64,56},{72,6... | collective-permute-start | bytes 1572872 | tf_op jit(solution)/shard_map/ppermute | solution.py:745
  10.1 19.7 %collective-permute-start.1 = (f32[4,256,128]{2,1,0:T(8,128)}, f32[4,256,128]{2,1,0:T(8,128)}, u32[]{:S(2)}, u32[]{:S(2)}) collective-permute-start(f32[4,256,128]{2,1,0:T(8,128)} %get-tuple-element.24), channel_id=1, source_target_pairs={{1,0},{2,1},{3,2},{4,3},{5,4},{6,5},{7,6},{9,8},{10,9},{11,10},{12... | collective-permute-start | bytes 1572872 | tf_op jit(solution)/shard_map/ppermute | solution.py:748
  15.0 6.1 %copy-start.2 = (bf16[8,256,256]{2,1,0:T(8,128)(2,1)S(1)}, bf16[8,256,256]{2,1,0:T(8,128)(2,1)}, u32[]{:S(2)}) copy-start(bf16[8,256,256]{2,1,0:T(8,128)(2,1)} %constant.2.clone.tables.tables_ref) | copy-start | bytes 3145732
  15.0 6.1 %copy-start.7 = (f32[2,128,128]{2,1,0:T(8,128)S(1)}, f32[2,128,128]{2,1,0:T(8,128)}, u32[]{:S(2)}) copy-start(f32[2,128,128]{2,1,0:T(8,128)} %probe_ref.9) | copy-start | bytes 393220
  15.1 37.0 %all-to-all-start = ((f32[16,264,128]{2,1,0:T(8,128)}), f32[16,264,128]{2,1,0:T(8,128)S(1)}, u32[]{:S(2)}, u32[]{:S(2)}) async-start(f32[16,264,128]{2,1,0:T(8,128)} %pack_measured.1), calls=%async_computation | async-start | bytes 4325376 | tf_op jit(solution)/shard_map/all_to_all | solution.py:768
  21.2 1.6 %copy-start = (f32[2,2,256,512]{3,2,1,0:T(8,128)S(1)}, f32[2,2,256,512]{3,2,1,0:T(8,128)}, u32[]{:S(2)}) copy-start(f32[2,2,256,512]{3,2,1,0:T(8,128)} %param.5) | copy-start | bytes 6291460
  27.0 1.4 %copy-start.8 = (f32[9,256,256]{2,1,0:T(8,128)}, f32[9,256,256]{2,1,0:T(8,128)S(1)}, u32[]{:S(2)}) copy-start(f32[9,256,256]{2,1,0:T(8,128)S(1)} %get-tuple-element.34.far_ref) | copy-start | bytes 7077892
  28.4 1.4 %copy-start.10 = (f32[9,256,256]{2,1,0:T(8,128)}, f32[9,256,256]{2,1,0:T(8,128)S(1)}, u32[]{:S(2)}) copy-start(f32[9,256,256]{2,1,0:T(8,128)S(1)} %get-tuple-element.35.enter_ref) | copy-start | bytes 7077892
  34.7 1.0 %copy-start.3 = (f32[4,256,256]{2,1,0:T(8,128)}, f32[4,256,256]{2,1,0:T(8,128)S(1)}, u32[]{:S(2)}) copy-start(f32[4,256,256]{2,1,0:T(8,128)S(1)} %get-tuple-element.26.far_ref) | copy-start | bytes 3145732
  35.6 1.0 %copy-start.5 = (f32[4,256,256]{2,1,0:T(8,128)}, f32[4,256,256]{2,1,0:T(8,128)S(1)}, u32[]{:S(2)}) copy-start(f32[4,256,256]{2,1,0:T(8,128)S(1)} %get-tuple-element.27.enter_ref) | copy-start | bytes 3145732
  36.6 0.9 %copy-start.12 = (f32[3,256,256]{2,1,0:T(8,128)}, f32[3,256,256]{2,1,0:T(8,128)S(1)}, u32[]{:S(2)}) copy-start(f32[3,256,256]{2,1,0:T(8,128)S(1)} %get-tuple-element.29.far_ref) | copy-start | bytes 2359300
  37.6 0.9 %copy-start.14 = (f32[3,256,256]{2,1,0:T(8,128)}, f32[3,256,256]{2,1,0:T(8,128)S(1)}, u32[]{:S(2)}) copy-start(f32[3,256,256]{2,1,0:T(8,128)S(1)} %get-tuple-element.30.enter_ref) | copy-start | bytes 2359300
  52.1 1.6 %copy-start.1 = (f32[2,2,256,512]{3,2,1,0:T(8,128)S(1)}, f32[2,2,256,512]{3,2,1,0:T(8,128)}, u32[]{:S(2)}) copy-start(f32[2,2,256,512]{3,2,1,0:T(8,128)} %param.5) | copy-start | bytes 6291460
  53.7 1.2 %copy-start.4 = (f32[4,256,256]{2,1,0:T(8,128)S(1)}, f32[4,256,256]{2,1,0:T(8,128)}, u32[]{:S(2)}) copy-start(f32[4,256,256]{2,1,0:T(8,128)} %copy-done.3) | copy-start | bytes 3145732
  54.9 1.2 %copy-start.6 = (f32[4,256,256]{2,1,0:T(8,128)S(1)}, f32[4,256,256]{2,1,0:T(8,128)}, u32[]{:S(2)}) copy-start(f32[4,256,256]{2,1,0:T(8,128)} %copy-done.5) | copy-start | bytes 3145732
  56.1 8.0 %copy-start.13 = (f32[3,256,256]{2,1,0:T(8,128)S(1)}, f32[3,256,256]{2,1,0:T(8,128)}, u32[]{:S(2)}) copy-start(f32[3,256,256]{2,1,0:T(8,128)} %copy-done.12) | copy-start | bytes 2359300
  56.1 8.0 %copy-start.15 = (f32[3,256,256]{2,1,0:T(8,128)S(1)}, f32[3,256,256]{2,1,0:T(8,128)}, u32[]{:S(2)}) copy-start(f32[3,256,256]{2,1,0:T(8,128)} %copy-done.14) | copy-start | bytes 2359300
  59.8 17.0 %collective-permute-start.5 = (f32[4,64,128]{2,1,0:T(8,128)S(1)}, f32[4,64,128]{2,1,0:T(8,128)S(1)}, u32[]{:S(2)}, u32[]{:S(2)}) collective-permute-start(f32[4,64,128]{2,1,0:T(8,128)S(1)} %get-tuple-element.40), channel_id=1, source_target_pairs={{0,9},{1,10},{2,11},{3,12},{4,13},{5,14},{6,15},{8,17},{9,18},{10,... | collective-permute-start | bytes 393224 | tf_op jit(solution)/shard_map/ppermute | solution.py:755
  61.8 19.7 %collective-permute-start.3 = (f32[4,64,512]{2,1,0:T(8,128)S(1)}, f32[4,64,512]{2,1,0:T(8,128)S(1)}, u32[]{:S(2)}, u32[]{:S(2)}) collective-permute-start(f32[4,64,512]{2,1,0:T(8,128)S(1)} %get-tuple-element.38), channel_id=1, source_target_pairs={{0,8},{8,16},{16,24},{24,32},{32,40},{40,48},{48,56},{56,64},{64,7... | collective-permute-start | bytes 1572872 | tf_op jit(solution)/shard_map/ppermute | solution.py:745
  64.2 6.0 %copy-start.9 = (f32[9,256,256]{2,1,0:T(8,128)S(1)}, f32[9,256,256]{2,1,0:T(8,128)}, u32[]{:S(2)}) copy-start(f32[9,256,256]{2,1,0:T(8,128)} %copy-done.8) | copy-start | bytes 7077892
  64.2 6.0 %copy-start.11 = (f32[9,256,256]{2,1,0:T(8,128)S(1)}, f32[9,256,256]{2,1,0:T(8,128)}, u32[]{:S(2)}) copy-start(f32[9,256,256]{2,1,0:T(8,128)} %copy-done.10) | copy-start | bytes 7077892
  68.3 8.5 %collective-permute-start.4 = (f32[4,128,128]{2,1,0:T(8,128)S(1)}, f32[4,128,128]{2,1,0:T(8,128)S(1)}, u32[]{:S(2)}, u32[]{:S(2)}) collective-permute-start(f32[4,128,128]{2,1,0:T(8,128)S(1)} %get-tuple-element.39), channel_id=1, source_target_pairs={{0,1},{1,2},{2,3},{3,4},{4,5},{5,6},{6,7},{8,9},{9,10},{10,11},{11... | collective-permute-start | bytes 786440 | tf_op jit(solution)/shard_map/ppermute | solution.py:748

commit v4 on v3

--- a/solution.py
+++ b/solution.py
@@ -16,6 +16,7 @@
 CAP = 2
 META = 8
 VMEM_LIMIT = 28 * 1024 * 1024
+VMEM_MOST = 60 * 1024 * 1024
 
 
 def dft_matrix():
@@ -103,9 +104,19 @@
     return (left_re * right_re + left_im * right_im, left_re * right_im - left_im * right_re)
 
 
-def pack_kernel(off_ref, meas_ref, send_ref, meta_ref, count_ref, corner_ref, sems):
+def pack_kernel(
+    off_ref, meas_ref, tile_ref, send_ref, right_ref, diag_ref, meta_ref, count_ref, corner_ref, sems
+):
     owners = send_ref.shape[0]
     positions = meas_ref.shape[0]
+    left = pl.ds(0, SIDE)
+    strips = start_copies(
+        [
+            (tile_ref.at[:, :, left], right_ref),
+            (tile_ref.at[:, pl.ds(0, BLOCK), left], diag_ref),
+        ],
+        sems.at[pl.ds(positions + 1, 2)],
+    )
     for owner in range(owners):
         count_ref[owner] = 0
         for rank in range(CAP):
@@ -135,31 +146,30 @@
     )
     copy.start()
     copies.append(copy)
-    for copy in copies:
-        copy.wait()
-
-
-def pack(offsets, measured, owners):
+    wait_copies(copies + strips)
+
+
+def pack(offsets, measured, tile, owners):
     positions = measured.shape[0]
+    comps, rows, _ = tile.shape
     return pl.pallas_call(
         pack_kernel,
-        out_shape=jax.ShapeDtypeStruct((owners, CAP * SIDE + META, SIDE), jnp.float32),
-        in_specs=[
-            pl.BlockSpec(memory_space=pltpu.SMEM),
-            pl.BlockSpec(memory_space=pltpu.VMEM),
-        ],
-        out_specs=pl.BlockSpec(memory_space=pl.ANY),
+        out_shape=shapes_of(
+            (owners, CAP * SIDE + META, SIDE), (comps, rows, SIDE), (comps, BLOCK, SIDE)
+        ),
+        in_specs=[pl.BlockSpec(memory_space=pltpu.SMEM)] + in_vmem(1) + anywhere(1),
+        out_specs=tuple(anywhere(1) + in_vmem(2)),
         scratch_shapes=[
             pltpu.VMEM((owners, META, SIDE), jnp.float32),
             pltpu.SMEM((owners,), jnp.int32),
             pltpu.SMEM((owners * CAP,), jnp.int32),
-            pltpu.SemaphoreType.DMA((positions + 1,)),
+            pltpu.SemaphoreType.DMA((positions + 3,)),
         ],
         cost_estimate=pl.CostEstimate(
             flops=0, bytes_accessed=40 * 1024 * 1024, transcendentals=0
         ),
         name="pack_measured",
-    )(offsets, measured)
+    )(offsets, measured, tile)
 
 
 def pair_places(rows, cols):
@@ -307,37 +317,54 @@
     )(tile, below, right, diag, probe, tables)
 
 
-def gather_sums(corner_ref, recv_ref, sum_ref, count_ref, first):
-    corners = sum_ref.shape[0]
-    sum_ref[...] = jnp.zeros_like(sum_ref)
-    for corner in range(corners):
+def gather_sums(meta_ref, items_ref, sum_ref, count_ref):
+    spare = sum_ref.shape[0] - 1
+    for corner in range(spare + 1):
         count_ref[corner] = 0
-    for source in range(recv_ref.shape[0]):
+    for source in range(items_ref.shape[0]):
         for rank in range(CAP):
-            at = corner_ref[source, rank] - first
-
-            @pl.when(jnp.logical_and(at >= 0, at < corners))
-            def _():
-                count_ref[at] = count_ref[at] + 1
-                sum_ref[at] = sum_ref[at] + recv_ref[source, rank * SIDE : (rank + 1) * SIDE]
+            corner = meta_ref[source, rank * BLOCK].astype(jnp.int32)
+            at = jnp.where(corner < 0, spare, corner)
+            hits = count_ref[at]
+            count_ref[at] = hits + 1
+            item = items_ref[source, rank * SIDE : (rank + 1) * SIDE]
+            sum_ref[at] = jnp.where(hits > 0, sum_ref[at], 0.0) + item
+
+
+def summed(sum_ref, count_ref, at):
+    hits = count_ref[at]
+    return hits.astype(jnp.float32), jnp.where(hits > 0, sum_ref[at], 0.0)
 
 
 def backward_pairs(
-    places, corner_of, probe_ref, tables, far_ref, enter_ref, ext_ref, sum_ref, count_ref, store
+    places,
+    width,
+    probe_ref,
+    tables,
+    far_ref,
+    enter_ref,
+    ext_ref,
+    sum_ref,
+    count_ref,
+    store,
+    before_fields=None,
+    before_products=None,
 ):
-    probe_re = probe_ref[0]
-    probe_im = probe_ref[1]
     rows = []
     for pair, (row, col) in enumerate(places):
         waves = []
         for n in range(2):
-            at = corner_of(row, col) + n
-            hits = count_ref[at].astype(jnp.float32)
+            at = row * width + col // BLOCK + n
+            hits, total = summed(sum_ref, count_ref, at)
             far_re, far_im = halves(far_ref[pair], n)
-            misfit = 2.0 * (hits * (far_re * far_re + far_im * far_im) - sum_ref[at])
+            misfit = 2.0 * (hits * (far_re * far_re + far_im * far_im) - total)
             waves.append((misfit * far_re, misfit * far_im))
         rows.append(stacked(waves))
+    if before_products is not None:
+        before_products()
     backs = two_sided(rows, tables, 6, 4)
+    if before_fields is not None:
+        before_fields()
     rows = []
     for pair, (row, col) in enumerate(places):
         trans = [cut_pair(ext_ref, comp, row * BLOCK, col) for comp in range(2)]
@@ -350,6 +377,8 @@
             waves.append(conj_times(trans[0][n], trans[1][n], *back))
         rows.append(stacked(waves))
     backs = two_sided(rows, tables, 2, 0)
+    probe_re = probe_ref[0]
+    probe_im = probe_ref[1]
     for pair, (row, col) in enumerate(places):
         for n in range(2):
             grad = conj_times(probe_re, probe_im, *halves(backs[pair], n))
@@ -365,7 +394,7 @@
     return pltpu.roll(jnp.where(low_lanes(low.shape), high, low), BLOCK, 1)
 
 
-def backward_last_kernel(
+def backward_rim_kernel(
     places,
     recv_ref,
     tile_ref,
@@ -374,65 +403,68 @@
     diag_ref,
     probe_ref,
     tables_ref,
-    far_ref,
-    enter_ref,
+    far_last_ref,
+    enter_last_ref,
+    far_side_ref,
+    enter_side_ref,
     row_ref,
-    right_part_ref,
+    col_ref,
     out_below_ref,
+    out_right_ref,
     out_diag_ref,
-    corner_ref,
+    sum_ref,
+    count_ref,
     items_ref,
+    meta_ref,
     table_buf,
     probe_buf,
     far_buf,
     enter_buf,
     ext_ref,
-    sum_ref,
-    count_ref,
-    meta_ref,
     even_ref,
     odd_ref,
+    even_side_ref,
+    odd_side_ref,
     sems,
 ):
     rows, cols = tile_ref.shape[1:]
-    corners = sum_ref.shape[0]
-    start = rows - BLOCK
-    two = pl.ds(2, 2)
-    above = pl.ds(0, BLOCK)
-    under = pl.ds(BLOCK, BLOCK)
-    wide = pl.ds(0, cols)
-    beyond = pl.ds(cols, SIDE)
-    low = pl.ds(start, BLOCK)
+    last = rows // BLOCK - 1
+    first = pl.ds(0, far_last_ref.shape[0])
+    others = pl.ds(far_last_ref.shape[0], far_side_ref.shape[0])
     copies = start_copies(
         [
             (recv_ref.at[:, CAP * SIDE], meta_ref),
             (recv_ref.at[:, pl.ds(0, CAP * SIDE)], items_ref),
-            (far_ref, far_buf),
+            (far_last_ref, far_buf.at[first]),
+            (far_side_ref, far_buf.at[others]),
             (tables_ref, table_buf),
-            (tile_ref.at[two, low], ext_ref.at[:, above, wide]),
-            (below_ref.at[two], ext_ref.at[:, under, wide]),
-            (right_ref.at[two, low], ext_ref.at[:, above, beyond]),
-            (diag_ref.at[two], ext_ref.at[:, under, beyond]),
-            (enter_ref, enter_buf),
+            (enter_last_ref, enter_buf.at[first]),
+            (enter_side_ref, enter_buf.at[others]),
             (probe_ref, probe_buf),
-        ],
+        ]
+        + extended_parts(tile_ref, below_ref, right_ref, diag_ref, ext_ref, 2),
         sems,
     )
-    wait_copies(copies[:1])
-    for source in range(corner_ref.shape[0]):
-        for rank in range(CAP):
-            corner_ref[source, rank] = meta_ref[source, rank * BLOCK].astype(jnp.int32)
-    wait_copies(copies[1:2])
-    gather_sums(corner_ref, items_ref, sum_ref, count_ref, start // BLOCK * corners)
-    wait_copies(copies[2:])
+    wait_copies(copies[:2])
+    gather_sums(meta_ref, items_ref, sum_ref, count_ref)
+    wait_copies(copies[2:4])
     bands = (even_ref, odd_ref)
+    sides = (even_side_ref, odd_side_ref)
 
     def store(n, comp, row, col, value):
-        bands[n][comp, :, col : col + SIDE] = value
+        if row == last:
+            bands[n][comp, :, col : col + SIDE] = value
+        else:
+            at = row * BLOCK
+            top = value[:BLOCK]
+            if row > 0:
+                top = top + sides[n][comp, at : at + BLOCK]
+            sides[n][comp, at : at + BLOCK] = top
+            sides[n][comp, at + BLOCK : at + SIDE] = value[BLOCK:]
 
     backward_pairs(
-        [(0, col) for _, col in places],
-        lambda row, col: col // BLOCK,
+        places,
+        cols // BLOCK,
         probe_buf,
         table_buf,
         far_buf,
@@ -441,11 +473,15 @@
         sum_ref,
         count_ref,
         store,
-    )
+        lambda: wait_copies(copies[5:]),
+        lambda: wait_copies(copies[4:5]),
+    )
+    half = rows // 2
     for comp in range(4):
-        for out_ref, side_ref, part in (
-            (row_ref, right_part_ref, slice(0, BLOCK)),
-            (out_below_ref, out_diag_ref, slice(BLOCK, SIDE)),
+        beyond = []
+        for out_ref, part in (
+            (row_ref, slice(0, BLOCK)),
+            (out_below_ref, slice(BLOCK, SIDE)),
         ):
             before = None
             for col in range(0, cols, SIDE):
@@ -454,74 +490,15 @@
                     comp, part, col : col + SIDE
                 ] + shifted(before, here)
                 before = here
-            side_ref[comp] = shifted(before, None)
-
-
-def backward_side_kernel(
-    places,
-    corner_ref,
-    recv_ref,
-    tile_ref,
-    right_ref,
-    probe_ref,
-    tables,
-    far_ref,
-    enter_ref,
-    right_part_ref,
-    col_ref,
-    out_right_ref,
-    sum_ref,
-    count_ref,
-    ext_ref,
-    even_ref,
-    odd_ref,
-    sems,
-):
-    rows, cols = tile_ref.shape[1:]
-    edge = cols - SIDE
-    last = rows - BLOCK
-    width = cols // BLOCK
-    two = pl.ds(2, 2)
-    copies = start_copies(
-        [
-            (tile_ref.at[two, :, pl.ds(edge, SIDE)], ext_ref.at[:, :, pl.ds(0, SIDE)]),
-            (right_ref.at[two], ext_ref.at[:, :, pl.ds(SIDE, SIDE)]),
-        ],
-        sems,
-    )
-    gather_sums(corner_ref, recv_ref, sum_ref, count_ref, 0)
-    wait_copies(copies)
-    acc = (even_ref, odd_ref)
-
-    def store(n, comp, row, col, value):
-        at = row * BLOCK
-        top = value[:BLOCK]
-        if row > 0:
-            top = top + acc[n][comp, at : at + BLOCK]
-        acc[n][comp, at : at + BLOCK] = top
-        acc[n][comp, at + BLOCK : at + SIDE] = value[BLOCK:]
-
-    backward_pairs(
-        [(row, 0) for row, _ in places],
-        lambda row, col: row * width + edge // BLOCK,
-        probe_ref,
-        tables,
-        far_ref,
-        enter_ref,
-        ext_ref,
-        sum_ref,
-        count_ref,
-        store,
-    )
-    half = rows // 2
-    for comp in range(4):
-        col_ref[comp] = even_ref[comp] + shifted(None, odd_ref[comp])
-        side = shifted(odd_ref[comp], None)
-        first = side[:half]
+            beyond.append(shifted(before, None))
+        out_diag_ref[comp] = beyond[1]
+        odd_side = odd_side_ref[comp]
+        col_ref[comp] = even_side_ref[comp] + shifted(None, odd_side)
+        side = shifted(odd_side, None)
         second = jnp.concatenate(
-            [side[half:last], side[last:] + right_part_ref[comp]], axis=0
+            [side[half : rows - BLOCK], side[rows - BLOCK :] + beyond[0]], axis=0
         )
-        out_right_ref[comp] = first + pltpu.roll(second, BLOCK, 1)
+        out_right_ref[comp] = side[:half] + pltpu.roll(second, BLOCK, 1)
 
 
 def backward_inner_kernel(
@@ -541,7 +518,6 @@
 ):
     rows, cols = out_ref.shape[1:]
     last = rows - BLOCK
-    width = cols // BLOCK
     acc = (even_ref, odd_ref)
 
     def store(n, comp, row, col, value):
@@ -555,7 +531,7 @@
 
     backward_pairs(
         places,
-        lambda row, col: row * width + col // BLOCK,
+        cols // BLOCK,
         probe_ref,
         tables,
         far_ref,
@@ -583,62 +559,42 @@
     return tuple(jax.ShapeDtypeStruct(shape, jnp.float32) for shape in shapes)
 
 
-def backward_last(places, recv, tile, below, right, diag, probe, tables, far, enter):
+def backward_rim(recv, tile, below, right, diag, probe, tables, fields_last, fields_side, places):
     comps, rows, cols = tile.shape
-    corners = cols // BLOCK
+    corners = (rows // BLOCK) * (cols // BLOCK) + 1
     sources = recv.shape[0]
-    edge = (comps, BLOCK, cols)
-    side = (comps, BLOCK, SIDE)
+    field = (len(places), 2 * SIDE, 2 * SIDE)
     return pl.pallas_call(
-        functools.partial(backward_last_kernel, places),
-        out_shape=shapes_of(edge, side, edge, side)
-        + (jax.ShapeDtypeStruct((sources, CAP), jnp.int32),),
-        in_specs=anywhere(9),
-        out_specs=tuple(in_vmem(4)) + (pl.BlockSpec(memory_space=pltpu.SMEM),),
+        functools.partial(backward_rim_kernel, places),
+        out_shape=shapes_of(
+            (comps, BLOCK, cols),
+            (comps, rows, SIDE),
+            (comps, BLOCK, cols),
+            (comps, rows // 2, SIDE),
+            (comps, BLOCK, SIDE),
+            (corners, SIDE, SIDE),
+        )
+        + (jax.ShapeDtypeStruct((corners,), jnp.int32),),
+        in_specs=anywhere(11),
+        out_specs=tuple(in_vmem(6)) + (pl.BlockSpec(memory_space=pltpu.SMEM),),
         scratch_shapes=[
             pltpu.VMEM((sources, CAP * SIDE, SIDE), jnp.float32),
+            pltpu.SMEM((sources, SIDE), jnp.float32),
             pltpu.VMEM(tables.shape, tables.dtype),
             pltpu.VMEM(probe.shape, jnp.float32),
-            pltpu.VMEM(far.shape, jnp.float32),
-            pltpu.VMEM(enter.shape, jnp.float32),
-            pltpu.VMEM((2, SIDE, cols + SIDE), jnp.float32),
-            pltpu.VMEM((corners, SIDE, SIDE), jnp.float32),
-            pltpu.SMEM((corners,), jnp.int32),
-            pltpu.SMEM((sources, SIDE), jnp.float32),
+            pltpu.VMEM(field, jnp.float32),
+            pltpu.VMEM(field, jnp.float32),
+            extended_shape(tile, 2),
             pltpu.VMEM((comps, SIDE, cols), jnp.float32),
             pltpu.VMEM((comps, SIDE, cols), jnp.float32),
-            pltpu.SemaphoreType.DMA((10,)),
-        ],
-        compiler_params=pltpu.CompilerParams(vmem_limit_bytes=VMEM_LIMIT),
-        cost_estimate=stage_cost(len(places)),
-        name="backward_last_row",
-    )(recv, tile, below, right, diag, probe, tables, far, enter)
-
-
-def backward_side(places, corner, recv, tile, right, probe, tables, far, enter, right_part):
-    comps, rows, cols = tile.shape
-    corners = (rows // BLOCK - 1) * (cols // BLOCK)
-    return pl.pallas_call(
-        functools.partial(backward_side_kernel, places),
-        out_shape=shapes_of(
-            (comps, rows, SIDE), (comps, rows // 2, SIDE), (corners, SIDE, SIDE)
-        )
-        + (jax.ShapeDtypeStruct((corners,), jnp.int32),),
-        in_specs=[pl.BlockSpec(memory_space=pltpu.SMEM)]
-        + in_vmem(1)
-        + anywhere(2)
-        + in_vmem(5),
-        out_specs=tuple(in_vmem(3)) + (pl.BlockSpec(memory_space=pltpu.SMEM),),
-        scratch_shapes=[
-            pltpu.VMEM((2, rows, 2 * SIDE), jnp.float32),
             pltpu.VMEM((comps, rows, SIDE), jnp.float32),
             pltpu.VMEM((comps, rows, SIDE), jnp.float32),
-            pltpu.SemaphoreType.DMA((2,)),
+            pltpu.SemaphoreType.DMA((12,)),
         ],
-        compiler_params=pltpu.CompilerParams(vmem_limit_bytes=VMEM_LIMIT),
-        cost_estimate=stage_cost(8 * len(places)),
-        name="backward_last_column",
-    )(corner, recv, tile, right, probe, tables, far, enter, right_part)
+        compiler_params=pltpu.CompilerParams(vmem_limit_bytes=VMEM_MOST),
+        cost_estimate=stage_cost(len(places)),
+        name="backward_rim",
+    )(recv, tile, below, right, diag, probe, tables, *fields_last, *fields_side)
 
 
 def backward_inner(places, count, sums, tile, probe, tables, far, enter, row, col):
@@ -710,30 +666,20 @@
     )(own, above, left, diag)
 
 
-def strip_kernel(tile_ref, below_ref, right_ref, diag_ref, sems):
-    top = pl.ds(0, BLOCK)
-    left = pl.ds(0, SIDE)
-    wait_copies(
-        start_copies(
-            [
-                (tile_ref.at[:, top], below_ref),
-                (tile_ref.at[:, :, left], right_ref),
-                (tile_ref.at[:, top, left], diag_ref),
-            ],
-            sems,
-        )
-    )
-
-
-def strips(tile):
+def strip_kernel(tile_ref, below_ref, sems):
+    wait_copies(start_copies([(tile_ref.at[:, pl.ds(0, BLOCK)], below_ref)], sems))
+
+
+def row_strip(tile):
     comps, rows, cols = tile.shape
     return pl.pallas_call(
         strip_kernel,
-        out_shape=shapes_of((comps, BLOCK, cols), (comps, rows, SIDE), (comps, BLOCK, SIDE)),
+        out_shape=jax.ShapeDtypeStruct((comps, BLOCK, cols), jnp.float32),
         in_specs=anywhere(1),
-        out_specs=tuple(in_vmem(3)),
-        scratch_shapes=[pltpu.SemaphoreType.DMA((3,))],
-        name="halo_strips",
+        out_specs=pl.BlockSpec(memory_space=pltpu.VMEM),
+        scratch_shapes=[pltpu.SemaphoreType.DMA((1,))],
+        compiler_params=pltpu.CompilerParams(vmem_limit_bytes=VMEM_MOST),
+        name="row_strip",
     )(tile)
 
 
@@ -760,24 +706,30 @@
     tile = object_slices.reshape(slices * parts, tile_rows, tile_cols)
     row_total = lax.axis_size("row")
     tables = jnp.asarray(TABLES)
-    strip_below, strip_right, strip_diag = strips(tile)
-    below = moved(strip_below, -1, 0)
+    below = moved(row_strip(tile), -1, 0)
+    send, strip_right, strip_diag = pack(offsets, measured, tile, row_total)
     right = moved(strip_right, 0, -1)
     diag = moved(strip_diag, -1, -1)
-    send = pack(offsets, measured, row_total)
     recv = lax.all_to_all(send, "row", split_axis=0, concat_axis=0, tiled=True)
     last, side, inner = pair_places(tile_rows, tile_cols)
     far_inner, enter_inner = forward_inner(inner, tile, probe, tables)
+    far_inner, enter_inner, right = lax.optimization_barrier((far_inner, enter_inner, right))
     far_last, enter_last, far_side, enter_side = forward_rim(
         last, side, tile, below, right, diag, probe, tables
     )
-    row, right_part, to_below, to_diag, corner = backward_last(
-        last, recv, tile, below, right, diag, probe, tables, far_last, enter_last
+    row, col, to_below, to_right, to_diag, sums, count = backward_rim(
+        recv,
+        tile,
+        below,
+        right,
+        diag,
+        probe,
+        tables,
+        (far_last, enter_last),
+        (far_side, enter_side),
+        last + side,
     )
     above = moved(to_below, 1, 0)
-    col, to_right, sums, count = backward_side(
-        side, corner, recv, tile, right, probe, tables, far_side, enter_side, right_part
-    )
     left = moved(to_right, 0, 1)
     corner_part = moved(to_diag, 1, 1)
     own = backward_inner(

time: 84.5 us -> 92.9 us (1.099)
  the two profiles are of different devices: /device:TPU:26 before, /device:TPU:33 now
where the time goes in v4:
time: 92.9 us; the launch traced here: 92.3 us
  starting transfers between devices  32.7 us (35%)
  Pallas kernels  30.8 us (33%)
  local copies, waits for them, and re-layouts  15.5 us (17%)
  waiting for transfers between devices  12.9 us (14%)
    unnamed x44, local copies, waits for them, and re-layouts  15.5 us
    ppermute x2, starting transfers between devices, moved(): return lax.ppermute(shard, ('row', 'col'), pairs)  14.9 us
    ppermute x2, waiting for transfers between devices, moved(): return lax.ppermute(shard, ('row', 'col'), pairs)  12.1 us
    pallas_call x1, Pallas kernels, backward_rim(): pl.pallas_call(functools.partial(backward_rim_kernel, places), out_shape=...  8.36 us
    all_to_all x1, starting transfers between devices, body(): recv = lax.all_to_all(send, 'row', split_axis=0, concat_axis=0, tiled=True)  7.75 us
    pallas_call x1, Pallas kernels, backward_inner(): pl.pallas_call(functools.partial(backward_inner_kernel, places), out_shap...  6.68 us
    ppermute x2, starting transfers between devices, moved(): return lax.ppermute(shard, 'col', pairs)  5.88 us
    pallas_call x1, Pallas kernels, forward_inner(): pl.pallas_call(functools.partial(forward_inner_kernel, places), out_shape...  4.21 us
  transfers between devices with their start and end apart: 7, of which 2 were waited for; matrix products, arithmetic and copies ran while one was open for 0% of the time, Pallas kernels for 20%

profile of v4, /device:TPU:33, one launch (start us, length us, event | category | flops | bytes accessed | tf_op | source)
XLA Modules:
  0.0 92.3 jit_solution(17629703937570388558)
XLA Ops:
  0.0 1.8 %row_strip.1 = f32[4,64,512]{2,1,0:T(8,128)} custom-call(f32[4,256,512]{2,1,0:T(8,128)} %bitcast.2), custom_call_target="tpu_custom_call" | custom-call | tf_op jit(solution)/shard_map/row_strip/pallas_call | solution.py:675
  1.9 1.9 %collective-permute-start = (f32[4,64,512]{2,1,0:T(8,128)}, f32[4,64,512]{2,1,0:T(8,128)S(1)}, u32[]{:S(2)}, u32[]{:S(2)}) collective-permute-start(f32[4,64,512]{2,1,0:T(8,128)} %row_strip.1), channel_id=1, source_target_pairs={{8,0},{16,8},{24,16},{32,24},{40,32},{48,40},{56,48},{64,56},{72,6... | collective-permute-start | bytes 1572872 | tf_op jit(solution)/shard_map/ppermute | solution.py:691
  3.8 3.7 %pack_measured.1 = (f32[16,264,128]{2,1,0:T(8,128)}, f32[4,256,128]{2,1,0:T(8,128)}, f32[4,64,128]{2,1,0:T(8,128)}) custom-call(s32[2,16]{1,0:T(2,128)} %off_ref.1, f32[16,128,128]{2,1,0:T(8,128)} %meas_ref.1, f32[4,256,512]{2,1,0:T(8,128)} %bitcast.3), custom_call_target="tpu_custom_call" | custom-call | bytes 41943040 | tf_op jit(solution)/shard_map/pack_measured/pallas_call | solution.py:155
  7.5 0.0 copy-start
  7.5 7.7 %all-to-all-start = ((f32[16,264,128]{2,1,0:T(8,128)}), f32[16,264,128]{2,1,0:T(8,128)}, u32[]{:S(2)}, u32[]{:S(2)}) async-start(f32[16,264,128]{2,1,0:T(8,128)} %get-tuple-element.24), calls=%async_computation | async-start | bytes 4325376 | tf_op jit(solution)/shard_map/all_to_all | solution.py:713
  15.3 3.2 %collective-permute-start.2 = (f32[4,64,128]{2,1,0:T(8,128)S(1)}, f32[4,64,128]{2,1,0:T(8,128)S(1)}, u32[]{:S(2)}, u32[]{:S(2)}) collective-permute-start(f32[4,64,128]{2,1,0:T(8,128)S(1)} %copy-done.21), channel_id=1, source_target_pairs={{9,0},{10,1},{11,2},{12,3},{13,4},{14,5},{15,6},{17,8},{18,9},{19,... | collective-permute-start | bytes 393224 | tf_op jit(solution)/shard_map/ppermute | solution.py:701
  18.5 1.9 %collective-permute-start.1 = (f32[4,256,128]{2,1,0:T(8,128)}, f32[4,256,128]{2,1,0:T(8,128)S(1)}, u32[]{:S(2)}, u32[]{:S(2)}) collective-permute-start(f32[4,256,128]{2,1,0:T(8,128)} %get-tuple-element.27), channel_id=1, source_target_pairs={{1,0},{2,1},{3,2},{4,3},{5,4},{6,5},{7,6},{9,8},{10,9},{11,10},{12... | collective-permute-start | bytes 1572872 | tf_op jit(solution)/shard_map/ppermute | solution.py:694
  20.4 0.0 copy-start.7
  20.4 1.2 %copy-done.7 = bf16[8,256,256]{2,1,0:T(8,128)(2,1)S(1)} copy-done((bf16[8,256,256]{2,1,0:T(8,128)(2,1)S(1)}, bf16[8,256,256]{2,1,0:T(8,128)(2,1)}, u32[]{:S(2)}) %copy-start.7) | copy-done | bytes 1048600
  21.6 4.2 %forward_inner.1 = (f32[9,256,256]{2,1,0:T(8,128)S(1)}, f32[9,256,256]{2,1,0:T(8,128)S(1)}) custom-call(f32[4,256,512]{2,1,0:T(8,128)S(1)} %bitcast.5, f32[2,128,128]{2,1,0:T(8,128)S(1)} %copy-done.4, bf16[8,256,256]{2,1,0:T(8,128)(2,1)S(1)} %copy-done.7), custom_call_target="tpu_custom_call" | custom-call | flops 28991029248 | bytes 1048576 | tf_op jit(solution)/shard_map/forward_inner/pallas_call | solution.py:291
  25.9 1.4 %copy-done.9 = f32[9,256,256]{2,1,0:T(8,128)} copy-done((f32[9,256,256]{2,1,0:T(8,128)}, f32[9,256,256]{2,1,0:T(8,128)S(1)}, u32[]{:S(2)}) %copy-start.9) | copy-done | bytes 2359320
  27.3 1.4 %copy-done.11 = f32[9,256,256]{2,1,0:T(8,128)} copy-done((f32[9,256,256]{2,1,0:T(8,128)}, f32[9,256,256]{2,1,0:T(8,128)S(1)}, u32[]{:S(2)}) %copy-start.11) | copy-done | bytes 2359320
  28.7 0.9 collective-permute-done.1.right_ref
  29.6 12.0 %collective-permute-done.2.diag_ref = f32[4,64,128]{2,1,0:T(8,128)S(1)} collective-permute-done((f32[4,64,128]{2,1,0:T(8,128)S(1)}, f32[4,64,128]{2,1,0:T(8,128)S(1)}, u32[]{:S(2)}, u32[]{:S(2)}) %collective-permute-start.2) | collective-permute-done | bytes 131104 | tf_op jit(solution)/shard_map/ppermute | solution.py:701
  41.6 3.7 %forward_rim.1 = (f32[4,256,256]{2,1,0:T(8,128)S(1)}, f32[4,256,256]{2,1,0:T(8,128)S(1)}, f32[3,256,256]{2,1,0:T(8,128)S(1)}, f32[3,256,256]{2,1,0:T(8,128)S(1)}) custom-call(f32[4,256,512]{2,1,0:T(8,128)S(1)} %bitcast.6, f32[4,64,512]{2,1,0:T(8,128)S(1)} %collective-permute-done.below_ref, f32[4,256,128]{2,1,0:T(8,128)S(1)} %collective-permute-done.1.right_ref, ...), custom_call_target="tpu_custom_call" | custom-call | flops 22548578304 | bytes 1048576 | tf_op jit(solution)/shard_map/forward_rim/pallas_call | solution.py:308
  45.4 0.0 copy-start.14
  45.4 1.0 %copy-done.14 = f32[4,256,256]{2,1,0:T(8,128)} copy-done((f32[4,256,256]{2,1,0:T(8,128)}, f32[4,256,256]{2,1,0:T(8,128)S(1)}, u32[]{:S(2)}) %copy-start.14) | copy-done | bytes 1048600
  46.3 1.0 %copy-done.15 = f32[4,256,256]{2,1,0:T(8,128)} copy-done((f32[4,256,256]{2,1,0:T(8,128)}, f32[4,256,256]{2,1,0:T(8,128)S(1)}, u32[]{:S(2)}) %copy-start.15) | copy-done | bytes 1048600
  47.3 0.9 copy-done.18
  48.2 0.9 copy-done.19
  49.1 8.4 %backward_rim.1 = (f32[4,64,512]{2,1,0:T(8,128)}, f32[4,256,128]{2,1,0:T(8,128)}, f32[4,64,512]{2,1,0:T(8,128)}, f32[4,128,128]{2,1,0:T(8,128)}, f32[4,64,128]{2...) custom-call(f32[16,264,128]{2,1,0:T(8,128)} %all-to-all-done.recv_ref, f32[4,256,512]{2,1,0:T(8,128)} %bitcast.4, ...), custom_call_target="tpu_custom_call" | custom-call | flops 2818572288 | bytes 1048576 | tf_op jit(solution)/shard_map/backward_rim/pallas_call | solution.py:567
  57.4 2.2 %collective-permute-start.3 = (f32[4,64,512]{2,1,0:T(8,128)}, f32[4,64,512]{2,1,0:T(8,128)S(1)}, u32[]{:S(2)}, u32[]{:S(2)}) collective-permute-start(f32[4,64,512]{2,1,0:T(8,128)} %get-tuple-element.40), channel_id=1, source_target_pairs={{0,8},{8,16},{16,24},{24,32},{32,40},{40,48},{48,56},{56,64},{64,7... | collective-permute-start | bytes 1572872 | tf_op jit(solution)/shard_map/ppermute | solution.py:691
  59.6 11.8 %collective-permute-start.5 = (f32[4,64,128]{2,1,0:T(8,128)}, f32[4,64,128]{2,1,0:T(8,128)S(1)}, u32[]{:S(2)}, u32[]{:S(2)}) collective-permute-start(f32[4,64,128]{2,1,0:T(8,128)} %get-tuple-element.42), channel_id=1, source_target_pairs={{0,9},{1,10},{2,11},{3,12},{4,13},{5,14},{6,15},{8,17},{9,18},{10,... | collective-permute-start | bytes 393224 | tf_op jit(solution)/shard_map/ppermute | solution.py:701
  71.4 4.0 %collective-permute-start.4 = (f32[4,128,128]{2,1,0:T(8,128)}, f32[4,128,128]{2,1,0:T(8,128)S(1)}, u32[]{:S(2)}, u32[]{:S(2)}) collective-permute-start(f32[4,128,128]{2,1,0:T(8,128)} %get-tuple-element.41), channel_id=1, source_target_pairs={{0,1},{1,2},{2,3},{3,4},{4,5},{5,6},{6,7},{8,9},{9,10},{10,11},{11... | collective-permute-start | bytes 786440 | tf_op jit(solution)/shard_map/ppermute | solution.py:694
  75.4 1.7 %copy-done.10 = f32[9,256,256]{2,1,0:T(8,128)S(1)} copy-done((f32[9,256,256]{2,1,0:T(8,128)S(1)}, f32[9,256,256]{2,1,0:T(8,128)}, u32[]{:S(2)}) %copy-start.10) | copy-done | bytes 2359320
  77.0 1.7 %copy-done.12 = f32[9,256,256]{2,1,0:T(8,128)S(1)} copy-done((f32[9,256,256]{2,1,0:T(8,128)S(1)}, f32[9,256,256]{2,1,0:T(8,128)}, u32[]{:S(2)}) %copy-start.12) | copy-done | bytes 2359320
  78.7 1.6 %copy-done.13 = f32[33,128,128]{2,1,0:T(8,128)S(1)} copy-done((f32[33,128,128]{2,1,0:T(8,128)S(1)}, f32[33,128,128]{2,1,0:T(8,128)}, u32[]{:S(2)}) %copy-start.13) | copy-done | bytes 2162712
  80.3 1.0 %copy-done.16 = f32[4,64,512]{2,1,0:T(8,128)S(1)} copy-done((f32[4,64,512]{2,1,0:T(8,128)S(1)}, f32[4,64,512]{2,1,0:T(8,128)}, u32[]{:S(2)}) %copy-start.16) | copy-done | bytes 524312
  81.4 1.0 %copy-done.17 = f32[4,256,128]{2,1,0:T(8,128)S(1)} copy-done((f32[4,256,128]{2,1,0:T(8,128)S(1)}, f32[4,256,128]{2,1,0:T(8,128)}, u32[]{:S(2)}) %copy-start.17) | copy-done | bytes 524312
  82.4 0.7 copy-done.20
  83.0 6.7 %backward_inner.1.own_ref = f32[4,256,512]{2,1,0:T(8,128)} custom-call(s32[33]{0:T(128)S(1)} %copy-done.20, f32[33,128,128]{2,1,0:T(8,128)S(1)} %copy-done.13, f32[4,256,512]{2,1,0:T(8,128)S(1)} %bitcast.7, f32[2,128,128]{2,1,0:T(8,128)S(1)} %copy-done.5, bf16[8,256,256]{2,1,0:T(8,128)(2,1)S(1)} %copy-done.8, f32[9,256,256]{2,1,0:T(8,128)S(1)} %copy-done.10, ...), custom_call_target="tpu_custom_call" | custom-call | flops 3623878656 | bytes 1048576 | tf_op jit(solution)/shard_map/backward_inner/pallas_call | solution.py:602
  89.7 2.4 %add_borders.1 = f32[4,256,512]{2,1,0:T(8,128)} custom-call(f32[4,256,512]{2,1,0:T(8,128)} %backward_inner.1.own_ref, f32[4,64,512]{2,1,0:T(8,128)S(1)} %collective-permute-done.3.above_ref, f32[4,128,128]{2,1,0:T(8,128)S(1)} %collective-permute-done.4.left_ref, f32[4,64,128]{2,1,0:T(8,128)S(1)} %collective-permute-done.5.diag_ref), custom_call_target="tpu_custom_call", output_to_operand_aliasing={{}: (0, {})} | custom-call | tf_op jit(solution)/shard_map/add_borders/pallas_call | solution.py:650
  (33 shorter events, 0.1 us)
Async XLA Ops:
  1.9 39.8 %collective-permute-start = (f32[4,64,512]{2,1,0:T(8,128)}, f32[4,64,512]{2,1,0:T(8,128)S(1)}, u32[]{:S(2)}, u32[]{:S(2)}) collective-permute-start(f32[4,64,512]{2,1,0:T(8,128)} %row_strip.1), channel_id=1, source_target_pairs={{8,0},{16,8},{24,16},{32,24},{40,32},{48,40},{56,48},{64,56},{72,6... | collective-permute-start | bytes 1572872 | tf_op jit(solution)/shard_map/ppermute | solution.py:691
  7.5 7.8 %copy-start.21 = (f32[4,64,128]{2,1,0:T(8,128)S(1)}, f32[4,64,128]{2,1,0:T(8,128)}, u32[]{:S(2)}) copy-start(f32[4,64,128]{2,1,0:T(8,128)} %get-tuple-element.29) | copy-start | bytes 393220
  7.5 12.9 %copy-start = (f32[2,2,256,512]{3,2,1,0:T(8,128)S(1)}, f32[2,2,256,512]{3,2,1,0:T(8,128)}, u32[]{:S(2)}) copy-start(f32[2,2,256,512]{3,2,1,0:T(8,128)} %param.5) | copy-start | bytes 6291460
  7.5 12.9 %copy-start.4 = (f32[2,128,128]{2,1,0:T(8,128)S(1)}, f32[2,128,128]{2,1,0:T(8,128)}, u32[]{:S(2)}) copy-start(f32[2,128,128]{2,1,0:T(8,128)} %probe_ref.7) | copy-start | bytes 393220
  7.5 41.5 %all-to-all-start = ((f32[16,264,128]{2,1,0:T(8,128)}), f32[16,264,128]{2,1,0:T(8,128)}, u32[]{:S(2)}, u32[]{:S(2)}) async-start(f32[16,264,128]{2,1,0:T(8,128)} %get-tuple-element.24), calls=%async_computation | async-start | bytes 4325376 | tf_op jit(solution)/shard_map/all_to_all | solution.py:713
  15.3 26.3 %collective-permute-start.2 = (f32[4,64,128]{2,1,0:T(8,128)S(1)}, f32[4,64,128]{2,1,0:T(8,128)S(1)}, u32[]{:S(2)}, u32[]{:S(2)}) collective-permute-start(f32[4,64,128]{2,1,0:T(8,128)S(1)} %copy-done.21), channel_id=1, source_target_pairs={{9,0},{10,1},{11,2},{12,3},{13,4},{14,5},{15,6},{17,8},{18,9},{19,... | collective-permute-start | bytes 393224 | tf_op jit(solution)/shard_map/ppermute | solution.py:701
  18.5 11.1 %collective-permute-start.1 = (f32[4,256,128]{2,1,0:T(8,128)}, f32[4,256,128]{2,1,0:T(8,128)S(1)}, u32[]{:S(2)}, u32[]{:S(2)}) collective-permute-start(f32[4,256,128]{2,1,0:T(8,128)} %get-tuple-element.27), channel_id=1, source_target_pairs={{1,0},{2,1},{3,2},{4,3},{5,4},{6,5},{7,6},{9,8},{10,9},{11,10},{12... | collective-permute-start | bytes 1572872 | tf_op jit(solution)/shard_map/ppermute | solution.py:694
  20.4 1.2 %copy-start.7 = (bf16[8,256,256]{2,1,0:T(8,128)(2,1)S(1)}, bf16[8,256,256]{2,1,0:T(8,128)(2,1)}, u32[]{:S(2)}) copy-start(bf16[8,256,256]{2,1,0:T(8,128)(2,1)} %constant.2.clone.tables.tables_ref) | copy-start | bytes 3145732
  25.9 1.4 %copy-start.9 = (f32[9,256,256]{2,1,0:T(8,128)}, f32[9,256,256]{2,1,0:T(8,128)S(1)}, u32[]{:S(2)}) copy-start(f32[9,256,256]{2,1,0:T(8,128)S(1)} %get-tuple-element.36.far_ref) | copy-start | bytes 7077892
  27.3 1.4 %copy-start.11 = (f32[9,256,256]{2,1,0:T(8,128)}, f32[9,256,256]{2,1,0:T(8,128)S(1)}, u32[]{:S(2)}) copy-start(f32[9,256,256]{2,1,0:T(8,128)S(1)} %get-tuple-element.37.enter_ref) | copy-start | bytes 7077892
  29.6 15.8 %copy-start.3 = (f32[4,256,128]{2,1,0:T(8,128)}, f32[4,256,128]{2,1,0:T(8,128)S(1)}, u32[]{:S(2)}) copy-start(f32[4,256,128]{2,1,0:T(8,128)S(1)} %collective-permute-done.1.right_ref) | copy-start | bytes 1572868
  41.6 3.7 %copy-start.6 = (f32[4,64,128]{2,1,0:T(8,128)}, f32[4,64,128]{2,1,0:T(8,128)S(1)}, u32[]{:S(2)}) copy-start(f32[4,64,128]{2,1,0:T(8,128)S(1)} %collective-permute-done.2.diag_ref) | copy-start | bytes 393220
  41.6 3.7 %copy-start.2 = (f32[4,64,512]{2,1,0:T(8,128)}, f32[4,64,512]{2,1,0:T(8,128)S(1)}, u32[]{:S(2)}) copy-start(f32[4,64,512]{2,1,0:T(8,128)S(1)} %collective-permute-done.below_ref) | copy-start | bytes 1572868
  45.4 1.0 %copy-start.14 = (f32[4,256,256]{2,1,0:T(8,128)}, f32[4,256,256]{2,1,0:T(8,128)S(1)}, u32[]{:S(2)}) copy-start(f32[4,256,256]{2,1,0:T(8,128)S(1)} %get-tuple-element.30.far_last_ref) | copy-start | bytes 3145732
  46.3 1.0 %copy-start.15 = (f32[4,256,256]{2,1,0:T(8,128)}, f32[4,256,256]{2,1,0:T(8,128)S(1)}, u32[]{:S(2)}) copy-start(f32[4,256,256]{2,1,0:T(8,128)S(1)} %get-tuple-element.31.enter_last_ref) | copy-start | bytes 3145732
  47.3 0.9 copy-start.18
  48.2 0.9 copy-start.19
  49.1 26.3 %copy-start.1 = (f32[2,2,256,512]{3,2,1,0:T(8,128)S(1)}, f32[2,2,256,512]{3,2,1,0:T(8,128)}, u32[]{:S(2)}) copy-start(f32[2,2,256,512]{3,2,1,0:T(8,128)} %param.5) | copy-start | bytes 6291460
  49.1 26.3 %copy-start.5 = (f32[2,128,128]{2,1,0:T(8,128)S(1)}, f32[2,128,128]{2,1,0:T(8,128)}, u32[]{:S(2)}) copy-start(f32[2,128,128]{2,1,0:T(8,128)} %probe_ref.7) | copy-start | bytes 393220
  49.1 26.3 %copy-start.8 = (bf16[8,256,256]{2,1,0:T(8,128)(2,1)S(1)}, bf16[8,256,256]{2,1,0:T(8,128)(2,1)}, u32[]{:S(2)}) copy-start(bf16[8,256,256]{2,1,0:T(8,128)(2,1)} %constant.2.clone.tables.tables_ref) | copy-start | bytes 3145732
  57.4 32.3 %collective-permute-start.3 = (f32[4,64,512]{2,1,0:T(8,128)}, f32[4,64,512]{2,1,0:T(8,128)S(1)}, u32[]{:S(2)}, u32[]{:S(2)}) collective-permute-start(f32[4,64,512]{2,1,0:T(8,128)} %get-tuple-element.40), channel_id=1, source_target_pairs={{0,8},{8,16},{16,24},{24,32},{32,40},{40,48},{48,56},{56,64},{64,7... | collective-permute-start | bytes 1572872 | tf_op jit(solution)/shard_map/ppermute | solution.py:691
  59.6 30.1 %collective-permute-start.5 = (f32[4,64,128]{2,1,0:T(8,128)}, f32[4,64,128]{2,1,0:T(8,128)S(1)}, u32[]{:S(2)}, u32[]{:S(2)}) collective-permute-start(f32[4,64,128]{2,1,0:T(8,128)} %get-tuple-element.42), channel_id=1, source_target_pairs={{0,9},{1,10},{2,11},{3,12},{4,13},{5,14},{6,15},{8,17},{9,18},{10,... | collective-permute-start | bytes 393224 | tf_op jit(solution)/shard_map/ppermute | solution.py:701
  71.4 18.4 %collective-permute-start.4 = (f32[4,128,128]{2,1,0:T(8,128)}, f32[4,128,128]{2,1,0:T(8,128)S(1)}, u32[]{:S(2)}, u32[]{:S(2)}) collective-permute-start(f32[4,128,128]{2,1,0:T(8,128)} %get-tuple-element.41), channel_id=1, source_target_pairs={{0,1},{1,2},{2,3},{3,4},{4,5},{5,6},{6,7},{8,9},{9,10},{10,11},{11... | collective-permute-start | bytes 786440 | tf_op jit(solution)/shard_map/ppermute | solution.py:694
  75.4 1.7 %copy-start.10 = (f32[9,256,256]{2,1,0:T(8,128)S(1)}, f32[9,256,256]{2,1,0:T(8,128)}, u32[]{:S(2)}) copy-start(f32[9,256,256]{2,1,0:T(8,128)} %copy-done.9) | copy-start | bytes 7077892
  77.0 1.7 %copy-start.12 = (f32[9,256,256]{2,1,0:T(8,128)S(1)}, f32[9,256,256]{2,1,0:T(8,128)}, u32[]{:S(2)}) copy-start(f32[9,256,256]{2,1,0:T(8,128)} %copy-done.11) | copy-start | bytes 7077892
  78.7 1.6 %copy-start.13 = (f32[33,128,128]{2,1,0:T(8,128)S(1)}, f32[33,128,128]{2,1,0:T(8,128)}, u32[]{:S(2)}) copy-start(f32[33,128,128]{2,1,0:T(8,128)} %get-tuple-element.35.sum_ref) | copy-start | bytes 6488068
  80.3 1.0 %copy-start.16 = (f32[4,64,512]{2,1,0:T(8,128)S(1)}, f32[4,64,512]{2,1,0:T(8,128)}, u32[]{:S(2)}) copy-start(f32[4,64,512]{2,1,0:T(8,128)} %get-tuple-element.38.row_ref) | copy-start | bytes 1572868
  81.4 1.0 %copy-start.17 = (f32[4,256,128]{2,1,0:T(8,128)S(1)}, f32[4,256,128]{2,1,0:T(8,128)}, u32[]{:S(2)}) copy-start(f32[4,256,128]{2,1,0:T(8,128)} %get-tuple-element.39.col_ref) | copy-start | bytes 1572868
  82.4 0.7 copy-start.20

commit v5 on v4

--- a/solution.py
+++ b/solution.py
@@ -15,8 +15,8 @@
 BLOCK = 64
 CAP = 2
 META = 8
-VMEM_LIMIT = 28 * 1024 * 1024
-VMEM_MOST = 60 * 1024 * 1024
+CHUNKS = 4
+VMEM_LIMIT = 64 * 1024 * 1024
 
 
 def dft_matrix():
@@ -104,19 +104,9 @@
     return (left_re * right_re + left_im * right_im, left_re * right_im - left_im * right_re)
 
 
-def pack_kernel(
-    off_ref, meas_ref, tile_ref, send_ref, right_ref, diag_ref, meta_ref, count_ref, corner_ref, sems
-):
+def pack_kernel(off_ref, meas_ref, send_ref, meta_ref, count_ref, corner_ref, sems):
     owners = send_ref.shape[0]
     positions = meas_ref.shape[0]
-    left = pl.ds(0, SIDE)
-    strips = start_copies(
-        [
-            (tile_ref.at[:, :, left], right_ref),
-            (tile_ref.at[:, pl.ds(0, BLOCK), left], diag_ref),
-        ],
-        sems.at[pl.ds(positions + 1, 2)],
-    )
     for owner in range(owners):
         count_ref[owner] = 0
         for rank in range(CAP):
@@ -146,30 +136,32 @@
     )
     copy.start()
     copies.append(copy)
-    wait_copies(copies + strips)
-
-
-def pack(offsets, measured, tile, owners):
+    for copy in copies:
+        copy.wait()
+
+
+def pack(offsets, measured, owners):
     positions = measured.shape[0]
-    comps, rows, _ = tile.shape
     return pl.pallas_call(
         pack_kernel,
-        out_shape=shapes_of(
-            (owners, CAP * SIDE + META, SIDE), (comps, rows, SIDE), (comps, BLOCK, SIDE)
-        ),
-        in_specs=[pl.BlockSpec(memory_space=pltpu.SMEM)] + in_vmem(1) + anywhere(1),
-        out_specs=tuple(anywhere(1) + in_vmem(2)),
+        out_shape=jax.ShapeDtypeStruct((owners, CAP * SIDE + META, SIDE), jnp.float32),
+        in_specs=[
+            pl.BlockSpec(memory_space=pltpu.SMEM),
+            pl.BlockSpec(memory_space=pltpu.VMEM),
+        ],
+        out_specs=pl.BlockSpec(memory_space=pl.ANY),
         scratch_shapes=[
             pltpu.VMEM((owners, META, SIDE), jnp.float32),
             pltpu.SMEM((owners,), jnp.int32),
             pltpu.SMEM((owners * CAP,), jnp.int32),
-            pltpu.SemaphoreType.DMA((positions + 3,)),
+            pltpu.SemaphoreType.DMA((positions + 1,)),
         ],
+        compiler_params=pltpu.CompilerParams(vmem_limit_bytes=VMEM_LIMIT),
         cost_estimate=pl.CostEstimate(
             flops=0, bytes_accessed=40 * 1024 * 1024, transcendentals=0
         ),
         name="pack_measured",
-    )(offsets, measured, tile)
+    )(offsets, measured)
 
 
 def pair_places(rows, cols):
@@ -208,17 +200,6 @@
     return [ref.at[pair] for pair in range(ref.shape[0])]
 
 
-def extended_parts(tile_ref, below_ref, right_ref, diag_ref, ext_ref, first):
-    rows, cols = tile_ref.shape[1:]
-    comps = pl.ds(first, tile_ref.shape[0] - first)
-    return [
-        (tile_ref.at[comps], ext_ref.at[:, pl.ds(0, rows), pl.ds(0, cols)]),
-        (below_ref.at[comps], ext_ref.at[:, pl.ds(rows, BLOCK), pl.ds(0, cols)]),
-        (right_ref.at[comps], ext_ref.at[:, pl.ds(0, rows), pl.ds(cols, SIDE)]),
-        (diag_ref.at[comps], ext_ref.at[:, pl.ds(rows, BLOCK), pl.ds(cols, SIDE)]),
-    ]
-
-
 def start_copies(parts, sems):
     copies = [
         pltpu.make_async_copy(source, target, sems.at[n])
@@ -253,9 +234,16 @@
     ext_ref,
     sems,
 ):
+    rows, cols = tile_ref.shape[1:]
     wait_copies(
         start_copies(
-            extended_parts(tile_ref, below_ref, right_ref, diag_ref, ext_ref, 0), sems
+            [
+                (tile_ref, ext_ref.at[:, pl.ds(0, rows), pl.ds(0, cols)]),
+                (below_ref, ext_ref.at[:, pl.ds(rows, BLOCK), pl.ds(0, cols)]),
+                (right_ref, ext_ref.at[:, pl.ds(0, rows), pl.ds(cols, SIDE)]),
+                (diag_ref, ext_ref.at[:, pl.ds(rows, BLOCK), pl.ds(cols, SIDE)]),
+            ],
+            sems,
         )
     )
     forward_pairs(
@@ -285,6 +273,10 @@
 
 def anywhere(count):
     return [pl.BlockSpec(memory_space=pl.ANY)] * count
+
+
+def in_hbm(count):
+    return [pl.BlockSpec(memory_space=pltpu.HBM)] * count
 
 
 def forward_inner(places, tile, probe, tables):
@@ -308,7 +300,7 @@
     return pl.pallas_call(
         functools.partial(forward_rim_kernel, places),
         out_shape=fields(last) + fields(side),
-        in_specs=anywhere(4) + in_vmem(2),
+        in_specs=in_hbm(4) + in_vmem(2),
         out_specs=tuple(in_vmem(4)),
         scratch_shapes=[extended_shape(tile, tile.shape[0]), pltpu.SemaphoreType.DMA((4,))],
         compiler_params=pltpu.CompilerParams(vmem_limit_bytes=VMEM_LIMIT),
@@ -317,11 +309,14 @@
     )(tile, below, right, diag, probe, tables)
 
 
-def gather_sums(meta_ref, items_ref, sum_ref, count_ref):
+def gather_sums(meta_ref, items_ref, sum_ref, count_ref, arrivals):
     spare = sum_ref.shape[0] - 1
+    sources = items_ref.shape[0]
     for corner in range(spare + 1):
         count_ref[corner] = 0
-    for source in range(items_ref.shape[0]):
+    for source in range(sources):
+        if source % (sources // len(arrivals)) == 0:
+            arrivals[source * len(arrivals) // sources].wait()
         for rank in range(CAP):
             corner = meta_ref[source, rank * BLOCK].astype(jnp.int32)
             at = jnp.where(corner < 0, spare, corner)
@@ -347,11 +342,14 @@
     sum_ref,
     count_ref,
     store,
-    before_fields=None,
-    before_products=None,
+    before_pair,
+    before_products,
+    before_fields,
+    after_fields,
 ):
     rows = []
     for pair, (row, col) in enumerate(places):
+        before_pair(pair)
         waves = []
         for n in range(2):
             at = row * width + col // BLOCK + n
@@ -360,11 +358,9 @@
             misfit = 2.0 * (hits * (far_re * far_re + far_im * far_im) - total)
             waves.append((misfit * far_re, misfit * far_im))
         rows.append(stacked(waves))
-    if before_products is not None:
-        before_products()
+    before_products()
     backs = two_sided(rows, tables, 6, 4)
-    if before_fields is not None:
-        before_fields()
+    before_fields()
     rows = []
     for pair, (row, col) in enumerate(places):
         trans = [cut_pair(ext_ref, comp, row * BLOCK, col) for comp in range(2)]
@@ -376,6 +372,7 @@
             store(n, 3, row, col, grad[1])
             waves.append(conj_times(trans[0][n], trans[1][n], *back))
         rows.append(stacked(waves))
+    after_fields()
     backs = two_sided(rows, tables, 2, 0)
     probe_re = probe_ref[0]
     probe_im = probe_ref[1]
@@ -412,7 +409,7 @@
     out_below_ref,
     out_right_ref,
     out_diag_ref,
-    sum_ref,
+    out_sum_ref,
     count_ref,
     items_ref,
     meta_ref,
@@ -421,35 +418,57 @@
     far_buf,
     enter_buf,
     ext_ref,
+    sum_ref,
     even_ref,
     odd_ref,
     even_side_ref,
     odd_side_ref,
+    row_buf,
+    col_buf,
+    below_buf,
+    right_buf,
+    diag_buf,
     sems,
+    out_sems,
 ):
     rows, cols = tile_ref.shape[1:]
     last = rows // BLOCK - 1
-    first = pl.ds(0, far_last_ref.shape[0])
-    others = pl.ds(far_last_ref.shape[0], far_side_ref.shape[0])
+    corners = sum_ref.shape[0] - 1
+    near = far_last_ref.shape[0]
+    first = pl.ds(0, near)
+    others = pl.ds(near, far_side_ref.shape[0])
+    two = pl.ds(2, 2)
+    chunk = recv_ref.shape[0] // CHUNKS
+    wide = pl.ds(0, cols)
+    beyond = pl.ds(cols, SIDE)
     copies = start_copies(
-        [
-            (recv_ref.at[:, CAP * SIDE], meta_ref),
-            (recv_ref.at[:, pl.ds(0, CAP * SIDE)], items_ref),
+        [(recv_ref.at[:, CAP * SIDE], meta_ref)]
+        + [
+            (recv_ref.at[part, pl.ds(0, CAP * SIDE)], items_ref.at[part])
+            for part in (pl.ds(n * chunk, chunk) for n in range(CHUNKS))
+        ]
+        + [
             (far_last_ref, far_buf.at[first]),
+            (tables_ref, table_buf),
             (far_side_ref, far_buf.at[others]),
-            (tables_ref, table_buf),
             (enter_last_ref, enter_buf.at[first]),
             (enter_side_ref, enter_buf.at[others]),
+            (tile_ref.at[two], ext_ref.at[:, pl.ds(0, rows), wide]),
+            (below_ref.at[two], ext_ref.at[:, pl.ds(rows, BLOCK), wide]),
+            (right_ref.at[two], ext_ref.at[:, pl.ds(0, rows), beyond]),
+            (diag_ref.at[two], ext_ref.at[:, pl.ds(rows, BLOCK), beyond]),
             (probe_ref, probe_buf),
-        ]
-        + extended_parts(tile_ref, below_ref, right_ref, diag_ref, ext_ref, 2),
+        ],
         sems,
     )
-    wait_copies(copies[:2])
-    gather_sums(meta_ref, items_ref, sum_ref, count_ref)
-    wait_copies(copies[2:4])
+    wait_copies(copies[:1])
+    rest = copies[1 + CHUNKS :]
+    gather_sums(meta_ref, items_ref, sum_ref, count_ref, copies[1 : 1 + CHUNKS])
     bands = (even_ref, odd_ref)
     sides = (even_side_ref, odd_side_ref)
+    stores = start_copies(
+        [(sum_ref.at[pl.ds(0, corners)], out_sum_ref)], out_sems.at[pl.ds(20, 1)]
+    )
 
     def store(n, comp, row, col, value):
         if row == last:
@@ -461,6 +480,51 @@
                 top = top + sides[n][comp, at : at + BLOCK]
             sides[n][comp, at : at + BLOCK] = top
             sides[n][comp, at + BLOCK : at + SIDE] = value[BLOCK:]
+
+    half = rows // 2
+
+    def finish(comp):
+        beyond_cols = []
+        for buf, part in ((row_buf, slice(0, BLOCK)), (below_buf, slice(BLOCK, SIDE))):
+            before = None
+            for col in range(0, cols, SIDE):
+                here = odd_ref[comp, part, col : col + SIDE]
+                buf[comp, :, col : col + SIDE] = even_ref[
+                    comp, part, col : col + SIDE
+                ] + shifted(before, here)
+                before = here
+            beyond_cols.append(shifted(before, None))
+        corner = beyond_cols[1]
+        diag_buf[comp] = corner[: BLOCK // 2] + pltpu.roll(corner[BLOCK // 2 :], BLOCK, 1)
+        odd_side = odd_side_ref[comp]
+        col_buf[comp] = even_side_ref[comp] + shifted(None, odd_side)
+        side = shifted(odd_side, None)
+        second = jnp.concatenate(
+            [side[half : rows - BLOCK], side[rows - BLOCK :] + beyond_cols[0]], axis=0
+        )
+        right_buf[comp] = side[:half] + pltpu.roll(second, BLOCK, 1)
+        stores.extend(
+            start_copies(
+                [
+                    (below_buf.at[comp], out_below_ref.at[comp]),
+                    (diag_buf.at[comp], out_diag_ref.at[comp]),
+                    (right_buf.at[comp], out_right_ref.at[comp]),
+                    (row_buf.at[comp], row_ref.at[comp]),
+                    (col_buf.at[comp], col_ref.at[comp]),
+                ],
+                out_sems.at[pl.ds(5 * comp, 5)],
+            )
+        )
+
+    def before_pair(pair):
+        if pair == 0:
+            rest[0].wait()
+        if pair == near:
+            rest[2].wait()
+
+    def after_fields():
+        finish(2)
+        finish(3)
 
     backward_pairs(
         places,
@@ -473,32 +537,14 @@
         sum_ref,
         count_ref,
         store,
-        lambda: wait_copies(copies[5:]),
-        lambda: wait_copies(copies[4:5]),
-    )
-    half = rows // 2
-    for comp in range(4):
-        beyond = []
-        for out_ref, part in (
-            (row_ref, slice(0, BLOCK)),
-            (out_below_ref, slice(BLOCK, SIDE)),
-        ):
-            before = None
-            for col in range(0, cols, SIDE):
-                here = odd_ref[comp, part, col : col + SIDE]
-                out_ref[comp, :, col : col + SIDE] = even_ref[
-                    comp, part, col : col + SIDE
-                ] + shifted(before, here)
-                before = here
-            beyond.append(shifted(before, None))
-        out_diag_ref[comp] = beyond[1]
-        odd_side = odd_side_ref[comp]
-        col_ref[comp] = even_side_ref[comp] + shifted(None, odd_side)
-        side = shifted(odd_side, None)
-        second = jnp.concatenate(
-            [side[half : rows - BLOCK], side[rows - BLOCK :] + beyond[0]], axis=0
-        )
-        out_right_ref[comp] = side[:half] + pltpu.roll(second, BLOCK, 1)
+        before_pair,
+        lambda: wait_copies(rest[1:2]),
+        lambda: wait_copies(rest[3:]),
+        after_fields,
+    )
+    finish(0)
+    finish(1)
+    wait_copies(stores)
 
 
 def backward_inner_kernel(
@@ -507,18 +553,54 @@
     sum_ref,
     tile_ref,
     probe_ref,
-    tables,
+    tables_ref,
     far_ref,
     enter_ref,
     row_ref,
     col_ref,
     out_ref,
+    sum_buf,
+    trans_buf,
+    probe_buf,
+    table_buf,
+    far_buf,
+    enter_buf,
+    row_buf,
+    col_buf,
+    out_buf,
     even_ref,
     odd_ref,
+    sems,
+    out_sems,
 ):
-    rows, cols = out_ref.shape[1:]
+    comps, rows, cols = out_buf.shape
     last = rows - BLOCK
+    width = cols // BLOCK
     acc = (even_ref, odd_ref)
+    row_blocks = last // BLOCK
+    group = len(places) // row_blocks
+    parts = []
+    for n in range(row_blocks):
+        here = pl.ds(n * width, width)
+        parts.append((sum_ref.at[here], sum_buf.at[here]))
+        here = pl.ds(n * group, group)
+        parts.append((far_ref.at[here], far_buf.at[here]))
+        if n == 0:
+            parts.append((tables_ref, table_buf))
+    copies = start_copies(
+        parts
+        + [
+            (enter_ref, enter_buf),
+            (tile_ref.at[pl.ds(2, 2)], trans_buf),
+            (probe_ref, probe_buf),
+            (row_ref, row_buf),
+            (col_ref, col_buf),
+        ],
+        sems,
+    )
+    table_copy = copies.pop(2)
+    rest = copies[2 * row_blocks :]
+    stores = []
 
     def store(n, comp, row, col, value):
         at = row * BLOCK
@@ -529,19 +611,7 @@
         acc[n][comp, at : at + BLOCK, lanes] = top
         acc[n][comp, at + BLOCK : at + SIDE, lanes] = value[BLOCK:]
 
-    backward_pairs(
-        places,
-        cols // BLOCK,
-        probe_ref,
-        tables,
-        far_ref,
-        enter_ref,
-        tile_ref.at[pl.ds(2, 2)],
-        sum_ref,
-        count_ref,
-        store,
-    )
-    for comp in range(4):
+    def finish(comp):
         before = None
         for col in range(0, cols, SIDE):
             lanes = slice(col, col + SIDE)
@@ -550,33 +620,67 @@
                 value = even_ref[comp, :, lanes] + shifted(before, here)
                 before = here
             else:
-                value = col_ref[comp] + shifted(before, None)
-            out_ref[comp, :last, lanes] = value[:last]
-            out_ref[comp, last:, lanes] = value[last:] + row_ref[comp, :, lanes]
+                value = col_buf[comp] + shifted(before, None)
+            out_buf[comp, :last, lanes] = value[:last]
+            out_buf[comp, last:, lanes] = value[last:] + row_buf[comp, :, lanes]
+        stores.extend(
+            start_copies(
+                [(out_buf.at[comp], out_ref.at[comp])], out_sems.at[pl.ds(comp, 1)]
+            )
+        )
+
+    def before_pair(pair):
+        if pair % group == 0:
+            at = 2 * (pair // group)
+            wait_copies(copies[at : at + 2])
+
+    def after_fields():
+        finish(2)
+        finish(3)
+
+    backward_pairs(
+        places,
+        width,
+        probe_buf,
+        table_buf,
+        far_buf,
+        enter_buf,
+        trans_buf,
+        sum_buf,
+        count_ref,
+        store,
+        before_pair,
+        table_copy.wait,
+        lambda: wait_copies(rest),
+        after_fields,
+    )
+    finish(0)
+    finish(1)
+    wait_copies(stores)
 
 
 def shapes_of(*shapes):
     return tuple(jax.ShapeDtypeStruct(shape, jnp.float32) for shape in shapes)
 
 
-def backward_rim(recv, tile, below, right, diag, probe, tables, fields_last, fields_side, places):
+def backward_rim(places, recv, tile, below, right, diag, probe, tables, fields_last, fields_side):
     comps, rows, cols = tile.shape
-    corners = (rows // BLOCK) * (cols // BLOCK) + 1
+    corners = (rows // BLOCK) * (cols // BLOCK)
     sources = recv.shape[0]
     field = (len(places), 2 * SIDE, 2 * SIDE)
+    outs = (
+        (comps, BLOCK, cols),
+        (comps, rows, SIDE),
+        (comps, BLOCK, cols),
+        (comps, rows // 2, SIDE),
+        (comps, BLOCK // 2, SIDE),
+    )
     return pl.pallas_call(
         functools.partial(backward_rim_kernel, places),
-        out_shape=shapes_of(
-            (comps, BLOCK, cols),
-            (comps, rows, SIDE),
-            (comps, BLOCK, cols),
-            (comps, rows // 2, SIDE),
-            (comps, BLOCK, SIDE),
-            (corners, SIDE, SIDE),
-        )
-        + (jax.ShapeDtypeStruct((corners,), jnp.int32),),
-        in_specs=anywhere(11),
-        out_specs=tuple(in_vmem(6)) + (pl.BlockSpec(memory_space=pltpu.SMEM),),
+        out_shape=shapes_of(*outs, (corners, SIDE, SIDE))
+        + (jax.ShapeDtypeStruct((corners + 1,), jnp.int32),),
+        in_specs=in_hbm(11),
+        out_specs=tuple(in_hbm(6)) + (pl.BlockSpec(memory_space=pltpu.SMEM),),
         scratch_shapes=[
             pltpu.VMEM((sources, CAP * SIDE, SIDE), jnp.float32),
             pltpu.SMEM((sources, SIDE), jnp.float32),
@@ -585,13 +689,15 @@
             pltpu.VMEM(field, jnp.float32),
             pltpu.VMEM(field, jnp.float32),
             extended_shape(tile, 2),
+            pltpu.VMEM((corners + 1, SIDE, SIDE), jnp.float32),
             pltpu.VMEM((comps, SIDE, cols), jnp.float32),
             pltpu.VMEM((comps, SIDE, cols), jnp.float32),
             pltpu.VMEM((comps, rows, SIDE), jnp.float32),
             pltpu.VMEM((comps, rows, SIDE), jnp.float32),
-            pltpu.SemaphoreType.DMA((12,)),
-        ],
-        compiler_params=pltpu.CompilerParams(vmem_limit_bytes=VMEM_MOST),
+        ]
+        + [pltpu.VMEM(shape, jnp.float32) for shape in outs]
+        + [pltpu.SemaphoreType.DMA((CHUNKS + 11,)), pltpu.SemaphoreType.DMA((21,))],
+        compiler_params=pltpu.CompilerParams(vmem_limit_bytes=VMEM_LIMIT),
         cost_estimate=stage_cost(len(places)),
         name="backward_rim",
     )(recv, tile, below, right, diag, probe, tables, *fields_last, *fields_side)
@@ -602,11 +708,22 @@
     return pl.pallas_call(
         functools.partial(backward_inner_kernel, places),
         out_shape=jax.ShapeDtypeStruct(tile.shape, jnp.float32),
-        in_specs=[pl.BlockSpec(memory_space=pltpu.SMEM)] + in_vmem(8),
-        out_specs=pl.BlockSpec(memory_space=pltpu.VMEM),
+        in_specs=[pl.BlockSpec(memory_space=pltpu.SMEM)] + in_hbm(8),
+        out_specs=in_hbm(1)[0],
         scratch_shapes=[
+            pltpu.VMEM(sums.shape, jnp.float32),
+            pltpu.VMEM((2, rows, cols), jnp.float32),
+            pltpu.VMEM(probe.shape, jnp.float32),
+            pltpu.VMEM(tables.shape, tables.dtype),
+            pltpu.VMEM(far.shape, jnp.float32),
+            pltpu.VMEM(enter.shape, jnp.float32),
+            pltpu.VMEM(row.shape, jnp.float32),
+            pltpu.VMEM(col.shape, jnp.float32),
+            pltpu.VMEM(tile.shape, jnp.float32),
             pltpu.VMEM((comps, rows, cols - SIDE), jnp.float32),
             pltpu.VMEM((comps, rows, cols - SIDE), jnp.float32),
+            pltpu.SemaphoreType.DMA((2 * (rows // BLOCK - 1) + 6,)),
+            pltpu.SemaphoreType.DMA((comps,)),
         ],
         compiler_params=pltpu.CompilerParams(vmem_limit_bytes=VMEM_LIMIT),
         cost_estimate=stage_cost(len(places)),
@@ -631,17 +748,22 @@
         ],
         sems,
     )
-    wait_copies(loads)
-    left = col_buf[...]
-    low = low_lanes(left.shape)
-    upper = jnp.where(low, left, 0.0)
-    lower = pltpu.roll(jnp.where(low, 0.0, left), BLOCK, 2)
+    def unpacked(packed):
+        low = low_lanes(packed.shape)
+        upper = jnp.where(low, packed, 0.0)
+        return upper, pltpu.roll(jnp.where(low, 0.0, packed), BLOCK, 2)
+
+    wait_copies(loads[:2])
     top_ref[...] = top_ref[...] + row_buf[...]
-    top_ref[:, :, :SIDE] = top_ref[:, :, :SIDE] + upper[:, :BLOCK] + diag_buf[...]
-    stores = start_copies([(top_ref, top)], sems)
+    wait_copies(loads[2:4])
+    upper, lower = unpacked(col_buf[...])
+    corner = jnp.concatenate(unpacked(diag_buf[...]), axis=1)
+    top_ref[:, :, :SIDE] = top_ref[:, :, :SIDE] + upper[:, :BLOCK] + corner
+    stores = start_copies([(top_ref, top)], sems.at[pl.ds(5, 1)])
+    wait_copies(loads[4:])
     side_ref[:, : half - BLOCK] = side_ref[:, : half - BLOCK] + upper[:, BLOCK:]
     side_ref[:, half - BLOCK :] = side_ref[:, half - BLOCK :] + lower
-    stores += start_copies([(side_ref, side)], sems.at[pl.ds(1, 1)])
+    stores += start_copies([(side_ref, side)], sems.at[pl.ds(6, 1)])
     wait_copies(stores)
 
 
@@ -658,7 +780,7 @@
             pltpu.VMEM(above.shape, jnp.float32),
             pltpu.VMEM(left.shape, jnp.float32),
             pltpu.VMEM(diag.shape, jnp.float32),
-            pltpu.SemaphoreType.DMA((5,)),
+            pltpu.SemaphoreType.DMA((7,)),
         ],
         input_output_aliases={0: 0},
         compiler_params=pltpu.CompilerParams(vmem_limit_bytes=VMEM_LIMIT),
@@ -666,21 +788,47 @@
     )(own, above, left, diag)
 
 
-def strip_kernel(tile_ref, below_ref, sems):
-    wait_copies(start_copies([(tile_ref.at[:, pl.ds(0, BLOCK)], below_ref)], sems))
+def row_strip_kernel(tile_ref, row_ref, corner_ref, sems):
+    top = pl.ds(0, BLOCK)
+    wait_copies(
+        start_copies(
+            [
+                (tile_ref.at[:, top], row_ref),
+                (tile_ref.at[:, top, pl.ds(0, SIDE)], corner_ref),
+            ],
+            sems,
+        )
+    )
 
 
 def row_strip(tile):
     comps, rows, cols = tile.shape
     return pl.pallas_call(
-        strip_kernel,
-        out_shape=jax.ShapeDtypeStruct((comps, BLOCK, cols), jnp.float32),
-        in_specs=anywhere(1),
+        row_strip_kernel,
+        out_shape=shapes_of((comps, BLOCK, cols), (comps, BLOCK, SIDE)),
+        in_specs=in_hbm(1),
+        out_specs=tuple(in_vmem(2)),
+        scratch_shapes=[pltpu.SemaphoreType.DMA((2,))],
+        compiler_params=pltpu.CompilerParams(vmem_limit_bytes=VMEM_LIMIT),
+        name="row_strip",
+    )(tile)
+
+
+def column_strip_kernel(tile_ref, send_ref, out_ref, sems):
+    wait_copies(start_copies([(tile_ref.at[:, :, pl.ds(0, SIDE)], out_ref)], sems))
+
+
+def column_strip(tile, send):
+    comps, rows, cols = tile.shape
+    return pl.pallas_call(
+        column_strip_kernel,
+        out_shape=jax.ShapeDtypeStruct((comps, rows, SIDE), jnp.float32),
+        in_specs=in_hbm(2),
         out_specs=pl.BlockSpec(memory_space=pltpu.VMEM),
         scratch_shapes=[pltpu.SemaphoreType.DMA((1,))],
-        compiler_params=pltpu.CompilerParams(vmem_limit_bytes=VMEM_MOST),
-        name="row_strip",
-    )(tile)
+        compiler_params=pltpu.CompilerParams(vmem_limit_bytes=VMEM_LIMIT),
+        name="column_strip",
+    )(tile, send)
 
 
 def moved(shard, down, across):
@@ -706,11 +854,12 @@
     tile = object_slices.reshape(slices * parts, tile_rows, tile_cols)
     row_total = lax.axis_size("row")
     tables = jnp.asarray(TABLES)
-    below = moved(row_strip(tile), -1, 0)
-    send, strip_right, strip_diag = pack(offsets, measured, tile, row_total)
-    right = moved(strip_right, 0, -1)
+    strip_below, strip_diag = row_strip(tile)
+    below = moved(strip_below, -1, 0)
     diag = moved(strip_diag, -1, -1)
+    send = pack(offsets, measured, row_total)
     recv = lax.all_to_all(send, "row", split_axis=0, concat_axis=0, tiled=True)
+    right = moved(column_strip(tile, send), 0, -1)
     last, side, inner = pair_places(tile_rows, tile_cols)
     far_inner, enter_inner = forward_inner(inner, tile, probe, tables)
     far_inner, enter_inner, right = lax.optimization_barrier((far_inner, enter_inner, right))
@@ -718,6 +867,7 @@
         last, side, tile, below, right, diag, probe, tables
     )
     row, col, to_below, to_right, to_diag, sums, count = backward_rim(
+        last + side,
         recv,
         tile,
         below,
@@ -727,7 +877,6 @@
         tables,
         (far_last, enter_last),
         (far_side, enter_side),
-        last + side,
     )
     above = moved(to_below, 1, 0)
     left = moved(to_right, 0, 1)

time: 92.9 us -> 82.3 us (0.89)
  the two profiles are of different devices: /device:TPU:33 before, /device:TPU:17 now
where the time goes in v5:
time: 82.3 us; the launch traced here: 81.9 us
  Pallas kernels  41.1 us (50%)
  starting transfers between devices  30.2 us (37%)
  waiting for transfers between devices  10.3 us (13%)
    all_to_all x1, starting transfers between devices, body(): recv = lax.all_to_all(send, 'row', split_axis=0, concat_axis=0, tiled=True)  10.9 us
    ppermute x2, starting transfers between devices, moved(): return lax.ppermute(shard, ('row', 'col'), pairs)  9.13 us
    pallas_call x1, Pallas kernels, backward_inner(): pl.pallas_call(functools.partial(backward_inner_kernel, places), out_shap...  9.12 us
    all_to_all x1, waiting for transfers between devices, body(): recv = lax.all_to_all(send, 'row', split_axis=0, concat_axis=0, tiled=True)  8.92 us
    pallas_call x1, Pallas kernels, backward_rim(): pl.pallas_call(functools.partial(backward_rim_kernel, places), out_shape=...  8.33 us
    pallas_call x1, Pallas kernels, forward_inner(): pl.pallas_call(functools.partial(forward_inner_kernel, places), out_shape...  7.53 us
    pallas_call x1, Pallas kernels, forward_rim(): pl.pallas_call(functools.partial(forward_rim_kernel, places), out_shape=f...  7.51 us
    ppermute x2, starting transfers between devices, moved(): return lax.ppermute(shard, 'row', pairs)  5.88 us
  transfers between devices with their start and end apart: 7, of which 2 were waited for; matrix products, arithmetic and copies ran while one was open for 0% of the time, Pallas kernels for 35%

profile of v5, /device:TPU:17, one launch (start us, length us, event | category | flops | bytes accessed | tf_op | source)
XLA Modules:
  0.0 81.9 jit_solution(7737751480676662115)
XLA Ops:
  0.0 1.9 %row_strip.1 = (f32[4,64,512]{2,1,0:T(8,128)}, f32[4,64,128]{2,1,0:T(8,128)}) custom-call(f32[4,256,512]{2,1,0:T(8,128)} %bitcast.2), custom_call_target="tpu_custom_call" | custom-call | tf_op jit(solution)/shard_map/row_strip/pallas_call | solution.py:806
  1.9 1.3 %collective-permute-start.2 = (f32[4,64,128]{2,1,0:T(8,128)}, f32[4,64,128]{2,1,0:T(8,128)}, u32[]{:S(2)}, u32[]{:S(2)}) collective-permute-start(f32[4,64,128]{2,1,0:T(8,128)} %get-tuple-element.27), channel_id=1, source_target_pairs={{9,0},{10,1},{11,2},{12,3},{13,4},{14,5},{15,6},{17,8},{18,9},{19,... | collective-permute-start | bytes 393224 | tf_op jit(solution)/shard_map/ppermute | solution.py:849
  3.2 1.3 %collective-permute-start = (f32[4,64,512]{2,1,0:T(8,128)}, f32[4,64,512]{2,1,0:T(8,128)}, u32[]{:S(2)}, u32[]{:S(2)}) collective-permute-start(f32[4,64,512]{2,1,0:T(8,128)} %get-tuple-element.23), channel_id=1, source_target_pairs={{8,0},{16,8},{24,16},{32,24},{40,32},{48,40},{56,48},{64,56},{72,6... | collective-permute-start | bytes 1572872 | tf_op jit(solution)/shard_map/ppermute | solution.py:839
  4.5 2.4 %pack_measured.1.send_ref = f32[16,264,128]{2,1,0:T(8,128)} custom-call(s32[2,16]{1,0:T(2,128)} %off_ref.1, f32[16,128,128]{2,1,0:T(8,128)} %meas_ref.1), custom_call_target="tpu_custom_call" | custom-call | bytes 41943040 | tf_op jit(solution)/shard_map/pack_measured/pallas_call | solution.py:145
  7.0 10.9 %all-to-all-start = ((f32[16,264,128]{2,1,0:T(8,128)}), f32[16,264,128]{2,1,0:T(8,128)}, u32[]{:S(2)}, u32[]{:S(2)}) async-start(f32[16,264,128]{2,1,0:T(8,128)} %pack_measured.1.send_ref), calls=%async_computation | async-start | bytes 4325376 | tf_op jit(solution)/shard_map/all_to_all | solution.py:861
  17.9 1.9 %column_strip.1 = f32[4,256,128]{2,1,0:T(8,128)} custom-call(f32[4,256,512]{2,1,0:T(8,128)} %bitcast.3, f32[16,264,128]{2,1,0:T(8,128)} %pack_measured.1.send_ref), custom_call_target="tpu_custom_call" | custom-call | tf_op jit(solution)/shard_map/column_strip/pallas_call | solution.py:823
  19.7 2.2 %collective-permute-start.1 = (f32[4,256,128]{2,1,0:T(8,128)}, f32[4,256,128]{2,1,0:T(8,128)}, u32[]{:S(2)}, u32[]{:S(2)}) collective-permute-start(f32[4,256,128]{2,1,0:T(8,128)} %column_strip.1), channel_id=1, source_target_pairs={{1,0},{2,1},{3,2},{4,3},{5,4},{6,5},{7,6},{9,8},{10,9},{11,10},{12... | collective-permute-start | bytes 1572872 | tf_op jit(solution)/shard_map/ppermute | solution.py:842
  21.9 7.5 %forward_inner.1 = (f32[9,256,256]{2,1,0:T(8,128)}, f32[9,256,256]{2,1,0:T(8,128)}) custom-call(f32[4,256,512]{2,1,0:T(8,128)} %bitcast.4, f32[2,128,128]{2,1,0:T(8,128)} %probe_ref.7, bf16[8,256,256]{2,1,0:T(8,128)(2,1)} %constant.2.clone.tables.tables_ref), custom_call_target="tpu_custom_call" | custom-call | flops 28991029248 | bytes 1048576 | tf_op jit(solution)/shard_map/forward_inner/pallas_call | solution.py:283
  29.5 1.4 %collective-permute-done.1.right_ref = f32[4,256,128]{2,1,0:T(8,128)} collective-permute-done((f32[4,256,128]{2,1,0:T(8,128)}, f32[4,256,128]{2,1,0:T(8,128)}, u32[]{:S(2)}, u32[]{:S(2)}) %collective-permute-start.1) | collective-permute-done | bytes 524320 | tf_op jit(solution)/shard_map/ppermute | solution.py:842
  30.8 0.0 collective-permute-done.2.diag_ref
  30.8 0.0 collective-permute-done.below_ref
  30.8 7.5 %forward_rim.1 = (f32[4,256,256]{2,1,0:T(8,128)}, f32[4,256,256]{2,1,0:T(8,128)}, f32[3,256,256]{2,1,0:T(8,128)}, f32[3,256,256]{2,1,0:T(8,128)}) custom-call(f32[4,256,512]{2,1,0:T(8,128)} %bitcast.5, f32[4,64,512]{2,1,0:T(8,128)} %collective-permute-done.below_ref, f32[4,256,128]{2,1,0:T(8,128)} %collective-permute-done.1.right_ref, ...), custom_call_target="tpu_custom_call" | custom-call | flops 22548578304 | bytes 1048576 | tf_op jit(solution)/shard_map/forward_rim/pallas_call | solution.py:300
  38.4 8.9 %all-to-all-done.recv_ref = f32[16,264,128]{2,1,0:T(8,128)} async-done(((f32[16,264,128]{2,1,0:T(8,128)}), f32[16,264,128]{2,1,0:T(8,128)}, u32[]{:S(2)}, u32[]{:S(2)}) %all-to-all-start) | async-done | bytes 2162720 | tf_op jit(solution)/shard_map/all_to_all | solution.py:861
  47.3 8.3 %backward_rim.1 = (f32[4,64,512]{2,1,0:T(8,128)}, f32[4,256,128]{2,1,0:T(8,128)}, f32[4,64,512]{2,1,0:T(8,128)}, f32[4,128,128]{2,1,0:T(8,128)}, f32[4,32,128]{2...) custom-call(f32[16,264,128]{2,1,0:T(8,128)} %all-to-all-done.recv_ref, f32[4,256,512]{2,1,0:T(8,128)} %bitcast.6, ...), custom_call_target="tpu_custom_call" | custom-call | flops 2818572288 | bytes 1048576 | tf_op jit(solution)/shard_map/backward_rim/pallas_call | solution.py:678
  55.6 4.6 %collective-permute-start.3 = (f32[4,64,512]{2,1,0:T(8,128)}, f32[4,64,512]{2,1,0:T(8,128)}, u32[]{:S(2)}, u32[]{:S(2)}) collective-permute-start(f32[4,64,512]{2,1,0:T(8,128)} %get-tuple-element.38), channel_id=1, source_target_pairs={{0,8},{8,16},{16,24},{24,32},{32,40},{40,48},{48,56},{56,64},{64,7... | collective-permute-start | bytes 1572872 | tf_op jit(solution)/shard_map/ppermute | solution.py:839
  60.2 7.8 %collective-permute-start.5 = (f32[4,32,128]{2,1,0:T(8,128)}, f32[4,32,128]{2,1,0:T(8,128)}, u32[]{:S(2)}, u32[]{:S(2)}) collective-permute-start(f32[4,32,128]{2,1,0:T(8,128)} %get-tuple-element.40), channel_id=1, source_target_pairs={{0,9},{1,10},{2,11},{3,12},{4,13},{5,14},{6,15},{8,17},{9,18},{10,... | collective-permute-start | bytes 196616 | tf_op jit(solution)/shard_map/ppermute | solution.py:849
  68.1 2.1 %collective-permute-start.4 = (f32[4,128,128]{2,1,0:T(8,128)}, f32[4,128,128]{2,1,0:T(8,128)}, u32[]{:S(2)}, u32[]{:S(2)}) collective-permute-start(f32[4,128,128]{2,1,0:T(8,128)} %get-tuple-element.39), channel_id=1, source_target_pairs={{0,1},{1,2},{2,3},{3,4},{4,5},{5,6},{6,7},{8,9},{9,10},{10,11},{11... | collective-permute-start | bytes 786440 | tf_op jit(solution)/shard_map/ppermute | solution.py:842
  70.2 9.1 %backward_inner.1.own_ref = f32[4,256,512]{2,1,0:T(8,128)} custom-call(s32[33]{0:T(128)} %get-tuple-element.32.count_ref, f32[32,128,128]{2,1,0:T(8,128)} %get-tuple-element.33.sum_ref, f32[4,256,512]{2,1,0:T(8,128)} %bitcast.7, f32[2,128,128]{2,1,0:T(8,128)} %probe_ref.7, bf16[8,256,256]{2,1,0:T(8,128)(2,1)} %constant.2.clone.tables.tables_ref, ...), custom_call_target="tpu_custom_call" | custom-call | flops 3623878656 | bytes 1048576 | tf_op jit(solution)/shard_map/backward_inner/pallas_call | solution.py:708
  79.3 0.0 collective-permute-done.5.diag_ref
  79.3 0.0 collective-permute-done.4.left_ref
  79.3 0.0 collective-permute-done.3.above_ref
  79.3 2.4 %add_borders.1 = f32[4,256,512]{2,1,0:T(8,128)} custom-call(f32[4,256,512]{2,1,0:T(8,128)} %backward_inner.1.own_ref, f32[4,64,512]{2,1,0:T(8,128)} %collective-permute-done.3.above_ref, f32[4,128,128]{2,1,0:T(8,128)} %collective-permute-done.4.left_ref, f32[4,32,128]{2,1,0:T(8,128)} %collective-permute-done.5.diag_ref), custom_call_target="tpu_custom_call", output_to_operand_aliasing={{}: (0, {})} | custom-call | tf_op jit(solution)/shard_map/add_borders/pallas_call | solution.py:772
Async XLA Ops:
  1.9 28.9 %collective-permute-start.2 = (f32[4,64,128]{2,1,0:T(8,128)}, f32[4,64,128]{2,1,0:T(8,128)}, u32[]{:S(2)}, u32[]{:S(2)}) collective-permute-start(f32[4,64,128]{2,1,0:T(8,128)} %get-tuple-element.27), channel_id=1, source_target_pairs={{9,0},{10,1},{11,2},{12,3},{13,4},{14,5},{15,6},{17,8},{18,9},{19,... | collective-permute-start | bytes 393224 | tf_op jit(solution)/shard_map/ppermute | solution.py:849
  3.2 27.6 %collective-permute-start = (f32[4,64,512]{2,1,0:T(8,128)}, f32[4,64,512]{2,1,0:T(8,128)}, u32[]{:S(2)}, u32[]{:S(2)}) collective-permute-start(f32[4,64,512]{2,1,0:T(8,128)} %get-tuple-element.23), channel_id=1, source_target_pairs={{8,0},{16,8},{24,16},{32,24},{40,32},{48,40},{56,48},{64,56},{72,6... | collective-permute-start | bytes 1572872 | tf_op jit(solution)/shard_map/ppermute | solution.py:839
  7.0 40.3 %all-to-all-start = ((f32[16,264,128]{2,1,0:T(8,128)}), f32[16,264,128]{2,1,0:T(8,128)}, u32[]{:S(2)}, u32[]{:S(2)}) async-start(f32[16,264,128]{2,1,0:T(8,128)} %pack_measured.1.send_ref), calls=%async_computation | async-start | bytes 4325376 | tf_op jit(solution)/shard_map/all_to_all | solution.py:861
  19.7 11.1 %collective-permute-start.1 = (f32[4,256,128]{2,1,0:T(8,128)}, f32[4,256,128]{2,1,0:T(8,128)}, u32[]{:S(2)}, u32[]{:S(2)}) collective-permute-start(f32[4,256,128]{2,1,0:T(8,128)} %column_strip.1), channel_id=1, source_target_pairs={{1,0},{2,1},{3,2},{4,3},{5,4},{6,5},{7,6},{9,8},{10,9},{11,10},{12... | collective-permute-start | bytes 1572872 | tf_op jit(solution)/shard_map/ppermute | solution.py:842
  55.6 23.7 %collective-permute-start.3 = (f32[4,64,512]{2,1,0:T(8,128)}, f32[4,64,512]{2,1,0:T(8,128)}, u32[]{:S(2)}, u32[]{:S(2)}) collective-permute-start(f32[4,64,512]{2,1,0:T(8,128)} %get-tuple-element.38), channel_id=1, source_target_pairs={{0,8},{8,16},{16,24},{24,32},{32,40},{40,48},{48,56},{56,64},{64,7... | collective-permute-start | bytes 1572872 | tf_op jit(solution)/shard_map/ppermute | solution.py:839
  60.2 19.1 %collective-permute-start.5 = (f32[4,32,128]{2,1,0:T(8,128)}, f32[4,32,128]{2,1,0:T(8,128)}, u32[]{:S(2)}, u32[]{:S(2)}) collective-permute-start(f32[4,32,128]{2,1,0:T(8,128)} %get-tuple-element.40), channel_id=1, source_target_pairs={{0,9},{1,10},{2,11},{3,12},{4,13},{5,14},{6,15},{8,17},{9,18},{10,... | collective-permute-start | bytes 196616 | tf_op jit(solution)/shard_map/ppermute | solution.py:849
  68.1 11.2 %collective-permute-start.4 = (f32[4,128,128]{2,1,0:T(8,128)}, f32[4,128,128]{2,1,0:T(8,128)}, u32[]{:S(2)}, u32[]{:S(2)}) collective-permute-start(f32[4,128,128]{2,1,0:T(8,128)} %get-tuple-element.39), channel_id=1, source_target_pairs={{0,1},{1,2},{2,3},{3,4},{4,5},{5,6},{6,7},{8,9},{9,10},{10,11},{11... | collective-permute-start | bytes 786440 | tf_op jit(solution)/shard_map/ppermute | solution.py:842

commit v6 on v5

--- a/solution.py
+++ b/solution.py
@@ -219,7 +219,25 @@
     forward_pairs(places, tile_ref, probe_ref, tables, each(far_ref), each(enter_ref))
 
 
-def forward_rim_kernel(
+def forward_side_kernel(
+    places, tile_ref, right_ref, probe_ref, tables, far_ref, enter_ref, ext_ref, sems
+):
+    cols = tile_ref.shape[2]
+    wait_copies(
+        start_copies(
+            [
+                (tile_ref.at[:, :, pl.ds(cols - SIDE, SIDE)], ext_ref.at[:, :, pl.ds(0, SIDE)]),
+                (right_ref, ext_ref.at[:, :, pl.ds(SIDE, SIDE)]),
+            ],
+            sems,
+        )
+    )
+    forward_pairs(
+        [(row, 0) for row, _ in places], ext_ref, probe_ref, tables, each(far_ref), each(enter_ref)
+    )
+
+
+def forward_last_kernel(
     places,
     tile_ref,
     below_ref,
@@ -227,32 +245,28 @@
     diag_ref,
     probe_ref,
     tables,
-    far_last_ref,
-    enter_last_ref,
-    far_side_ref,
-    enter_side_ref,
+    far_ref,
+    enter_ref,
     ext_ref,
     sems,
 ):
     rows, cols = tile_ref.shape[1:]
+    low = pl.ds(rows - BLOCK, BLOCK)
+    upper, lower = pl.ds(0, BLOCK), pl.ds(BLOCK, BLOCK)
+    wide, beyond = pl.ds(0, cols), pl.ds(cols, SIDE)
     wait_copies(
         start_copies(
             [
-                (tile_ref, ext_ref.at[:, pl.ds(0, rows), pl.ds(0, cols)]),
-                (below_ref, ext_ref.at[:, pl.ds(rows, BLOCK), pl.ds(0, cols)]),
-                (right_ref, ext_ref.at[:, pl.ds(0, rows), pl.ds(cols, SIDE)]),
-                (diag_ref, ext_ref.at[:, pl.ds(rows, BLOCK), pl.ds(cols, SIDE)]),
+                (tile_ref.at[:, low], ext_ref.at[:, upper, wide]),
+                (below_ref, ext_ref.at[:, lower, wide]),
+                (right_ref.at[:, low], ext_ref.at[:, upper, beyond]),
+                (diag_ref, ext_ref.at[:, lower, beyond]),
             ],
             sems,
         )
     )
     forward_pairs(
-        places,
-        ext_ref,
-        probe_ref,
-        tables,
-        each(far_last_ref) + each(far_side_ref),
-        each(enter_last_ref) + each(enter_side_ref),
+        [(0, col) for _, col in places], ext_ref, probe_ref, tables, each(far_ref), each(enter_ref)
     )
 
 
@@ -295,17 +309,37 @@
     return pltpu.VMEM((comps, tile.shape[1] + BLOCK, tile.shape[2] + SIDE), jnp.float32)
 
 
-def forward_rim(last, side, tile, below, right, diag, probe, tables):
-    places = last + side
+def forward_side(places, tile, right, probe, tables):
+    comps, rows, _ = tile.shape
     return pl.pallas_call(
-        functools.partial(forward_rim_kernel, places),
-        out_shape=fields(last) + fields(side),
-        in_specs=in_hbm(4) + in_vmem(2),
-        out_specs=tuple(in_vmem(4)),
-        scratch_shapes=[extended_shape(tile, tile.shape[0]), pltpu.SemaphoreType.DMA((4,))],
+        functools.partial(forward_side_kernel, places),
+        out_shape=fields(places),
+        in_specs=in_hbm(2) + in_vmem(2),
+        out_specs=tuple(in_vmem(2)),
+        scratch_shapes=[
+            pltpu.VMEM((comps, rows, 2 * SIDE), jnp.float32),
+            pltpu.SemaphoreType.DMA((2,)),
+        ],
         compiler_params=pltpu.CompilerParams(vmem_limit_bytes=VMEM_LIMIT),
         cost_estimate=stage_cost(8 * len(places)),
-        name="forward_rim",
+        name="forward_last_column",
+    )(tile, right, probe, tables)
+
+
+def forward_last(places, tile, below, right, diag, probe, tables):
+    comps, _, cols = tile.shape
+    return pl.pallas_call(
+        functools.partial(forward_last_kernel, places),
+        out_shape=fields(places),
+        in_specs=in_hbm(4) + in_vmem(2),
+        out_specs=tuple(in_vmem(2)),
+        scratch_shapes=[
+            pltpu.VMEM((comps, SIDE, cols + SIDE), jnp.float32),
+            pltpu.SemaphoreType.DMA((4,)),
+        ],
+        compiler_params=pltpu.CompilerParams(vmem_limit_bytes=VMEM_LIMIT),
+        cost_estimate=stage_cost(8 * len(places)),
+        name="forward_last_row",
     )(tile, below, right, diag, probe, tables)
 
 
@@ -788,27 +822,18 @@
     )(own, above, left, diag)
 
 
-def row_strip_kernel(tile_ref, row_ref, corner_ref, sems):
-    top = pl.ds(0, BLOCK)
-    wait_copies(
-        start_copies(
-            [
-                (tile_ref.at[:, top], row_ref),
-                (tile_ref.at[:, top, pl.ds(0, SIDE)], corner_ref),
-            ],
-            sems,
-        )
-    )
+def row_strip_kernel(tile_ref, row_ref, sems):
+    wait_copies(start_copies([(tile_ref.at[:, pl.ds(0, BLOCK)], row_ref)], sems))
 
 
 def row_strip(tile):
     comps, rows, cols = tile.shape
     return pl.pallas_call(
         row_strip_kernel,
-        out_shape=shapes_of((comps, BLOCK, cols), (comps, BLOCK, SIDE)),
+        out_shape=jax.ShapeDtypeStruct((comps, BLOCK, cols), jnp.float32),
         in_specs=in_hbm(1),
-        out_specs=tuple(in_vmem(2)),
-        scratch_shapes=[pltpu.SemaphoreType.DMA((2,))],
+        out_specs=in_vmem(1)[0],
+        scratch_shapes=[pltpu.SemaphoreType.DMA((1,))],
         compiler_params=pltpu.CompilerParams(vmem_limit_bytes=VMEM_LIMIT),
         name="row_strip",
     )(tile)
@@ -854,18 +879,17 @@
     tile = object_slices.reshape(slices * parts, tile_rows, tile_cols)
     row_total = lax.axis_size("row")
     tables = jnp.asarray(TABLES)
-    strip_below, strip_diag = row_strip(tile)
-    below = moved(strip_below, -1, 0)
-    diag = moved(strip_diag, -1, -1)
+    below = moved(row_strip(tile), -1, 0)
     send = pack(offsets, measured, row_total)
     recv = lax.all_to_all(send, "row", split_axis=0, concat_axis=0, tiled=True)
     right = moved(column_strip(tile, send), 0, -1)
     last, side, inner = pair_places(tile_rows, tile_cols)
     far_inner, enter_inner = forward_inner(inner, tile, probe, tables)
-    far_inner, enter_inner, right = lax.optimization_barrier((far_inner, enter_inner, right))
-    far_last, enter_last, far_side, enter_side = forward_rim(
-        last, side, tile, below, right, diag, probe, tables
-    )
+    below, right, far_inner = lax.optimization_barrier((below, right, far_inner))
+    diag = moved(below[:, :, :SIDE], 0, -1)
+    far_side, enter_side = forward_side(side, tile, right, probe, tables)
+    diag, far_side = lax.optimization_barrier((diag, far_side))
+    far_last, enter_last = forward_last(last, tile, below, right, diag, probe, tables)
     row, col, to_below, to_right, to_diag, sums, count = backward_rim(
         last + side,
         recv,

time: 82.3 us -> 80.2 us (0.974)
  the two profiles are of different devices: /device:TPU:17 before, /device:TPU:7 now
where the time goes in v6:
time: 80.2 us; the launch traced here: 79.4 us
  Pallas kernels  44.1 us (55%)
  starting transfers between devices  32.3 us (40%)
  local copies, waits for them, and re-layouts  1.57 us (2%)
  waiting for transfers between devices  1.18 us (1%)
    ppermute x2, starting transfers between devices, moved(): return lax.ppermute(shard, 'row', pairs)  16.8 us
    pallas_call x1, Pallas kernels, backward_inner(): pl.pallas_call(functools.partial(backward_inner_kernel, places), out_shap...  9.12 us
    pallas_call x1, Pallas kernels, backward_rim(): pl.pallas_call(functools.partial(backward_rim_kernel, places), out_shape=...  8.34 us
    ppermute x3, starting transfers between devices, moved(): return lax.ppermute(shard, 'col', pairs)  8.26 us
    pallas_call x1, Pallas kernels, forward_inner(): pl.pallas_call(functools.partial(forward_inner_kernel, places), out_shape...  7.53 us
    pallas_call x1, Pallas kernels, forward_last(): pl.pallas_call(functools.partial(forward_last_kernel, places), out_shape=...  5.54 us
    pallas_call x1, Pallas kernels, forward_side(): pl.pallas_call(functools.partial(forward_side_kernel, places), out_shape=...  5.04 us
    all_to_all x1, starting transfers between devices, body(): recv = lax.all_to_all(send, 'row', split_axis=0, concat_axis=0, tiled=True)  4.35 us
  transfers between devices with their start and end apart: 7, of which 1 were waited for; matrix products, arithmetic and copies ran while one was open for 2% of the time, Pallas kernels for 40%

profile of v6, /device:TPU:7, one launch (start us, length us, event | category | flops | bytes accessed | tf_op | source)
XLA Modules:
  0.0 79.4 jit_solution(102003187126509998)
XLA Ops:
  0.0 1.8 %row_strip.1 = f32[4,64,512]{2,1,0:T(8,128)} custom-call(f32[4,256,512]{2,1,0:T(8,128)} %bitcast.2), custom_call_target="tpu_custom_call" | custom-call | tf_op jit(solution)/shard_map/row_strip/pallas_call | solution.py:831
  1.8 5.9 %collective-permute-start = (f32[4,64,512]{2,1,0:T(8,128)}, f32[4,64,512]{2,1,0:T(8,128)}, u32[]{:S(2)}, u32[]{:S(2)}) collective-permute-start(f32[4,64,512]{2,1,0:T(8,128)} %row_strip.1), channel_id=1, source_target_pairs={{8,0},{16,8},{24,16},{32,24},{40,32},{48,40},{56,48},{64,56},{72,6... | collective-permute-start | bytes 1572872 | tf_op jit(solution)/shard_map/ppermute | solution.py:864
  7.8 2.4 %pack_measured.1.send_ref = f32[16,264,128]{2,1,0:T(8,128)} custom-call(s32[2,16]{1,0:T(2,128)} %off_ref.1, f32[16,128,128]{2,1,0:T(8,128)} %meas_ref.1), custom_call_target="tpu_custom_call" | custom-call | bytes 41943040 | tf_op jit(solution)/shard_map/pack_measured/pallas_call | solution.py:145
  10.2 4.4 %all-to-all-start = ((f32[16,264,128]{2,1,0:T(8,128)}), f32[16,264,128]{2,1,0:T(8,128)}, u32[]{:S(2)}, u32[]{:S(2)}) async-start(f32[16,264,128]{2,1,0:T(8,128)} %pack_measured.1.send_ref), calls=%async_computation | async-start | bytes 4325376 | tf_op jit(solution)/shard_map/all_to_all | solution.py:884
  14.6 1.9 %column_strip.1 = f32[4,256,128]{2,1,0:T(8,128)} custom-call(f32[4,256,512]{2,1,0:T(8,128)} %bitcast.3, f32[16,264,128]{2,1,0:T(8,128)} %pack_measured.1.send_ref), custom_call_target="tpu_custom_call" | custom-call | tf_op jit(solution)/shard_map/column_strip/pallas_call | solution.py:848
  16.4 3.4 %collective-permute-start.1 = (f32[4,256,128]{2,1,0:T(8,128)}, f32[4,256,128]{2,1,0:T(8,128)}, u32[]{:S(2)}, u32[]{:S(2)}) collective-permute-start(f32[4,256,128]{2,1,0:T(8,128)} %column_strip.1), channel_id=1, source_target_pairs={{1,0},{2,1},{3,2},{4,3},{5,4},{6,5},{7,6},{9,8},{10,9},{11,10},{12... | collective-permute-start | bytes 1572872 | tf_op jit(solution)/shard_map/ppermute | solution.py:867
  19.8 7.5 %forward_inner.1 = (f32[9,256,256]{2,1,0:T(8,128)}, f32[9,256,256]{2,1,0:T(8,128)}) custom-call(f32[4,256,512]{2,1,0:T(8,128)} %bitcast.4, f32[2,128,128]{2,1,0:T(8,128)} %probe_ref.9, bf16[8,256,256]{2,1,0:T(8,128)(2,1)} %constant.2.clone.tables.tables_ref), custom_call_target="tpu_custom_call" | custom-call | flops 28991029248 | bytes 1048576 | tf_op jit(solution)/shard_map/forward_inner/pallas_call | solution.py:297
  27.4 0.0 collective-permute-done.below_ref
  27.4 1.2 %collective-permute-done.1.right_ref = f32[4,256,128]{2,1,0:T(8,128)} collective-permute-done((f32[4,256,128]{2,1,0:T(8,128)}, f32[4,256,128]{2,1,0:T(8,128)}, u32[]{:S(2)}, u32[]{:S(2)}) %collective-permute-start.1) | collective-permute-done | bytes 524320 | tf_op jit(solution)/shard_map/ppermute | solution.py:867
  28.5 1.6 %slice.3 = f32[4,64,128]{2,1,0:T(8,128)} slice(f32[4,64,512]{2,1,0:T(8,128)} %collective-permute-done.below_ref), slice={[0:4], [0:64], [0:128]} | slice | bytes 262144 | tf_op jit(solution)/shard_map/slice | solution.py:889
  30.1 2.1 %collective-permute-start.2 = (f32[4,64,128]{2,1,0:T(8,128)}, f32[4,64,128]{2,1,0:T(8,128)}, u32[]{:S(2)}, u32[]{:S(2)}) collective-permute-start(f32[4,64,128]{2,1,0:T(8,128)} %slice.3), channel_id=1, source_target_pairs={{1,0},{2,1},{3,2},{4,3},{5,4},{6,5},{7,6},{9,8},{10,9},{11,10},{12... | collective-permute-start | bytes 393224 | tf_op jit(solution)/shard_map/ppermute | solution.py:867
  32.2 5.0 %forward_last_column.1 = (f32[3,256,256]{2,1,0:T(8,128)}, f32[3,256,256]{2,1,0:T(8,128)}) custom-call(f32[4,256,512]{2,1,0:T(8,128)} %bitcast.5, f32[4,256,128]{2,1,0:T(8,128)} %collective-permute-done.1.right_ref, f32[2,128,128]{2,1,0:T(8,128)} %probe_ref.9, bf16[8,256,256]{2,1,0:T(8,128)(2,1)} %constant.2.clone.tables.tables_ref), custom_call_target="tpu_custom_call" | custom-call | flops 9663676416 | bytes 1048576 | tf_op jit(solution)/shard_map/forward_last_column/pallas_call | solution.py:314
  37.2 0.0 collective-permute-done.2.diag_ref
  37.2 5.5 %forward_last_row.1 = (f32[4,256,256]{2,1,0:T(8,128)}, f32[4,256,256]{2,1,0:T(8,128)}) custom-call(f32[4,256,512]{2,1,0:T(8,128)} %bitcast.6, f32[4,64,512]{2,1,0:T(8,128)} %collective-permute-done.below_ref, f32[4,256,128]{2,1,0:T(8,128)} %collective-permute-done.1.right_ref, f32[4,64,128]{2,1,0:T(8,128)} %collective-permute-done.2.diag_ref, ...), custom_call_target="tpu_custom_call" | custom-call | flops 12884901888 | bytes 1048576 | tf_op jit(solution)/shard_map/forward_last_row/pallas_call | solution.py:331
  42.8 0.0 all-to-all-done.recv_ref
  42.8 8.3 %backward_rim.1 = (f32[4,64,512]{2,1,0:T(8,128)}, f32[4,256,128]{2,1,0:T(8,128)}, f32[4,64,512]{2,1,0:T(8,128)}, f32[4,128,128]{2,1,0:T(8,128)}, f32[4,32,128]{2...) custom-call(f32[16,264,128]{2,1,0:T(8,128)} %all-to-all-done.recv_ref, f32[4,256,512]{2,1,0:T(8,128)} %bitcast.7, ...), custom_call_target="tpu_custom_call" | custom-call | flops 2818572288 | bytes 1048576 | tf_op jit(solution)/shard_map/backward_rim/pallas_call | solution.py:712
  51.2 10.9 %collective-permute-start.3 = (f32[4,64,512]{2,1,0:T(8,128)}, f32[4,64,512]{2,1,0:T(8,128)}, u32[]{:S(2)}, u32[]{:S(2)}) collective-permute-start(f32[4,64,512]{2,1,0:T(8,128)} %get-tuple-element.38), channel_id=1, source_target_pairs={{0,8},{8,16},{16,24},{24,32},{32,40},{40,48},{48,56},{56,64},{64,7... | collective-permute-start | bytes 1572872 | tf_op jit(solution)/shard_map/ppermute | solution.py:864
  62.1 2.8 %collective-permute-start.5 = (f32[4,32,128]{2,1,0:T(8,128)}, f32[4,32,128]{2,1,0:T(8,128)}, u32[]{:S(2)}, u32[]{:S(2)}) collective-permute-start(f32[4,32,128]{2,1,0:T(8,128)} %get-tuple-element.40), channel_id=1, source_target_pairs={{0,9},{1,10},{2,11},{3,12},{4,13},{5,14},{6,15},{8,17},{9,18},{10,... | collective-permute-start | bytes 196616 | tf_op jit(solution)/shard_map/ppermute | solution.py:874
  64.9 2.8 %collective-permute-start.4 = (f32[4,128,128]{2,1,0:T(8,128)}, f32[4,128,128]{2,1,0:T(8,128)}, u32[]{:S(2)}, u32[]{:S(2)}) collective-permute-start(f32[4,128,128]{2,1,0:T(8,128)} %get-tuple-element.39), channel_id=1, source_target_pairs={{0,1},{1,2},{2,3},{3,4},{4,5},{5,6},{6,7},{8,9},{9,10},{10,11},{11... | collective-permute-start | bytes 786440 | tf_op jit(solution)/shard_map/ppermute | solution.py:867
  67.7 9.1 %backward_inner.1.own_ref = f32[4,256,512]{2,1,0:T(8,128)} custom-call(s32[33]{0:T(128)} %get-tuple-element.32.count_ref, f32[32,128,128]{2,1,0:T(8,128)} %get-tuple-element.33.sum_ref, f32[4,256,512]{2,1,0:T(8,128)} %bitcast.8, f32[2,128,128]{2,1,0:T(8,128)} %probe_ref.9, bf16[8,256,256]{2,1,0:T(8,128)(2,1)} %constant.2.clone.tables.tables_ref, ...), custom_call_target="tpu_custom_call" | custom-call | flops 3623878656 | bytes 1048576 | tf_op jit(solution)/shard_map/backward_inner/pallas_call | solution.py:742
  76.9 0.0 collective-permute-done.5.diag_ref
  76.9 0.0 collective-permute-done.4.left_ref
  76.9 0.0 collective-permute-done.3.above_ref
  76.9 2.4 %add_borders.1 = f32[4,256,512]{2,1,0:T(8,128)} custom-call(f32[4,256,512]{2,1,0:T(8,128)} %backward_inner.1.own_ref, f32[4,64,512]{2,1,0:T(8,128)} %collective-permute-done.3.above_ref, f32[4,128,128]{2,1,0:T(8,128)} %collective-permute-done.4.left_ref, f32[4,32,128]{2,1,0:T(8,128)} %collective-permute-done.5.diag_ref), custom_call_target="tpu_custom_call", output_to_operand_aliasing={{}: (0, {})} | custom-call | tf_op jit(solution)/shard_map/add_borders/pallas_call | solution.py:806
Async XLA Ops:
  1.8 25.5 %collective-permute-start = (f32[4,64,512]{2,1,0:T(8,128)}, f32[4,64,512]{2,1,0:T(8,128)}, u32[]{:S(2)}, u32[]{:S(2)}) collective-permute-start(f32[4,64,512]{2,1,0:T(8,128)} %row_strip.1), channel_id=1, source_target_pairs={{8,0},{16,8},{24,16},{32,24},{40,32},{48,40},{56,48},{64,56},{72,6... | collective-permute-start | bytes 1572872 | tf_op jit(solution)/shard_map/ppermute | solution.py:864
  10.2 32.6 %all-to-all-start = ((f32[16,264,128]{2,1,0:T(8,128)}), f32[16,264,128]{2,1,0:T(8,128)}, u32[]{:S(2)}, u32[]{:S(2)}) async-start(f32[16,264,128]{2,1,0:T(8,128)} %pack_measured.1.send_ref), calls=%async_computation | async-start | bytes 4325376 | tf_op jit(solution)/shard_map/all_to_all | solution.py:884
  16.4 12.1 %collective-permute-start.1 = (f32[4,256,128]{2,1,0:T(8,128)}, f32[4,256,128]{2,1,0:T(8,128)}, u32[]{:S(2)}, u32[]{:S(2)}) collective-permute-start(f32[4,256,128]{2,1,0:T(8,128)} %column_strip.1), channel_id=1, source_target_pairs={{1,0},{2,1},{3,2},{4,3},{5,4},{6,5},{7,6},{9,8},{10,9},{11,10},{12... | collective-permute-start | bytes 1572872 | tf_op jit(solution)/shard_map/ppermute | solution.py:867
  30.1 7.1 %collective-permute-start.2 = (f32[4,64,128]{2,1,0:T(8,128)}, f32[4,64,128]{2,1,0:T(8,128)}, u32[]{:S(2)}, u32[]{:S(2)}) collective-permute-start(f32[4,64,128]{2,1,0:T(8,128)} %slice.3), channel_id=1, source_target_pairs={{1,0},{2,1},{3,2},{4,3},{5,4},{6,5},{7,6},{9,8},{10,9},{11,10},{12... | collective-permute-start | bytes 393224 | tf_op jit(solution)/shard_map/ppermute | solution.py:867
  51.2 25.7 %collective-permute-start.3 = (f32[4,64,512]{2,1,0:T(8,128)}, f32[4,64,512]{2,1,0:T(8,128)}, u32[]{:S(2)}, u32[]{:S(2)}) collective-permute-start(f32[4,64,512]{2,1,0:T(8,128)} %get-tuple-element.38), channel_id=1, source_target_pairs={{0,8},{8,16},{16,24},{24,32},{32,40},{40,48},{48,56},{56,64},{64,7... | collective-permute-start | bytes 1572872 | tf_op jit(solution)/shard_map/ppermute | solution.py:864
  62.1 14.8 %collective-permute-start.5 = (f32[4,32,128]{2,1,0:T(8,128)}, f32[4,32,128]{2,1,0:T(8,128)}, u32[]{:S(2)}, u32[]{:S(2)}) collective-permute-start(f32[4,32,128]{2,1,0:T(8,128)} %get-tuple-element.40), channel_id=1, source_target_pairs={{0,9},{1,10},{2,11},{3,12},{4,13},{5,14},{6,15},{8,17},{9,18},{10,... | collective-permute-start | bytes 196616 | tf_op jit(solution)/shard_map/ppermute | solution.py:874
  64.9 11.9 %collective-permute-start.4 = (f32[4,128,128]{2,1,0:T(8,128)}, f32[4,128,128]{2,1,0:T(8,128)}, u32[]{:S(2)}, u32[]{:S(2)}) collective-permute-start(f32[4,128,128]{2,1,0:T(8,128)} %get-tuple-element.39), channel_id=1, source_target_pairs={{0,1},{1,2},{2,3},{3,4},{4,5},{5,6},{6,7},{8,9},{9,10},{10,11},{11... | collective-permute-start | bytes 786440 | tf_op jit(solution)/shard_map/ppermute | solution.py:867

commit v7 on v6

--- a/solution.py
+++ b/solution.py
@@ -885,10 +885,10 @@
     right = moved(column_strip(tile, send), 0, -1)
     last, side, inner = pair_places(tile_rows, tile_cols)
     far_inner, enter_inner = forward_inner(inner, tile, probe, tables)
-    below, right, far_inner = lax.optimization_barrier((below, right, far_inner))
+    right, far_inner = lax.optimization_barrier((right, far_inner))
+    far_side, enter_side = forward_side(side, tile, right, probe, tables)
+    below, far_side = lax.optimization_barrier((below, far_side))
     diag = moved(below[:, :, :SIDE], 0, -1)
-    far_side, enter_side = forward_side(side, tile, right, probe, tables)
-    diag, far_side = lax.optimization_barrier((diag, far_side))
     far_last, enter_last = forward_last(last, tile, below, right, diag, probe, tables)
     row, col, to_below, to_right, to_diag, sums, count = backward_rim(
         last + side,

time: 80.2 us -> 78.5 us (0.979)
  starting transfers between devices: 32.3 us -> 26.2 us
  waiting for transfers between devices: 1.18 us -> 5.7 us
    ppermute x2, starting transfers between devices: 16.8 us -> 11 us  [moved(): return lax.ppermute(shard, 'row', pairs)]
    ppermute x3, waiting for transfers between devices: 1.17 us -> 5.69 us  [moved(): return lax.ppermute(shard, 'col', pairs)]
    ppermute x1, starting transfers between devices: 2.84 us -> 1.92 us  [moved(): return lax.ppermute(shard, ('row', 'col'), pairs)]
  transfers between devices with their start and end apart: 7 -> 7, of which waited for: 1 -> 2; matrix products, arithmetic and copies ran while one was open for 2% -> 1% of each run, Pallas kernels for 40% -> 41%
where the time goes in v7:
time: 78.5 us; the launch traced here: 77.2 us
  Pallas kernels  44.1 us (56%)
  starting transfers between devices  26.2 us (33%)
  waiting for transfers between devices  5.7 us (7%)
  local copies, waits for them, and re-layouts  0.92 us (1%)
    ppermute x2, starting transfers between devices, moved(): return lax.ppermute(shard, 'row', pairs)  11 us
    pallas_call x1, Pallas kernels, backward_inner(): pl.pallas_call(functools.partial(backward_inner_kernel, places), out_shap...  9.11 us
    ppermute x3, starting transfers between devices, moved(): return lax.ppermute(shard, 'col', pairs)  8.97 us
    pallas_call x1, Pallas kernels, backward_rim(): pl.pallas_call(functools.partial(backward_rim_kernel, places), out_shape=...  8.34 us
    pallas_call x1, Pallas kernels, forward_inner(): pl.pallas_call(functools.partial(forward_inner_kernel, places), out_shape...  7.53 us
    ppermute x3, waiting for transfers between devices, moved(): return lax.ppermute(shard, 'col', pairs)  5.69 us
    pallas_call x1, Pallas kernels, forward_last(): pl.pallas_call(functools.partial(forward_last_kernel, places), out_shape=...  5.54 us
    pallas_call x1, Pallas kernels, forward_side(): pl.pallas_call(functools.partial(forward_side_kernel, places), out_shape=...  5.03 us
  transfers between devices with their start and end apart: 7, of which 2 were waited for; matrix products, arithmetic and copies ran while one was open for 1% of the time, Pallas kernels for 41%

profile of v7, /device:TPU:7, one launch (start us, length us, event | category | flops | bytes accessed | tf_op | source)
XLA Modules:
  0.0 77.2 jit_solution(14786473438758082294)
XLA Ops:
  0.0 1.8 %row_strip.1 = f32[4,64,512]{2,1,0:T(8,128)} custom-call(f32[4,256,512]{2,1,0:T(8,128)} %bitcast.2), custom_call_target="tpu_custom_call" | custom-call | tf_op jit(solution)/shard_map/row_strip/pallas_call | solution.py:831
  1.8 5.9 %collective-permute-start = (f32[4,64,512]{2,1,0:T(8,128)}, f32[4,64,512]{2,1,0:T(8,128)}, u32[]{:S(2)}, u32[]{:S(2)}) collective-permute-start(f32[4,64,512]{2,1,0:T(8,128)} %row_strip.1), channel_id=1, source_target_pairs={{8,0},{16,8},{24,16},{32,24},{40,32},{48,40},{56,48},{64,56},{72,6... | collective-permute-start | bytes 1572872 | tf_op jit(solution)/shard_map/ppermute | solution.py:864
  7.8 2.4 %pack_measured.1.send_ref = f32[16,264,128]{2,1,0:T(8,128)} custom-call(s32[2,16]{1,0:T(2,128)} %off_ref.1, f32[16,128,128]{2,1,0:T(8,128)} %meas_ref.1), custom_call_target="tpu_custom_call" | custom-call | bytes 41943040 | tf_op jit(solution)/shard_map/pack_measured/pallas_call | solution.py:145
  10.2 4.3 %all-to-all-start = ((f32[16,264,128]{2,1,0:T(8,128)}), f32[16,264,128]{2,1,0:T(8,128)}, u32[]{:S(2)}, u32[]{:S(2)}) async-start(f32[16,264,128]{2,1,0:T(8,128)} %pack_measured.1.send_ref), calls=%async_computation | async-start | bytes 4325376 | tf_op jit(solution)/shard_map/all_to_all | solution.py:884
  14.6 1.9 %column_strip.1 = f32[4,256,128]{2,1,0:T(8,128)} custom-call(f32[4,256,512]{2,1,0:T(8,128)} %bitcast.3, f32[16,264,128]{2,1,0:T(8,128)} %pack_measured.1.send_ref), custom_call_target="tpu_custom_call" | custom-call | tf_op jit(solution)/shard_map/column_strip/pallas_call | solution.py:848
  16.4 3.4 %collective-permute-start.1 = (f32[4,256,128]{2,1,0:T(8,128)}, f32[4,256,128]{2,1,0:T(8,128)}, u32[]{:S(2)}, u32[]{:S(2)}) collective-permute-start(f32[4,256,128]{2,1,0:T(8,128)} %column_strip.1), channel_id=1, source_target_pairs={{1,0},{2,1},{3,2},{4,3},{5,4},{6,5},{7,6},{9,8},{10,9},{11,10},{12... | collective-permute-start | bytes 1572872 | tf_op jit(solution)/shard_map/ppermute | solution.py:867
  19.8 7.5 %forward_inner.1 = (f32[9,256,256]{2,1,0:T(8,128)}, f32[9,256,256]{2,1,0:T(8,128)}) custom-call(f32[4,256,512]{2,1,0:T(8,128)} %bitcast.4, f32[2,128,128]{2,1,0:T(8,128)} %probe_ref.9, bf16[8,256,256]{2,1,0:T(8,128)(2,1)} %constant.2.clone.tables.tables_ref), custom_call_target="tpu_custom_call" | custom-call | flops 28991029248 | bytes 1048576 | tf_op jit(solution)/shard_map/forward_inner/pallas_call | solution.py:297
  27.4 1.1 %collective-permute-done.1.right_ref = f32[4,256,128]{2,1,0:T(8,128)} collective-permute-done((f32[4,256,128]{2,1,0:T(8,128)}, f32[4,256,128]{2,1,0:T(8,128)}, u32[]{:S(2)}, u32[]{:S(2)}) %collective-permute-start.1) | collective-permute-done | bytes 524320 | tf_op jit(solution)/shard_map/ppermute | solution.py:867
  28.5 5.0 %forward_last_column.1 = (f32[3,256,256]{2,1,0:T(8,128)}, f32[3,256,256]{2,1,0:T(8,128)}) custom-call(f32[4,256,512]{2,1,0:T(8,128)} %bitcast.5, f32[4,256,128]{2,1,0:T(8,128)} %collective-permute-done.1.right_ref, f32[2,128,128]{2,1,0:T(8,128)} %probe_ref.9, bf16[8,256,256]{2,1,0:T(8,128)(2,1)} %constant.2.clone.tables.tables_ref), custom_call_target="tpu_custom_call" | custom-call | flops 9663676416 | bytes 1048576 | tf_op jit(solution)/shard_map/forward_last_column/pallas_call | solution.py:314
  33.5 0.0 collective-permute-done.below_ref
  33.5 0.9 %slice.3 = f32[4,64,128]{2,1,0:T(8,128)S(1)} slice(f32[4,64,512]{2,1,0:T(8,128)} %collective-permute-done.below_ref), slice={[0:4], [0:64], [0:128]} | slice | bytes 262144 | tf_op jit(solution)/shard_map/slice | solution.py:891
  34.5 2.1 %collective-permute-start.2 = (f32[4,64,128]{2,1,0:T(8,128)S(1)}, f32[4,64,128]{2,1,0:T(8,128)}, u32[]{:S(2)}, u32[]{:S(2)}) collective-permute-start(f32[4,64,128]{2,1,0:T(8,128)S(1)} %slice.3), channel_id=1, source_target_pairs={{1,0},{2,1},{3,2},{4,3},{5,4},{6,5},{7,6},{9,8},{10,9},{11,10},{12... | collective-permute-start | bytes 393224 | tf_op jit(solution)/shard_map/ppermute | solution.py:867
  36.6 4.6 %collective-permute-done.2.diag_ref = f32[4,64,128]{2,1,0:T(8,128)} collective-permute-done((f32[4,64,128]{2,1,0:T(8,128)S(1)}, f32[4,64,128]{2,1,0:T(8,128)}, u32[]{:S(2)}, u32[]{:S(2)}) %collective-permute-start.2) | collective-permute-done | bytes 131104 | tf_op jit(solution)/shard_map/ppermute | solution.py:867
  41.1 5.5 %forward_last_row.1 = (f32[4,256,256]{2,1,0:T(8,128)}, f32[4,256,256]{2,1,0:T(8,128)}) custom-call(f32[4,256,512]{2,1,0:T(8,128)} %bitcast.6, f32[4,64,512]{2,1,0:T(8,128)} %collective-permute-done.below_ref, f32[4,256,128]{2,1,0:T(8,128)} %collective-permute-done.1.right_ref, f32[4,64,128]{2,1,0:T(8,128)} %collective-permute-done.2.diag_ref, ...), custom_call_target="tpu_custom_call" | custom-call | flops 12884901888 | bytes 1048576 | tf_op jit(solution)/shard_map/forward_last_row/pallas_call | solution.py:331
  46.7 0.0 all-to-all-done.recv_ref
  46.7 8.3 %backward_rim.1 = (f32[4,64,512]{2,1,0:T(8,128)}, f32[4,256,128]{2,1,0:T(8,128)}, f32[4,64,512]{2,1,0:T(8,128)}, f32[4,128,128]{2,1,0:T(8,128)}, f32[4,32,128]{2...) custom-call(f32[16,264,128]{2,1,0:T(8,128)} %all-to-all-done.recv_ref, f32[4,256,512]{2,1,0:T(8,128)} %bitcast.7, ...), custom_call_target="tpu_custom_call" | custom-call | flops 2818572288 | bytes 1048576 | tf_op jit(solution)/shard_map/backward_rim/pallas_call | solution.py:712
  55.1 5.1 %collective-permute-start.3 = (f32[4,64,512]{2,1,0:T(8,128)}, f32[4,64,512]{2,1,0:T(8,128)}, u32[]{:S(2)}, u32[]{:S(2)}) collective-permute-start(f32[4,64,512]{2,1,0:T(8,128)} %get-tuple-element.36), channel_id=1, source_target_pairs={{0,8},{8,16},{16,24},{24,32},{32,40},{40,48},{48,56},{56,64},{64,7... | collective-permute-start | bytes 1572872 | tf_op jit(solution)/shard_map/ppermute | solution.py:864
  60.1 1.9 %collective-permute-start.5 = (f32[4,32,128]{2,1,0:T(8,128)}, f32[4,32,128]{2,1,0:T(8,128)}, u32[]{:S(2)}, u32[]{:S(2)}) collective-permute-start(f32[4,32,128]{2,1,0:T(8,128)} %get-tuple-element.38), channel_id=1, source_target_pairs={{0,9},{1,10},{2,11},{3,12},{4,13},{5,14},{6,15},{8,17},{9,18},{10,... | collective-permute-start | bytes 196616 | tf_op jit(solution)/shard_map/ppermute | solution.py:874
  62.1 3.5 %collective-permute-start.4 = (f32[4,128,128]{2,1,0:T(8,128)}, f32[4,128,128]{2,1,0:T(8,128)}, u32[]{:S(2)}, u32[]{:S(2)}) collective-permute-start(f32[4,128,128]{2,1,0:T(8,128)} %get-tuple-element.37), channel_id=1, source_target_pairs={{0,1},{1,2},{2,3},{3,4},{4,5},{5,6},{6,7},{8,9},{9,10},{10,11},{11... | collective-permute-start | bytes 786440 | tf_op jit(solution)/shard_map/ppermute | solution.py:867
  65.5 9.1 %backward_inner.1.own_ref = f32[4,256,512]{2,1,0:T(8,128)} custom-call(s32[33]{0:T(128)} %get-tuple-element.30.count_ref, f32[32,128,128]{2,1,0:T(8,128)} %get-tuple-element.31.sum_ref, f32[4,256,512]{2,1,0:T(8,128)} %bitcast.8, f32[2,128,128]{2,1,0:T(8,128)} %probe_ref.9, bf16[8,256,256]{2,1,0:T(8,128)(2,1)} %constant.2.clone.tables.tables_ref, ...), custom_call_target="tpu_custom_call" | custom-call | flops 3623878656 | bytes 1048576 | tf_op jit(solution)/shard_map/backward_inner/pallas_call | solution.py:742
  74.7 0.0 collective-permute-done.5.diag_ref
  74.7 0.0 collective-permute-done.4.left_ref
  74.7 0.0 collective-permute-done.3.above_ref
  74.7 2.4 %add_borders.1 = f32[4,256,512]{2,1,0:T(8,128)} custom-call(f32[4,256,512]{2,1,0:T(8,128)} %backward_inner.1.own_ref, f32[4,64,512]{2,1,0:T(8,128)} %collective-permute-done.3.above_ref, f32[4,128,128]{2,1,0:T(8,128)} %collective-permute-done.4.left_ref, f32[4,32,128]{2,1,0:T(8,128)} %collective-permute-done.5.diag_ref), custom_call_target="tpu_custom_call", output_to_operand_aliasing={{}: (0, {})} | custom-call | tf_op jit(solution)/shard_map/add_borders/pallas_call | solution.py:806
Async XLA Ops:
  1.8 31.7 %collective-permute-start = (f32[4,64,512]{2,1,0:T(8,128)}, f32[4,64,512]{2,1,0:T(8,128)}, u32[]{:S(2)}, u32[]{:S(2)}) collective-permute-start(f32[4,64,512]{2,1,0:T(8,128)} %row_strip.1), channel_id=1, source_target_pairs={{8,0},{16,8},{24,16},{32,24},{40,32},{48,40},{56,48},{64,56},{72,6... | collective-permute-start | bytes 1572872 | tf_op jit(solution)/shard_map/ppermute | solution.py:864
  10.2 36.5 %all-to-all-start = ((f32[16,264,128]{2,1,0:T(8,128)}), f32[16,264,128]{2,1,0:T(8,128)}, u32[]{:S(2)}, u32[]{:S(2)}) async-start(f32[16,264,128]{2,1,0:T(8,128)} %pack_measured.1.send_ref), calls=%async_computation | async-start | bytes 4325376 | tf_op jit(solution)/shard_map/all_to_all | solution.py:884
  16.4 12.0 %collective-permute-start.1 = (f32[4,256,128]{2,1,0:T(8,128)}, f32[4,256,128]{2,1,0:T(8,128)}, u32[]{:S(2)}, u32[]{:S(2)}) collective-permute-start(f32[4,256,128]{2,1,0:T(8,128)} %column_strip.1), channel_id=1, source_target_pairs={{1,0},{2,1},{3,2},{4,3},{5,4},{6,5},{7,6},{9,8},{10,9},{11,10},{12... | collective-permute-start | bytes 1572872 | tf_op jit(solution)/shard_map/ppermute | solution.py:867
  34.5 6.7 %collective-permute-start.2 = (f32[4,64,128]{2,1,0:T(8,128)S(1)}, f32[4,64,128]{2,1,0:T(8,128)}, u32[]{:S(2)}, u32[]{:S(2)}) collective-permute-start(f32[4,64,128]{2,1,0:T(8,128)S(1)} %slice.3), channel_id=1, source_target_pairs={{1,0},{2,1},{3,2},{4,3},{5,4},{6,5},{7,6},{9,8},{10,9},{11,10},{12... | collective-permute-start | bytes 393224 | tf_op jit(solution)/shard_map/ppermute | solution.py:867
  55.1 19.6 %collective-permute-start.3 = (f32[4,64,512]{2,1,0:T(8,128)}, f32[4,64,512]{2,1,0:T(8,128)}, u32[]{:S(2)}, u32[]{:S(2)}) collective-permute-start(f32[4,64,512]{2,1,0:T(8,128)} %get-tuple-element.36), channel_id=1, source_target_pairs={{0,8},{8,16},{16,24},{24,32},{32,40},{40,48},{48,56},{56,64},{64,7... | collective-permute-start | bytes 1572872 | tf_op jit(solution)/shard_map/ppermute | solution.py:864
  60.1 14.5 %collective-permute-start.5 = (f32[4,32,128]{2,1,0:T(8,128)}, f32[4,32,128]{2,1,0:T(8,128)}, u32[]{:S(2)}, u32[]{:S(2)}) collective-permute-start(f32[4,32,128]{2,1,0:T(8,128)} %get-tuple-element.38), channel_id=1, source_target_pairs={{0,9},{1,10},{2,11},{3,12},{4,13},{5,14},{6,15},{8,17},{9,18},{10,... | collective-permute-start | bytes 196616 | tf_op jit(solution)/shard_map/ppermute | solution.py:874
  62.1 12.6 %collective-permute-start.4 = (f32[4,128,128]{2,1,0:T(8,128)}, f32[4,128,128]{2,1,0:T(8,128)}, u32[]{:S(2)}, u32[]{:S(2)}) collective-permute-start(f32[4,128,128]{2,1,0:T(8,128)} %get-tuple-element.37), channel_id=1, source_target_pairs={{0,1},{1,2},{2,3},{3,4},{4,5},{5,6},{6,7},{8,9},{9,10},{10,11},{11... | collective-permute-start | bytes 786440 | tf_op jit(solution)/shard_map/ppermute | solution.py:867

commit v8 on v7

--- a/solution.py
+++ b/solution.py
@@ -173,7 +173,7 @@
     return last, side, inner
 
 
-def forward_pairs(places, ext_ref, probe_ref, tables, far_refs, enter_refs):
+def forward_pairs(places, ext_ref, probe_ref, tables, far_refs, enter_refs, entered):
     probe_re = probe_ref[0]
     probe_im = probe_ref[1]
     rows = []
@@ -191,6 +191,7 @@
         rows.append(
             stacked([times(*halves(enter, n), trans[0][n], trans[1][n]) for n in range(2)])
         )
+    entered()
     fars = two_sided(rows, tables, 4, 6)
     for far_ref, far in zip(far_refs, fars):
         far_ref[...] = far
@@ -215,59 +216,25 @@
         copy.wait()
 
 
-def forward_inner_kernel(places, tile_ref, probe_ref, tables, far_ref, enter_ref):
-    forward_pairs(places, tile_ref, probe_ref, tables, each(far_ref), each(enter_ref))
-
-
-def forward_side_kernel(
-    places, tile_ref, right_ref, probe_ref, tables, far_ref, enter_ref, ext_ref, sems
-):
-    cols = tile_ref.shape[2]
+def forward_kernel(places, layout, count, *refs):
+    sources = refs[:count]
+    probe_ref, tables_ref, far_ref, enter_ref = refs[count : count + 4]
+    ext_ref, probe_buf, table_buf, far_buf, enter_buf, sems, out_sems = refs[count + 4 :]
     wait_copies(
         start_copies(
-            [
-                (tile_ref.at[:, :, pl.ds(cols - SIDE, SIDE)], ext_ref.at[:, :, pl.ds(0, SIDE)]),
-                (right_ref, ext_ref.at[:, :, pl.ds(SIDE, SIDE)]),
-            ],
-            sems,
+            [(tables_ref, table_buf), (probe_ref, probe_buf)] + layout(ext_ref, *sources), sems
         )
     )
+    stores = []
+
+    def entered():
+        stores.extend(start_copies([(enter_buf, enter_ref)], out_sems.at[pl.ds(0, 1)]))
+
     forward_pairs(
-        [(row, 0) for row, _ in places], ext_ref, probe_ref, tables, each(far_ref), each(enter_ref)
-    )
-
-
-def forward_last_kernel(
-    places,
-    tile_ref,
-    below_ref,
-    right_ref,
-    diag_ref,
-    probe_ref,
-    tables,
-    far_ref,
-    enter_ref,
-    ext_ref,
-    sems,
-):
-    rows, cols = tile_ref.shape[1:]
-    low = pl.ds(rows - BLOCK, BLOCK)
-    upper, lower = pl.ds(0, BLOCK), pl.ds(BLOCK, BLOCK)
-    wide, beyond = pl.ds(0, cols), pl.ds(cols, SIDE)
-    wait_copies(
-        start_copies(
-            [
-                (tile_ref.at[:, low], ext_ref.at[:, upper, wide]),
-                (below_ref, ext_ref.at[:, lower, wide]),
-                (right_ref.at[:, low], ext_ref.at[:, upper, beyond]),
-                (diag_ref, ext_ref.at[:, lower, beyond]),
-            ],
-            sems,
-        )
-    )
-    forward_pairs(
-        [(0, col) for _, col in places], ext_ref, probe_ref, tables, each(far_ref), each(enter_ref)
-    )
+        places, ext_ref, probe_buf, table_buf, each(far_buf), each(enter_buf), entered
+    )
+    stores.extend(start_copies([(far_buf, far_ref)], out_sems.at[pl.ds(1, 1)]))
+    wait_copies(stores)
 
 
 def stage_cost(pairs):
@@ -293,54 +260,71 @@
     return [pl.BlockSpec(memory_space=pltpu.HBM)] * count
 
 
-def forward_inner(places, tile, probe, tables):
+def forward(name, places, layout, ext, sources, probe, tables):
+    field = (len(places), 2 * SIDE, 2 * SIDE)
     return pl.pallas_call(
-        functools.partial(forward_inner_kernel, places),
+        functools.partial(forward_kernel, places, layout, len(sources)),
         out_shape=fields(places),
-        in_specs=in_vmem(3),
-        out_specs=tuple(in_vmem(2)),
-        compiler_params=pltpu.CompilerParams(vmem_limit_bytes=VMEM_LIMIT),
-        cost_estimate=stage_cost(8 * len(places)),
-        name="forward_inner",
-    )(tile, probe, tables)
-
-
-def extended_shape(tile, comps):
-    return pltpu.VMEM((comps, tile.shape[1] + BLOCK, tile.shape[2] + SIDE), jnp.float32)
-
-
-def forward_side(places, tile, right, probe, tables):
-    comps, rows, _ = tile.shape
-    return pl.pallas_call(
-        functools.partial(forward_side_kernel, places),
-        out_shape=fields(places),
-        in_specs=in_hbm(2) + in_vmem(2),
-        out_specs=tuple(in_vmem(2)),
+        in_specs=in_hbm(len(sources) + 2),
+        out_specs=tuple(in_hbm(2)),
         scratch_shapes=[
-            pltpu.VMEM((comps, rows, 2 * SIDE), jnp.float32),
+            pltpu.VMEM(ext, jnp.float32),
+            pltpu.VMEM(probe.shape, jnp.float32),
+            pltpu.VMEM(tables.shape, tables.dtype),
+            pltpu.VMEM(field, jnp.float32),
+            pltpu.VMEM(field, jnp.float32),
+            pltpu.SemaphoreType.DMA((len(sources) + 2,)),
             pltpu.SemaphoreType.DMA((2,)),
         ],
         compiler_params=pltpu.CompilerParams(vmem_limit_bytes=VMEM_LIMIT),
         cost_estimate=stage_cost(8 * len(places)),
-        name="forward_last_column",
-    )(tile, right, probe, tables)
+        name=name,
+    )(*sources, probe, tables)
+
+
+def forward_inner(places, tile, probe, tables):
+    def layout(ext_ref, tile_ref):
+        return [(tile_ref, ext_ref)]
+
+    return forward("forward_inner", places, layout, tile.shape, (tile,), probe, tables)
+
+
+def extended_shape(tile, comps):
+    return pltpu.VMEM((comps, tile.shape[1] + BLOCK, tile.shape[2] + SIDE), jnp.float32)
+
+
+def forward_side(places, tile, right, probe, tables):
+    comps, rows, cols = tile.shape
+
+    def layout(ext_ref, tile_ref, right_ref):
+        return [
+            (tile_ref.at[:, :, pl.ds(cols - SIDE, SIDE)], ext_ref.at[:, :, pl.ds(0, SIDE)]),
+            (right_ref, ext_ref.at[:, :, pl.ds(SIDE, SIDE)]),
+        ]
+
+    here = [(row, 0) for row, _ in places]
+    ext = (comps, rows, 2 * SIDE)
+    return forward("forward_last_column", here, layout, ext, (tile, right), probe, tables)
 
 
 def forward_last(places, tile, below, right, diag, probe, tables):
-    comps, _, cols = tile.shape
-    return pl.pallas_call(
-        functools.partial(forward_last_kernel, places),
-        out_shape=fields(places),
-        in_specs=in_hbm(4) + in_vmem(2),
-        out_specs=tuple(in_vmem(2)),
-        scratch_shapes=[
-            pltpu.VMEM((comps, SIDE, cols + SIDE), jnp.float32),
-            pltpu.SemaphoreType.DMA((4,)),
-        ],
-        compiler_params=pltpu.CompilerParams(vmem_limit_bytes=VMEM_LIMIT),
-        cost_estimate=stage_cost(8 * len(places)),
-        name="forward_last_row",
-    )(tile, below, right, diag, probe, tables)
+    comps, rows, cols = tile.shape
+
+    def layout(ext_ref, tile_ref, below_ref, right_ref, diag_ref):
+        low = pl.ds(rows - BLOCK, BLOCK)
+        upper, lower = pl.ds(0, BLOCK), pl.ds(BLOCK, BLOCK)
+        wide, beyond = pl.ds(0, cols), pl.ds(cols, SIDE)
+        return [
+            (tile_ref.at[:, low], ext_ref.at[:, upper, wide]),
+            (below_ref, ext_ref.at[:, lower, wide]),
+            (right_ref.at[:, low], ext_ref.at[:, upper, beyond]),
+            (diag_ref, ext_ref.at[:, lower, beyond]),
+        ]
+
+    here = [(0, col) for _, col in places]
+    ext = (comps, SIDE, cols + SIDE)
+    sources = (tile, below, right, diag)
+    return forward("forward_last_row", here, layout, ext, sources, probe, tables)
 
 
 def gather_sums(meta_ref, items_ref, sum_ref, count_ref, arrivals):

time: 78.5 us -> 76.9 us (0.980)
  Pallas kernels: 44.1 us -> 42.4 us
  starting transfers between devices: 26.2 us -> 27.5 us
    pallas_call x3, Pallas kernels: 18.1 us -> 16.4 us  [forward(): pl.pallas_call(functools.partial(forward_kernel, places, layout, len(sour...]
    ppermute x2, starting transfers between devices: 11 us -> 12.2 us  [moved(): return lax.ppermute(shard, 'row', pairs)]
  transfers between devices with their start and end apart: 7 -> 7, of which waited for: 2 -> 2; matrix products, arithmetic and copies ran while one was open for 1% -> 1% of each run, Pallas kernels for 41% -> 39%
where the time goes in v8:
time: 76.9 us; the launch traced here: 76.3 us
  Pallas kernels  42.4 us (55%)
  starting transfers between devices  27.5 us (36%)
  waiting for transfers between devices  5.25 us (7%)
  local copies, waits for them, and re-layouts  0.92 us (1%)
    pallas_call x3, Pallas kernels, forward(): pl.pallas_call(functools.partial(forward_kernel, places, layout, len(sour...  16.4 us
    ppermute x2, starting transfers between devices, moved(): return lax.ppermute(shard, 'row', pairs)  12.2 us
    pallas_call x1, Pallas kernels, backward_inner(): pl.pallas_call(functools.partial(backward_inner_kernel, places), out_shap...  9.11 us
    ppermute x3, starting transfers between devices, moved(): return lax.ppermute(shard, 'col', pairs)  9.03 us
    pallas_call x1, Pallas kernels, backward_rim(): pl.pallas_call(functools.partial(backward_rim_kernel, places), out_shape=...  8.34 us
    ppermute x3, waiting for transfers between devices, moved(): return lax.ppermute(shard, 'col', pairs)  5.24 us
    all_to_all x1, starting transfers between devices, body(): recv = lax.all_to_all(send, 'row', split_axis=0, concat_axis=0, tiled=True)  4.35 us
    pallas_call x1, Pallas kernels, pack(): pl.pallas_call(pack_kernel, out_shape=jax.ShapeDtypeStruct((owners, CAP *...  2.41 us
  transfers between devices with their start and end apart: 7, of which 2 were waited for; matrix products, arithmetic and copies ran while one was open for 1% of the time, Pallas kernels for 39%

profile of v8, /device:TPU:7, one launch (start us, length us, event | category | flops | bytes accessed | tf_op | source)
XLA Modules:
  0.0 76.3 jit_solution(15753130478993175247)
XLA Ops:
  0.0 1.8 %row_strip.1 = f32[4,64,512]{2,1,0:T(8,128)} custom-call(f32[4,256,512]{2,1,0:T(8,128)} %bitcast.2), custom_call_target="tpu_custom_call" | custom-call | tf_op jit(solution)/shard_map/row_strip/pallas_call | solution.py:815
  1.8 5.9 %collective-permute-start = (f32[4,64,512]{2,1,0:T(8,128)}, f32[4,64,512]{2,1,0:T(8,128)}, u32[]{:S(2)}, u32[]{:S(2)}) collective-permute-start(f32[4,64,512]{2,1,0:T(8,128)} %row_strip.1), channel_id=1, source_target_pairs={{8,0},{16,8},{24,16},{32,24},{40,32},{48,40},{56,48},{64,56},{72,6... | collective-permute-start | bytes 1572872 | tf_op jit(solution)/shard_map/ppermute | solution.py:848
  7.8 2.4 %pack_measured.1.send_ref = f32[16,264,128]{2,1,0:T(8,128)} custom-call(s32[2,16]{1,0:T(2,128)} %off_ref.1, f32[16,128,128]{2,1,0:T(8,128)} %meas_ref.1), custom_call_target="tpu_custom_call" | custom-call | bytes 41943040 | tf_op jit(solution)/shard_map/pack_measured/pallas_call | solution.py:145
  10.2 4.3 %all-to-all-start = ((f32[16,264,128]{2,1,0:T(8,128)}), f32[16,264,128]{2,1,0:T(8,128)}, u32[]{:S(2)}, u32[]{:S(2)}) async-start(f32[16,264,128]{2,1,0:T(8,128)} %pack_measured.1.send_ref), calls=%async_computation | async-start | bytes 4325376 | tf_op jit(solution)/shard_map/all_to_all | solution.py:868
  14.6 1.9 %column_strip.1 = f32[4,256,128]{2,1,0:T(8,128)} custom-call(f32[4,256,512]{2,1,0:T(8,128)} %bitcast.3, f32[16,264,128]{2,1,0:T(8,128)} %pack_measured.1.send_ref), custom_call_target="tpu_custom_call" | custom-call | tf_op jit(solution)/shard_map/column_strip/pallas_call | solution.py:832
  16.4 3.4 %collective-permute-start.1 = (f32[4,256,128]{2,1,0:T(8,128)}, f32[4,256,128]{2,1,0:T(8,128)}, u32[]{:S(2)}, u32[]{:S(2)}) collective-permute-start(f32[4,256,128]{2,1,0:T(8,128)} %column_strip.1), channel_id=1, source_target_pairs={{1,0},{2,1},{3,2},{4,3},{5,4},{6,5},{7,6},{9,8},{10,9},{11,10},{12... | collective-permute-start | bytes 1572872 | tf_op jit(solution)/shard_map/ppermute | solution.py:851
  19.9 7.7 %forward_inner.1 = (f32[9,256,256]{2,1,0:T(8,128)}, f32[9,256,256]{2,1,0:T(8,128)}) custom-call(f32[4,256,512]{2,1,0:T(8,128)} %bitcast.4, f32[2,128,128]{2,1,0:T(8,128)} %probe_ref.3, bf16[8,256,256]{2,1,0:T(8,128)(2,1)} %constant.2.clone.refs_2_.refs_3_.refs_5_.tables_ref), custom_call_target="tpu_custom_call" | custom-call | flops 28991029248 | bytes 1048576 | tf_op jit(solution)/shard_map/forward_inner/pallas_call | solution.py:265
  27.5 1.0 %collective-permute-done.1.refs_1_.refs_2_.right_ref = f32[4,256,128]{2,1,0:T(8,128)} collective-permute-done((f32[4,256,128]{2,1,0:T(8,128)}, f32[4,256,128]{2,1,0:T(8,128)}, u32[]{:S(2)}, u32[]{:S(2)}) %collective-permute-start.1) | collective-permute-done | bytes 524320 | tf_op jit(solution)/shard_map/ppermute | solution.py:851
  28.5 4.1 %forward_last_column.1 = (f32[3,256,256]{2,1,0:T(8,128)}, f32[3,256,256]{2,1,0:T(8,128)}) custom-call(f32[4,256,512]{2,1,0:T(8,128)} %bitcast.5, f32[4,256,128]{2,1,0:T(8,128)} %collective-permute-done.1.refs_1_.refs_2_.right_ref, f32[2,128,128]{2,1,0:T(8,128)} %probe_ref.3, bf16[8,256,256]{2,1,0:T(8,128)(2,1)} %constant.2.clone.refs_2_.refs_3_.refs_5_.tables_ref), custom_call_target="tpu_custom_call" | custom-call | flops 9663676416 | bytes 1048576 | tf_op jit(solution)/shard_map/forward_last_column/pallas_call | solution.py:265
  32.6 0.0 collective-permute-done.refs_1_.below_ref
  32.6 0.9 %slice.3 = f32[4,64,128]{2,1,0:T(8,128)S(1)} slice(f32[4,64,512]{2,1,0:T(8,128)} %collective-permute-done.refs_1_.below_ref), slice={[0:4], [0:64], [0:128]} | slice | bytes 262144 | tf_op jit(solution)/shard_map/slice | solution.py:875
  33.5 2.1 %collective-permute-start.2 = (f32[4,64,128]{2,1,0:T(8,128)S(1)}, f32[4,64,128]{2,1,0:T(8,128)}, u32[]{:S(2)}, u32[]{:S(2)}) collective-permute-start(f32[4,64,128]{2,1,0:T(8,128)S(1)} %slice.3), channel_id=1, source_target_pairs={{1,0},{2,1},{3,2},{4,3},{5,4},{6,5},{7,6},{9,8},{10,9},{11,10},{12... | collective-permute-start | bytes 393224 | tf_op jit(solution)/shard_map/ppermute | solution.py:851
  35.6 4.3 %collective-permute-done.2.refs_3_.diag_ref = f32[4,64,128]{2,1,0:T(8,128)} collective-permute-done((f32[4,64,128]{2,1,0:T(8,128)S(1)}, f32[4,64,128]{2,1,0:T(8,128)}, u32[]{:S(2)}, u32[]{:S(2)}) %collective-permute-start.2) | collective-permute-done | bytes 131104 | tf_op jit(solution)/shard_map/ppermute | solution.py:851
  39.9 4.6 %forward_last_row.1 = (f32[4,256,256]{2,1,0:T(8,128)}, f32[4,256,256]{2,1,0:T(8,128)}) custom-call(f32[4,256,512]{2,1,0:T(8,128)} %bitcast.6, f32[4,64,512]{2,1,0:T(8,128)} %collective-permute-done.refs_1_.below_ref, f32[4,256,128]{2,1,0:T(8,128)} %collective-permute-done.1.refs_1_.refs_2_.right_ref, f32[4,64,128]{2,1,0:T(8,128)} %collective-permute-done.2.refs_3_.diag_ref, ...), custom_call_target="tpu_custom_call" | custom-call | flops 12884901888 | bytes 1048576 | tf_op jit(solution)/shard_map/forward_last_row/pallas_call | solution.py:265
  44.6 0.0 all-to-all-done.recv_ref
  44.6 8.3 %backward_rim.1 = (f32[4,64,512]{2,1,0:T(8,128)}, f32[4,256,128]{2,1,0:T(8,128)}, f32[4,64,512]{2,1,0:T(8,128)}, f32[4,128,128]{2,1,0:T(8,128)}, f32[4,32,128]{2...) custom-call(f32[16,264,128]{2,1,0:T(8,128)} %all-to-all-done.recv_ref, f32[4,256,512]{2,1,0:T(8,128)} %bitcast.7, ...), custom_call_target="tpu_custom_call" | custom-call | flops 2818572288 | bytes 1048576 | tf_op jit(solution)/shard_map/backward_rim/pallas_call | solution.py:696
  52.9 6.3 %collective-permute-start.3 = (f32[4,64,512]{2,1,0:T(8,128)}, f32[4,64,512]{2,1,0:T(8,128)}, u32[]{:S(2)}, u32[]{:S(2)}) collective-permute-start(f32[4,64,512]{2,1,0:T(8,128)} %get-tuple-element.36), channel_id=1, source_target_pairs={{0,8},{8,16},{16,24},{24,32},{32,40},{40,48},{48,56},{56,64},{64,7... | collective-permute-start | bytes 1572872 | tf_op jit(solution)/shard_map/ppermute | solution.py:848
  59.2 1.9 %collective-permute-start.5 = (f32[4,32,128]{2,1,0:T(8,128)}, f32[4,32,128]{2,1,0:T(8,128)}, u32[]{:S(2)}, u32[]{:S(2)}) collective-permute-start(f32[4,32,128]{2,1,0:T(8,128)} %get-tuple-element.38), channel_id=1, source_target_pairs={{0,9},{1,10},{2,11},{3,12},{4,13},{5,14},{6,15},{8,17},{9,18},{10,... | collective-permute-start | bytes 196616 | tf_op jit(solution)/shard_map/ppermute | solution.py:858
  61.1 3.5 %collective-permute-start.4 = (f32[4,128,128]{2,1,0:T(8,128)}, f32[4,128,128]{2,1,0:T(8,128)}, u32[]{:S(2)}, u32[]{:S(2)}) collective-permute-start(f32[4,128,128]{2,1,0:T(8,128)} %get-tuple-element.37), channel_id=1, source_target_pairs={{0,1},{1,2},{2,3},{3,4},{4,5},{5,6},{6,7},{8,9},{9,10},{10,11},{11... | collective-permute-start | bytes 786440 | tf_op jit(solution)/shard_map/ppermute | solution.py:851
  64.7 9.1 %backward_inner.1.own_ref = f32[4,256,512]{2,1,0:T(8,128)} custom-call(s32[33]{0:T(128)} %get-tuple-element.30.count_ref, f32[32,128,128]{2,1,0:T(8,128)} %get-tuple-element.31.sum_ref, f32[4,256,512]{2,1,0:T(8,128)} %bitcast.8, f32[2,128,128]{2,1,0:T(8,128)} %probe_ref.3, bf16[8,256,256]{2,1,0:T(8,128)(2,1)} %constant.2.clone.refs_2_.refs_3_.refs_5_.tables_ref, ...), custom_call_target="tpu_custom_call" | custom-call | flops 3623878656 | bytes 1048576 | tf_op jit(solution)/shard_map/backward_inner/pallas_call | solution.py:726
  73.8 0.0 collective-permute-done.5.diag_ref
  73.8 0.0 collective-permute-done.4.left_ref
  73.8 0.0 collective-permute-done.3.above_ref
  73.8 2.4 %add_borders.1 = f32[4,256,512]{2,1,0:T(8,128)} custom-call(f32[4,256,512]{2,1,0:T(8,128)} %backward_inner.1.own_ref, f32[4,64,512]{2,1,0:T(8,128)} %collective-permute-done.3.above_ref, f32[4,128,128]{2,1,0:T(8,128)} %collective-permute-done.4.left_ref, f32[4,32,128]{2,1,0:T(8,128)} %collective-permute-done.5.diag_ref), custom_call_target="tpu_custom_call", output_to_operand_aliasing={{}: (0, {})} | custom-call | tf_op jit(solution)/shard_map/add_borders/pallas_call | solution.py:790
Async XLA Ops:
  1.8 30.8 %collective-permute-start = (f32[4,64,512]{2,1,0:T(8,128)}, f32[4,64,512]{2,1,0:T(8,128)}, u32[]{:S(2)}, u32[]{:S(2)}) collective-permute-start(f32[4,64,512]{2,1,0:T(8,128)} %row_strip.1), channel_id=1, source_target_pairs={{8,0},{16,8},{24,16},{32,24},{40,32},{48,40},{56,48},{64,56},{72,6... | collective-permute-start | bytes 1572872 | tf_op jit(solution)/shard_map/ppermute | solution.py:848
  10.2 34.4 %all-to-all-start = ((f32[16,264,128]{2,1,0:T(8,128)}), f32[16,264,128]{2,1,0:T(8,128)}, u32[]{:S(2)}, u32[]{:S(2)}) async-start(f32[16,264,128]{2,1,0:T(8,128)} %pack_measured.1.send_ref), calls=%async_computation | async-start | bytes 4325376 | tf_op jit(solution)/shard_map/all_to_all | solution.py:868
  16.4 12.1 %collective-permute-start.1 = (f32[4,256,128]{2,1,0:T(8,128)}, f32[4,256,128]{2,1,0:T(8,128)}, u32[]{:S(2)}, u32[]{:S(2)}) collective-permute-start(f32[4,256,128]{2,1,0:T(8,128)} %column_strip.1), channel_id=1, source_target_pairs={{1,0},{2,1},{3,2},{4,3},{5,4},{6,5},{7,6},{9,8},{10,9},{11,10},{12... | collective-permute-start | bytes 1572872 | tf_op jit(solution)/shard_map/ppermute | solution.py:851
  33.5 6.4 %collective-permute-start.2 = (f32[4,64,128]{2,1,0:T(8,128)S(1)}, f32[4,64,128]{2,1,0:T(8,128)}, u32[]{:S(2)}, u32[]{:S(2)}) collective-permute-start(f32[4,64,128]{2,1,0:T(8,128)S(1)} %slice.3), channel_id=1, source_target_pairs={{1,0},{2,1},{3,2},{4,3},{5,4},{6,5},{7,6},{9,8},{10,9},{11,10},{12... | collective-permute-start | bytes 393224 | tf_op jit(solution)/shard_map/ppermute | solution.py:851
  52.9 20.9 %collective-permute-start.3 = (f32[4,64,512]{2,1,0:T(8,128)}, f32[4,64,512]{2,1,0:T(8,128)}, u32[]{:S(2)}, u32[]{:S(2)}) collective-permute-start(f32[4,64,512]{2,1,0:T(8,128)} %get-tuple-element.36), channel_id=1, source_target_pairs={{0,8},{8,16},{16,24},{24,32},{32,40},{40,48},{48,56},{56,64},{64,7... | collective-permute-start | bytes 1572872 | tf_op jit(solution)/shard_map/ppermute | solution.py:848
  59.2 14.6 %collective-permute-start.5 = (f32[4,32,128]{2,1,0:T(8,128)}, f32[4,32,128]{2,1,0:T(8,128)}, u32[]{:S(2)}, u32[]{:S(2)}) collective-permute-start(f32[4,32,128]{2,1,0:T(8,128)} %get-tuple-element.38), channel_id=1, source_target_pairs={{0,9},{1,10},{2,11},{3,12},{4,13},{5,14},{6,15},{8,17},{9,18},{10,... | collective-permute-start | bytes 196616 | tf_op jit(solution)/shard_map/ppermute | solution.py:858
  61.1 12.6 %collective-permute-start.4 = (f32[4,128,128]{2,1,0:T(8,128)}, f32[4,128,128]{2,1,0:T(8,128)}, u32[]{:S(2)}, u32[]{:S(2)}) collective-permute-start(f32[4,128,128]{2,1,0:T(8,128)} %get-tuple-element.37), channel_id=1, source_target_pairs={{0,1},{1,2},{2,3},{3,4},{4,5},{5,6},{6,7},{8,9},{9,10},{10,11},{11... | collective-permute-start | bytes 786440 | tf_op jit(solution)/shard_map/ppermute | solution.py:851

commit v9 on v8

--- a/solution.py
+++ b/solution.py
@@ -173,7 +173,7 @@
     return last, side, inner
 
 
-def forward_pairs(places, ext_ref, probe_ref, tables, far_refs, enter_refs, entered):
+def forward_pairs(places, ext_ref, probe_ref, tables, far_refs, enter_refs, entered, ready):
     probe_re = probe_ref[0]
     probe_im = probe_ref[1]
     rows = []
@@ -193,8 +193,9 @@
         )
     entered()
     fars = two_sided(rows, tables, 4, 6)
-    for far_ref, far in zip(far_refs, fars):
-        far_ref[...] = far
+    for pair, far in enumerate(fars):
+        far_refs[pair][...] = far
+        ready(pair)
 
 
 def each(ref):
@@ -230,10 +231,14 @@
     def entered():
         stores.extend(start_copies([(enter_buf, enter_ref)], out_sems.at[pl.ds(0, 1)]))
 
+    def ready(pair):
+        stores.extend(
+            start_copies([(far_buf.at[pair], far_ref.at[pair])], out_sems.at[pl.ds(1 + pair, 1)])
+        )
+
     forward_pairs(
-        places, ext_ref, probe_buf, table_buf, each(far_buf), each(enter_buf), entered
-    )
-    stores.extend(start_copies([(far_buf, far_ref)], out_sems.at[pl.ds(1, 1)]))
+        places, ext_ref, probe_buf, table_buf, each(far_buf), each(enter_buf), entered, ready
+    )
     wait_copies(stores)
 
 
@@ -274,7 +279,7 @@
             pltpu.VMEM(field, jnp.float32),
             pltpu.VMEM(field, jnp.float32),
             pltpu.SemaphoreType.DMA((len(sources) + 2,)),
-            pltpu.SemaphoreType.DMA((2,)),
+            pltpu.SemaphoreType.DMA((1 + len(places),)),
         ],
         compiler_params=pltpu.CompilerParams(vmem_limit_bytes=VMEM_LIMIT),
         cost_estimate=stage_cost(8 * len(places)),

time: 76.9 us -> 76.7 us (level)
  Pallas kernels: 42.4 us -> 41.5 us
    pallas_call x3, Pallas kernels: 16.4 us -> 15.6 us  [forward(): pl.pallas_call(functools.partial(forward_kernel, places, layout, len(sour...]
  transfers between devices with their start and end apart: 7 -> 7, of which waited for: 2 -> 2; matrix products, arithmetic and copies ran while one was open for 1% -> 1% of each run, Pallas kernels for 39% -> 38%
where the time goes in v9:
time: 76.7 us; the launch traced here: 76.2 us
  Pallas kernels  41.5 us (54%)
  starting transfers between devices  27.6 us (36%)
  waiting for transfers between devices  5.9 us (8%)
  local copies, waits for them, and re-layouts  0.92 us (1%)
    pallas_call x3, Pallas kernels, forward(): pl.pallas_call(functools.partial(forward_kernel, places, layout, len(sour...  15.6 us
    ppermute x2, starting transfers between devices, moved(): return lax.ppermute(shard, 'row', pairs)  12.2 us
    pallas_call x1, Pallas kernels, backward_inner(): pl.pallas_call(functools.partial(backward_inner_kernel, places), out_shap...  9.11 us
    ppermute x3, starting transfers between devices, moved(): return lax.ppermute(shard, 'col', pairs)  9.06 us
    pallas_call x1, Pallas kernels, backward_rim(): pl.pallas_call(functools.partial(backward_rim_kernel, places), out_shape=...  8.33 us
    ppermute x3, waiting for transfers between devices, moved(): return lax.ppermute(shard, 'col', pairs)  5.89 us
    all_to_all x1, starting transfers between devices, body(): recv = lax.all_to_all(send, 'row', split_axis=0, concat_axis=0, tiled=True)  4.38 us
    pallas_call x1, Pallas kernels, pack(): pl.pallas_call(pack_kernel, out_shape=jax.ShapeDtypeStruct((owners, CAP *...  2.4 us
  transfers between devices with their start and end apart: 7, of which 2 were waited for; matrix products, arithmetic and copies ran while one was open for 1% of the time, Pallas kernels for 38%

profile of v9, /device:TPU:7, one launch (start us, length us, event | category | flops | bytes accessed | tf_op | source)
XLA Modules:
  0.0 76.2 jit_solution(17579069625905907641)
XLA Ops:
  0.0 1.8 %row_strip.1 = f32[4,64,512]{2,1,0:T(8,128)} custom-call(f32[4,256,512]{2,1,0:T(8,128)} %bitcast.2), custom_call_target="tpu_custom_call" | custom-call | tf_op jit(solution)/shard_map/row_strip/pallas_call | solution.py:820
  1.8 5.9 %collective-permute-start = (f32[4,64,512]{2,1,0:T(8,128)}, f32[4,64,512]{2,1,0:T(8,128)}, u32[]{:S(2)}, u32[]{:S(2)}) collective-permute-start(f32[4,64,512]{2,1,0:T(8,128)} %row_strip.1), channel_id=1, source_target_pairs={{8,0},{16,8},{24,16},{32,24},{40,32},{48,40},{56,48},{64,56},{72,6... | collective-permute-start | bytes 1572872 | tf_op jit(solution)/shard_map/ppermute | solution.py:853
  7.8 2.4 %pack_measured.1.send_ref = f32[16,264,128]{2,1,0:T(8,128)} custom-call(s32[2,16]{1,0:T(2,128)} %off_ref.1, f32[16,128,128]{2,1,0:T(8,128)} %meas_ref.1), custom_call_target="tpu_custom_call" | custom-call | bytes 41943040 | tf_op jit(solution)/shard_map/pack_measured/pallas_call | solution.py:145
  10.2 4.4 %all-to-all-start = ((f32[16,264,128]{2,1,0:T(8,128)}), f32[16,264,128]{2,1,0:T(8,128)}, u32[]{:S(2)}, u32[]{:S(2)}) async-start(f32[16,264,128]{2,1,0:T(8,128)} %pack_measured.1.send_ref), calls=%async_computation | async-start | bytes 4325376 | tf_op jit(solution)/shard_map/all_to_all | solution.py:873
  14.6 1.9 %column_strip.1 = f32[4,256,128]{2,1,0:T(8,128)} custom-call(f32[4,256,512]{2,1,0:T(8,128)} %bitcast.3, f32[16,264,128]{2,1,0:T(8,128)} %pack_measured.1.send_ref), custom_call_target="tpu_custom_call" | custom-call | tf_op jit(solution)/shard_map/column_strip/pallas_call | solution.py:837
  16.4 3.4 %collective-permute-start.1 = (f32[4,256,128]{2,1,0:T(8,128)}, f32[4,256,128]{2,1,0:T(8,128)}, u32[]{:S(2)}, u32[]{:S(2)}) collective-permute-start(f32[4,256,128]{2,1,0:T(8,128)} %column_strip.1), channel_id=1, source_target_pairs={{1,0},{2,1},{3,2},{4,3},{5,4},{6,5},{7,6},{9,8},{10,9},{11,10},{12... | collective-permute-start | bytes 1572872 | tf_op jit(solution)/shard_map/ppermute | solution.py:856
  19.9 7.1 %forward_inner.1 = (f32[9,256,256]{2,1,0:T(8,128)}, f32[9,256,256]{2,1,0:T(8,128)}) custom-call(f32[4,256,512]{2,1,0:T(8,128)} %bitcast.4, f32[2,128,128]{2,1,0:T(8,128)} %probe_ref.3, bf16[8,256,256]{2,1,0:T(8,128)(2,1)} %constant.2.clone.refs_2_.refs_3_.refs_5_.tables_ref), custom_call_target="tpu_custom_call" | custom-call | flops 28991029248 | bytes 1048576 | tf_op jit(solution)/shard_map/forward_inner/pallas_call | solution.py:270
  27.0 1.4 %collective-permute-done.1.refs_1_.refs_2_.right_ref = f32[4,256,128]{2,1,0:T(8,128)} collective-permute-done((f32[4,256,128]{2,1,0:T(8,128)}, f32[4,256,128]{2,1,0:T(8,128)}, u32[]{:S(2)}, u32[]{:S(2)}) %collective-permute-start.1) | collective-permute-done | bytes 524320 | tf_op jit(solution)/shard_map/ppermute | solution.py:856
  28.5 4.0 %forward_last_column.1 = (f32[3,256,256]{2,1,0:T(8,128)}, f32[3,256,256]{2,1,0:T(8,128)}) custom-call(f32[4,256,512]{2,1,0:T(8,128)} %bitcast.5, f32[4,256,128]{2,1,0:T(8,128)} %collective-permute-done.1.refs_1_.refs_2_.right_ref, f32[2,128,128]{2,1,0:T(8,128)} %probe_ref.3, bf16[8,256,256]{2,1,0:T(8,128)(2,1)} %constant.2.clone.refs_2_.refs_3_.refs_5_.tables_ref), custom_call_target="tpu_custom_call" | custom-call | flops 9663676416 | bytes 1048576 | tf_op jit(solution)/shard_map/forward_last_column/pallas_call | solution.py:270
  32.4 0.0 collective-permute-done.refs_1_.below_ref
  32.4 0.9 %slice.3 = f32[4,64,128]{2,1,0:T(8,128)S(1)} slice(f32[4,64,512]{2,1,0:T(8,128)} %collective-permute-done.refs_1_.below_ref), slice={[0:4], [0:64], [0:128]} | slice | bytes 262144 | tf_op jit(solution)/shard_map/slice | solution.py:880
  33.4 2.1 %collective-permute-start.2 = (f32[4,64,128]{2,1,0:T(8,128)S(1)}, f32[4,64,128]{2,1,0:T(8,128)}, u32[]{:S(2)}, u32[]{:S(2)}) collective-permute-start(f32[4,64,128]{2,1,0:T(8,128)S(1)} %slice.3), channel_id=1, source_target_pairs={{1,0},{2,1},{3,2},{4,3},{5,4},{6,5},{7,6},{9,8},{10,9},{11,10},{12... | collective-permute-start | bytes 393224 | tf_op jit(solution)/shard_map/ppermute | solution.py:856
  35.5 4.4 %collective-permute-done.2.refs_3_.diag_ref = f32[4,64,128]{2,1,0:T(8,128)} collective-permute-done((f32[4,64,128]{2,1,0:T(8,128)S(1)}, f32[4,64,128]{2,1,0:T(8,128)}, u32[]{:S(2)}, u32[]{:S(2)}) %collective-permute-start.2) | collective-permute-done | bytes 131104 | tf_op jit(solution)/shard_map/ppermute | solution.py:856
  39.9 4.5 %forward_last_row.1 = (f32[4,256,256]{2,1,0:T(8,128)}, f32[4,256,256]{2,1,0:T(8,128)}) custom-call(f32[4,256,512]{2,1,0:T(8,128)} %bitcast.6, f32[4,64,512]{2,1,0:T(8,128)} %collective-permute-done.refs_1_.below_ref, f32[4,256,128]{2,1,0:T(8,128)} %collective-permute-done.1.refs_1_.refs_2_.right_ref, f32[4,64,128]{2,1,0:T(8,128)} %collective-permute-done.2.refs_3_.diag_ref, ...), custom_call_target="tpu_custom_call" | custom-call | flops 12884901888 | bytes 1048576 | tf_op jit(solution)/shard_map/forward_last_row/pallas_call | solution.py:270
  44.4 0.0 all-to-all-done.recv_ref
  44.4 8.3 %backward_rim.1 = (f32[4,64,512]{2,1,0:T(8,128)}, f32[4,256,128]{2,1,0:T(8,128)}, f32[4,64,512]{2,1,0:T(8,128)}, f32[4,128,128]{2,1,0:T(8,128)}, f32[4,32,128]{2...) custom-call(f32[16,264,128]{2,1,0:T(8,128)} %all-to-all-done.recv_ref, f32[4,256,512]{2,1,0:T(8,128)} %bitcast.7, ...), custom_call_target="tpu_custom_call" | custom-call | flops 2818572288 | bytes 1048576 | tf_op jit(solution)/shard_map/backward_rim/pallas_call | solution.py:701
  52.8 6.3 %collective-permute-start.3 = (f32[4,64,512]{2,1,0:T(8,128)}, f32[4,64,512]{2,1,0:T(8,128)}, u32[]{:S(2)}, u32[]{:S(2)}) collective-permute-start(f32[4,64,512]{2,1,0:T(8,128)} %get-tuple-element.36), channel_id=1, source_target_pairs={{0,8},{8,16},{16,24},{24,32},{32,40},{40,48},{48,56},{56,64},{64,7... | collective-permute-start | bytes 1572872 | tf_op jit(solution)/shard_map/ppermute | solution.py:853
  59.1 1.9 %collective-permute-start.5 = (f32[4,32,128]{2,1,0:T(8,128)}, f32[4,32,128]{2,1,0:T(8,128)}, u32[]{:S(2)}, u32[]{:S(2)}) collective-permute-start(f32[4,32,128]{2,1,0:T(8,128)} %get-tuple-element.38), channel_id=1, source_target_pairs={{0,9},{1,10},{2,11},{3,12},{4,13},{5,14},{6,15},{8,17},{9,18},{10,... | collective-permute-start | bytes 196616 | tf_op jit(solution)/shard_map/ppermute | solution.py:863
  61.0 3.5 %collective-permute-start.4 = (f32[4,128,128]{2,1,0:T(8,128)}, f32[4,128,128]{2,1,0:T(8,128)}, u32[]{:S(2)}, u32[]{:S(2)}) collective-permute-start(f32[4,128,128]{2,1,0:T(8,128)} %get-tuple-element.37), channel_id=1, source_target_pairs={{0,1},{1,2},{2,3},{3,4},{4,5},{5,6},{6,7},{8,9},{9,10},{10,11},{11... | collective-permute-start | bytes 786440 | tf_op jit(solution)/shard_map/ppermute | solution.py:856
  64.5 9.1 %backward_inner.1.own_ref = f32[4,256,512]{2,1,0:T(8,128)} custom-call(s32[33]{0:T(128)} %get-tuple-element.30.count_ref, f32[32,128,128]{2,1,0:T(8,128)} %get-tuple-element.31.sum_ref, f32[4,256,512]{2,1,0:T(8,128)} %bitcast.8, f32[2,128,128]{2,1,0:T(8,128)} %probe_ref.3, bf16[8,256,256]{2,1,0:T(8,128)(2,1)} %constant.2.clone.refs_2_.refs_3_.refs_5_.tables_ref, ...), custom_call_target="tpu_custom_call" | custom-call | flops 3623878656 | bytes 1048576 | tf_op jit(solution)/shard_map/backward_inner/pallas_call | solution.py:731
  73.6 0.0 collective-permute-done.5.diag_ref
  73.6 0.0 collective-permute-done.4.left_ref
  73.6 0.0 collective-permute-done.3.above_ref
  73.7 2.4 %add_borders.1 = f32[4,256,512]{2,1,0:T(8,128)} custom-call(f32[4,256,512]{2,1,0:T(8,128)} %backward_inner.1.own_ref, f32[4,64,512]{2,1,0:T(8,128)} %collective-permute-done.3.above_ref, f32[4,128,128]{2,1,0:T(8,128)} %collective-permute-done.4.left_ref, f32[4,32,128]{2,1,0:T(8,128)} %collective-permute-done.5.diag_ref), custom_call_target="tpu_custom_call", output_to_operand_aliasing={{}: (0, {})} | custom-call | tf_op jit(solution)/shard_map/add_borders/pallas_call | solution.py:795
Async XLA Ops:
  1.8 30.6 %collective-permute-start = (f32[4,64,512]{2,1,0:T(8,128)}, f32[4,64,512]{2,1,0:T(8,128)}, u32[]{:S(2)}, u32[]{:S(2)}) collective-permute-start(f32[4,64,512]{2,1,0:T(8,128)} %row_strip.1), channel_id=1, source_target_pairs={{8,0},{16,8},{24,16},{32,24},{40,32},{48,40},{56,48},{64,56},{72,6... | collective-permute-start | bytes 1572872 | tf_op jit(solution)/shard_map/ppermute | solution.py:853
  10.2 34.2 %all-to-all-start = ((f32[16,264,128]{2,1,0:T(8,128)}), f32[16,264,128]{2,1,0:T(8,128)}, u32[]{:S(2)}, u32[]{:S(2)}) async-start(f32[16,264,128]{2,1,0:T(8,128)} %pack_measured.1.send_ref), calls=%async_computation | async-start | bytes 4325376 | tf_op jit(solution)/shard_map/all_to_all | solution.py:873
  16.4 12.0 %collective-permute-start.1 = (f32[4,256,128]{2,1,0:T(8,128)}, f32[4,256,128]{2,1,0:T(8,128)}, u32[]{:S(2)}, u32[]{:S(2)}) collective-permute-start(f32[4,256,128]{2,1,0:T(8,128)} %column_strip.1), channel_id=1, source_target_pairs={{1,0},{2,1},{3,2},{4,3},{5,4},{6,5},{7,6},{9,8},{10,9},{11,10},{12... | collective-permute-start | bytes 1572872 | tf_op jit(solution)/shard_map/ppermute | solution.py:856
  33.4 6.6 %collective-permute-start.2 = (f32[4,64,128]{2,1,0:T(8,128)S(1)}, f32[4,64,128]{2,1,0:T(8,128)}, u32[]{:S(2)}, u32[]{:S(2)}) collective-permute-start(f32[4,64,128]{2,1,0:T(8,128)S(1)} %slice.3), channel_id=1, source_target_pairs={{1,0},{2,1},{3,2},{4,3},{5,4},{6,5},{7,6},{9,8},{10,9},{11,10},{12... | collective-permute-start | bytes 393224 | tf_op jit(solution)/shard_map/ppermute | solution.py:856
  52.8 20.9 %collective-permute-start.3 = (f32[4,64,512]{2,1,0:T(8,128)}, f32[4,64,512]{2,1,0:T(8,128)}, u32[]{:S(2)}, u32[]{:S(2)}) collective-permute-start(f32[4,64,512]{2,1,0:T(8,128)} %get-tuple-element.36), channel_id=1, source_target_pairs={{0,8},{8,16},{16,24},{24,32},{32,40},{40,48},{48,56},{56,64},{64,7... | collective-permute-start | bytes 1572872 | tf_op jit(solution)/shard_map/ppermute | solution.py:853
  59.1 14.6 %collective-permute-start.5 = (f32[4,32,128]{2,1,0:T(8,128)}, f32[4,32,128]{2,1,0:T(8,128)}, u32[]{:S(2)}, u32[]{:S(2)}) collective-permute-start(f32[4,32,128]{2,1,0:T(8,128)} %get-tuple-element.38), channel_id=1, source_target_pairs={{0,9},{1,10},{2,11},{3,12},{4,13},{5,14},{6,15},{8,17},{9,18},{10,... | collective-permute-start | bytes 196616 | tf_op jit(solution)/shard_map/ppermute | solution.py:863
  61.0 12.6 %collective-permute-start.4 = (f32[4,128,128]{2,1,0:T(8,128)}, f32[4,128,128]{2,1,0:T(8,128)}, u32[]{:S(2)}, u32[]{:S(2)}) collective-permute-start(f32[4,128,128]{2,1,0:T(8,128)} %get-tuple-element.37), channel_id=1, source_target_pairs={{0,1},{1,2},{2,3},{3,4},{4,5},{5,6},{6,7},{8,9},{9,10},{10,11},{11... | collective-permute-start | bytes 786440 | tf_op jit(solution)/shard_map/ppermute | solution.py:856

commit v10 on v9

--- a/solution.py
+++ b/solution.py
@@ -395,8 +395,8 @@
             store(n, 3, row, col, grad[1])
             waves.append(conj_times(trans[0][n], trans[1][n], *back))
         rows.append(stacked(waves))
+    backs = two_sided(rows, tables, 2, 0)
     after_fields()
-    backs = two_sided(rows, tables, 2, 0)
     probe_re = probe_ref[0]
     probe_im = probe_ref[1]
     for pair, (row, col) in enumerate(places):

time: 76.7 us -> 76.7 us (level)
  no operation moved by 1% of the time
where the time goes in v10:
time: 76.7 us; the launch traced here: 76.2 us
  Pallas kernels  41.5 us (54%)
  starting transfers between devices  27.5 us (36%)
  waiting for transfers between devices  5.94 us (8%)
  local copies, waits for them, and re-layouts  0.92 us (1%)
    pallas_call x3, Pallas kernels, forward(): pl.pallas_call(functools.partial(forward_kernel, places, layout, len(sour...  15.6 us
    ppermute x2, starting transfers between devices, moved(): return lax.ppermute(shard, 'row', pairs)  12.2 us
    pallas_call x1, Pallas kernels, backward_inner(): pl.pallas_call(functools.partial(backward_inner_kernel, places), out_shap...  9.12 us
    ppermute x3, starting transfers between devices, moved(): return lax.ppermute(shard, 'col', pairs)  9 us
    pallas_call x1, Pallas kernels, backward_rim(): pl.pallas_call(functools.partial(backward_rim_kernel, places), out_shape=...  8.32 us
    ppermute x3, waiting for transfers between devices, moved(): return lax.ppermute(shard, 'col', pairs)  5.93 us
    all_to_all x1, starting transfers between devices, body(): recv = lax.all_to_all(send, 'row', split_axis=0, concat_axis=0, tiled=True)  4.38 us
    pallas_call x1, Pallas kernels, pack(): pl.pallas_call(pack_kernel, out_shape=jax.ShapeDtypeStruct((owners, CAP *...  2.42 us
  transfers between devices with their start and end apart: 7, of which 2 were waited for; matrix products, arithmetic and copies ran while one was open for 1% of the time, Pallas kernels for 38%

profile of v10, /device:TPU:7, one launch (start us, length us, event | category | flops | bytes accessed | tf_op | source)
XLA Modules:
  0.0 76.2 jit_solution(856965950279896762)
XLA Ops:
  0.0 1.8 %row_strip.1 = f32[4,64,512]{2,1,0:T(8,128)} custom-call(f32[4,256,512]{2,1,0:T(8,128)} %bitcast.2), custom_call_target="tpu_custom_call" | custom-call | tf_op jit(solution)/shard_map/row_strip/pallas_call | solution.py:820
  1.8 5.9 %collective-permute-start = (f32[4,64,512]{2,1,0:T(8,128)}, f32[4,64,512]{2,1,0:T(8,128)}, u32[]{:S(2)}, u32[]{:S(2)}) collective-permute-start(f32[4,64,512]{2,1,0:T(8,128)} %row_strip.1), channel_id=1, source_target_pairs={{8,0},{16,8},{24,16},{32,24},{40,32},{48,40},{56,48},{64,56},{72,6... | collective-permute-start | bytes 1572872 | tf_op jit(solution)/shard_map/ppermute | solution.py:853
  7.8 2.4 %pack_measured.1.send_ref = f32[16,264,128]{2,1,0:T(8,128)} custom-call(s32[2,16]{1,0:T(2,128)} %off_ref.1, f32[16,128,128]{2,1,0:T(8,128)} %meas_ref.1), custom_call_target="tpu_custom_call" | custom-call | bytes 41943040 | tf_op jit(solution)/shard_map/pack_measured/pallas_call | solution.py:145
  10.2 4.4 %all-to-all-start = ((f32[16,264,128]{2,1,0:T(8,128)}), f32[16,264,128]{2,1,0:T(8,128)}, u32[]{:S(2)}, u32[]{:S(2)}) async-start(f32[16,264,128]{2,1,0:T(8,128)} %pack_measured.1.send_ref), calls=%async_computation | async-start | bytes 4325376 | tf_op jit(solution)/shard_map/all_to_all | solution.py:873
  14.6 1.9 %column_strip.1 = f32[4,256,128]{2,1,0:T(8,128)} custom-call(f32[4,256,512]{2,1,0:T(8,128)} %bitcast.3, f32[16,264,128]{2,1,0:T(8,128)} %pack_measured.1.send_ref), custom_call_target="tpu_custom_call" | custom-call | tf_op jit(solution)/shard_map/column_strip/pallas_call | solution.py:837
  16.5 3.4 %collective-permute-start.1 = (f32[4,256,128]{2,1,0:T(8,128)}, f32[4,256,128]{2,1,0:T(8,128)}, u32[]{:S(2)}, u32[]{:S(2)}) collective-permute-start(f32[4,256,128]{2,1,0:T(8,128)} %column_strip.1), channel_id=1, source_target_pairs={{1,0},{2,1},{3,2},{4,3},{5,4},{6,5},{7,6},{9,8},{10,9},{11,10},{12... | collective-permute-start | bytes 1572872 | tf_op jit(solution)/shard_map/ppermute | solution.py:856
  19.9 7.1 %forward_inner.1 = (f32[9,256,256]{2,1,0:T(8,128)}, f32[9,256,256]{2,1,0:T(8,128)}) custom-call(f32[4,256,512]{2,1,0:T(8,128)} %bitcast.4, f32[2,128,128]{2,1,0:T(8,128)} %probe_ref.3, bf16[8,256,256]{2,1,0:T(8,128)(2,1)} %constant.2.clone.refs_2_.refs_3_.refs_5_.tables_ref), custom_call_target="tpu_custom_call" | custom-call | flops 28991029248 | bytes 1048576 | tf_op jit(solution)/shard_map/forward_inner/pallas_call | solution.py:270
  27.0 1.5 %collective-permute-done.1.refs_1_.refs_2_.right_ref = f32[4,256,128]{2,1,0:T(8,128)} collective-permute-done((f32[4,256,128]{2,1,0:T(8,128)}, f32[4,256,128]{2,1,0:T(8,128)}, u32[]{:S(2)}, u32[]{:S(2)}) %collective-permute-start.1) | collective-permute-done | bytes 524320 | tf_op jit(solution)/shard_map/ppermute | solution.py:856
  28.5 4.0 %forward_last_column.1 = (f32[3,256,256]{2,1,0:T(8,128)}, f32[3,256,256]{2,1,0:T(8,128)}) custom-call(f32[4,256,512]{2,1,0:T(8,128)} %bitcast.5, f32[4,256,128]{2,1,0:T(8,128)} %collective-permute-done.1.refs_1_.refs_2_.right_ref, f32[2,128,128]{2,1,0:T(8,128)} %probe_ref.3, bf16[8,256,256]{2,1,0:T(8,128)(2,1)} %constant.2.clone.refs_2_.refs_3_.refs_5_.tables_ref), custom_call_target="tpu_custom_call" | custom-call | flops 9663676416 | bytes 1048576 | tf_op jit(solution)/shard_map/forward_last_column/pallas_call | solution.py:270
  32.5 0.0 collective-permute-done.refs_1_.below_ref
  32.5 0.9 %slice.3 = f32[4,64,128]{2,1,0:T(8,128)S(1)} slice(f32[4,64,512]{2,1,0:T(8,128)} %collective-permute-done.refs_1_.below_ref), slice={[0:4], [0:64], [0:128]} | slice | bytes 262144 | tf_op jit(solution)/shard_map/slice | solution.py:880
  33.4 2.1 %collective-permute-start.2 = (f32[4,64,128]{2,1,0:T(8,128)S(1)}, f32[4,64,128]{2,1,0:T(8,128)}, u32[]{:S(2)}, u32[]{:S(2)}) collective-permute-start(f32[4,64,128]{2,1,0:T(8,128)S(1)} %slice.3), channel_id=1, source_target_pairs={{1,0},{2,1},{3,2},{4,3},{5,4},{6,5},{7,6},{9,8},{10,9},{11,10},{12... | collective-permute-start | bytes 393224 | tf_op jit(solution)/shard_map/ppermute | solution.py:856
  35.5 4.4 %collective-permute-done.2.refs_3_.diag_ref = f32[4,64,128]{2,1,0:T(8,128)} collective-permute-done((f32[4,64,128]{2,1,0:T(8,128)S(1)}, f32[4,64,128]{2,1,0:T(8,128)}, u32[]{:S(2)}, u32[]{:S(2)}) %collective-permute-start.2) | collective-permute-done | bytes 131104 | tf_op jit(solution)/shard_map/ppermute | solution.py:856
  39.9 4.5 %forward_last_row.1 = (f32[4,256,256]{2,1,0:T(8,128)}, f32[4,256,256]{2,1,0:T(8,128)}) custom-call(f32[4,256,512]{2,1,0:T(8,128)} %bitcast.6, f32[4,64,512]{2,1,0:T(8,128)} %collective-permute-done.refs_1_.below_ref, f32[4,256,128]{2,1,0:T(8,128)} %collective-permute-done.1.refs_1_.refs_2_.right_ref, f32[4,64,128]{2,1,0:T(8,128)} %collective-permute-done.2.refs_3_.diag_ref, ...), custom_call_target="tpu_custom_call" | custom-call | flops 12884901888 | bytes 1048576 | tf_op jit(solution)/shard_map/forward_last_row/pallas_call | solution.py:270
  44.4 0.0 all-to-all-done.recv_ref
  44.4 8.3 %backward_rim.1 = (f32[4,64,512]{2,1,0:T(8,128)}, f32[4,256,128]{2,1,0:T(8,128)}, f32[4,64,512]{2,1,0:T(8,128)}, f32[4,128,128]{2,1,0:T(8,128)}, f32[4,32,128]{2...) custom-call(f32[16,264,128]{2,1,0:T(8,128)} %all-to-all-done.recv_ref, f32[4,256,512]{2,1,0:T(8,128)} %bitcast.7, ...), custom_call_target="tpu_custom_call" | custom-call | flops 2818572288 | bytes 1048576 | tf_op jit(solution)/shard_map/backward_rim/pallas_call | solution.py:701
  52.8 6.3 %collective-permute-start.3 = (f32[4,64,512]{2,1,0:T(8,128)}, f32[4,64,512]{2,1,0:T(8,128)}, u32[]{:S(2)}, u32[]{:S(2)}) collective-permute-start(f32[4,64,512]{2,1,0:T(8,128)} %get-tuple-element.36), channel_id=1, source_target_pairs={{0,8},{8,16},{16,24},{24,32},{32,40},{40,48},{48,56},{56,64},{64,7... | collective-permute-start | bytes 1572872 | tf_op jit(solution)/shard_map/ppermute | solution.py:853
  59.1 1.9 %collective-permute-start.5 = (f32[4,32,128]{2,1,0:T(8,128)}, f32[4,32,128]{2,1,0:T(8,128)}, u32[]{:S(2)}, u32[]{:S(2)}) collective-permute-start(f32[4,32,128]{2,1,0:T(8,128)} %get-tuple-element.38), channel_id=1, source_target_pairs={{0,9},{1,10},{2,11},{3,12},{4,13},{5,14},{6,15},{8,17},{9,18},{10,... | collective-permute-start | bytes 196616 | tf_op jit(solution)/shard_map/ppermute | solution.py:863
  61.0 3.5 %collective-permute-start.4 = (f32[4,128,128]{2,1,0:T(8,128)}, f32[4,128,128]{2,1,0:T(8,128)}, u32[]{:S(2)}, u32[]{:S(2)}) collective-permute-start(f32[4,128,128]{2,1,0:T(8,128)} %get-tuple-element.37), channel_id=1, source_target_pairs={{0,1},{1,2},{2,3},{3,4},{4,5},{5,6},{6,7},{8,9},{9,10},{10,11},{11... | collective-permute-start | bytes 786440 | tf_op jit(solution)/shard_map/ppermute | solution.py:856
  64.5 9.1 %backward_inner.1.own_ref = f32[4,256,512]{2,1,0:T(8,128)} custom-call(s32[33]{0:T(128)} %get-tuple-element.30.count_ref, f32[32,128,128]{2,1,0:T(8,128)} %get-tuple-element.31.sum_ref, f32[4,256,512]{2,1,0:T(8,128)} %bitcast.8, f32[2,128,128]{2,1,0:T(8,128)} %probe_ref.3, bf16[8,256,256]{2,1,0:T(8,128)(2,1)} %constant.2.clone.refs_2_.refs_3_.refs_5_.tables_ref, ...), custom_call_target="tpu_custom_call" | custom-call | flops 3623878656 | bytes 1048576 | tf_op jit(solution)/shard_map/backward_inner/pallas_call | solution.py:731
  73.6 0.0 collective-permute-done.5.diag_ref
  73.6 0.0 collective-permute-done.4.left_ref
  73.6 0.0 collective-permute-done.3.above_ref
  73.7 2.4 %add_borders.1 = f32[4,256,512]{2,1,0:T(8,128)} custom-call(f32[4,256,512]{2,1,0:T(8,128)} %backward_inner.1.own_ref, f32[4,64,512]{2,1,0:T(8,128)} %collective-permute-done.3.above_ref, f32[4,128,128]{2,1,0:T(8,128)} %collective-permute-done.4.left_ref, f32[4,32,128]{2,1,0:T(8,128)} %collective-permute-done.5.diag_ref), custom_call_target="tpu_custom_call", output_to_operand_aliasing={{}: (0, {})} | custom-call | tf_op jit(solution)/shard_map/add_borders/pallas_call | solution.py:795
Async XLA Ops:
  1.8 30.7 %collective-permute-start = (f32[4,64,512]{2,1,0:T(8,128)}, f32[4,64,512]{2,1,0:T(8,128)}, u32[]{:S(2)}, u32[]{:S(2)}) collective-permute-start(f32[4,64,512]{2,1,0:T(8,128)} %row_strip.1), channel_id=1, source_target_pairs={{8,0},{16,8},{24,16},{32,24},{40,32},{48,40},{56,48},{64,56},{72,6... | collective-permute-start | bytes 1572872 | tf_op jit(solution)/shard_map/ppermute | solution.py:853
  10.2 34.2 %all-to-all-start = ((f32[16,264,128]{2,1,0:T(8,128)}), f32[16,264,128]{2,1,0:T(8,128)}, u32[]{:S(2)}, u32[]{:S(2)}) async-start(f32[16,264,128]{2,1,0:T(8,128)} %pack_measured.1.send_ref), calls=%async_computation | async-start | bytes 4325376 | tf_op jit(solution)/shard_map/all_to_all | solution.py:873
  16.5 12.1 %collective-permute-start.1 = (f32[4,256,128]{2,1,0:T(8,128)}, f32[4,256,128]{2,1,0:T(8,128)}, u32[]{:S(2)}, u32[]{:S(2)}) collective-permute-start(f32[4,256,128]{2,1,0:T(8,128)} %column_strip.1), channel_id=1, source_target_pairs={{1,0},{2,1},{3,2},{4,3},{5,4},{6,5},{7,6},{9,8},{10,9},{11,10},{12... | collective-permute-start | bytes 1572872 | tf_op jit(solution)/shard_map/ppermute | solution.py:856
  33.4 6.5 %collective-permute-start.2 = (f32[4,64,128]{2,1,0:T(8,128)S(1)}, f32[4,64,128]{2,1,0:T(8,128)}, u32[]{:S(2)}, u32[]{:S(2)}) collective-permute-start(f32[4,64,128]{2,1,0:T(8,128)S(1)} %slice.3), channel_id=1, source_target_pairs={{1,0},{2,1},{3,2},{4,3},{5,4},{6,5},{7,6},{9,8},{10,9},{11,10},{12... | collective-permute-start | bytes 393224 | tf_op jit(solution)/shard_map/ppermute | solution.py:856
  52.8 20.9 %collective-permute-start.3 = (f32[4,64,512]{2,1,0:T(8,128)}, f32[4,64,512]{2,1,0:T(8,128)}, u32[]{:S(2)}, u32[]{:S(2)}) collective-permute-start(f32[4,64,512]{2,1,0:T(8,128)} %get-tuple-element.36), channel_id=1, source_target_pairs={{0,8},{8,16},{16,24},{24,32},{32,40},{40,48},{48,56},{56,64},{64,7... | collective-permute-start | bytes 1572872 | tf_op jit(solution)/shard_map/ppermute | solution.py:853
  59.1 14.6 %collective-permute-start.5 = (f32[4,32,128]{2,1,0:T(8,128)}, f32[4,32,128]{2,1,0:T(8,128)}, u32[]{:S(2)}, u32[]{:S(2)}) collective-permute-start(f32[4,32,128]{2,1,0:T(8,128)} %get-tuple-element.38), channel_id=1, source_target_pairs={{0,9},{1,10},{2,11},{3,12},{4,13},{5,14},{6,15},{8,17},{9,18},{10,... | collective-permute-start | bytes 196616 | tf_op jit(solution)/shard_map/ppermute | solution.py:863
  61.0 12.6 %collective-permute-start.4 = (f32[4,128,128]{2,1,0:T(8,128)}, f32[4,128,128]{2,1,0:T(8,128)}, u32[]{:S(2)}, u32[]{:S(2)}) collective-permute-start(f32[4,128,128]{2,1,0:T(8,128)} %get-tuple-element.37), channel_id=1, source_target_pairs={{0,1},{1,2},{2,3},{3,4},{4,5},{5,6},{6,7},{8,9},{9,10},{10,11},{11... | collective-permute-start | bytes 786440 | tf_op jit(solution)/shard_map/ppermute | solution.py:856
